TPU v7x, 256 devices: a whole 4x4x8 slice. The times are simulated.
256 devices in a mesh: node: 8 (over z_hi, core), group: 32 (over x, y, z_lo).
Axes of the slice: x: 4, y: 4, z: 8 (z_hi: 4, z_lo: 2; z = z_hi * 2 + z_lo), core: 2. Of those that a mesh axis runs over, the one named last changes fastest.
Arguments:
- grads: float32 [256, 3145728], P(('node', 'group')), may hold values from -1.5 to 1.5
Outputs:
- reduced: float32 [3145728], P(('node', 'group'))
All inputs are finite; a program needn't handle non-finite values. Where the computation divides by a largest or mean magnitude, that divisor is 1e-20 or more.
Results may differ from a plain program's by a relative error of at most 0.0041.
Values may be sent and summed in bfloat16 or wider, within the bound.
No kernel may reach another device: no remote copies, remote signals or barrier semaphores. Data moves between devices by JAX's collectives and lax.ppermute only.
A program may use at most 128 MiB of HBM per device.

v0:
```python
import jax
import jax.numpy as jnp
from jax import lax
from jax.sharding import PartitionSpec as P

QB = 128


EPS = 1e-06


def quantize(values):
    scales = (jnp.max(jnp.abs(values), axis=-1) + EPS).astype(jnp.bfloat16)
    scales = lax.optimization_barrier(scales)
    quant = (values / scales.astype(jnp.float32)[..., None]).astype(jnp.bfloat16)
    return lax.optimization_barrier((quant, scales))


def expand(quant, scales):
    return quant.astype(jnp.float32) * scales.astype(jnp.float32)[..., None]


def within_node(pieces):
    partial_value = jnp.sum(expand(pieces[0], pieces[1]), axis=0)
    return quantize(partial_value)


def at_owner(pieces):
    return jnp.sum(expand(pieces[0], pieces[1]), axis=0)


def on_device(grads):
    nodes = lax.axis_size("node")
    groups = lax.axis_size("group")
    blocks = grads.shape[1] // (nodes * groups * QB)
    local = grads.reshape(nodes, groups, blocks, QB)
    quant, scales = quantize(local)
    quant_two, scales_two = within_node(
        (
            lax.all_to_all(quant, "node", split_axis=0, concat_axis=0, tiled=True),
            lax.all_to_all(scales, "node", split_axis=0, concat_axis=0, tiled=True),
        )
    )
    total = at_owner(
        (
            lax.all_to_all(quant_two, "group", split_axis=0, concat_axis=0, tiled=True),
            lax.all_to_all(scales_two, "group", split_axis=0, concat_axis=0, tiled=True),
        )
    )
    return total.reshape(blocks * QB)


def solution(mesh):
    placed = (P(("node", "group"), None),)
    return jax.shard_map(
        on_device, mesh=mesh, in_specs=placed, out_specs=P(("node", "group")), check_vma=False
    )
```

profile of v0, /device:TPU:2, one launch (start us, length us, event | category | flops | bytes accessed | tf_op | source)
XLA Modules:
  0.0 223.7 jit_solution(3560378873443418772)
XLA Ops:
  0.0 9.0 %abs_reduce_fusion = f32[8,32,96]{2,1,0:T(8,128)S(1)} fusion(f32[8,32,96,128]{3,2,1,0:T(8,128)} %bitcast.4), kind=kLoop, calls=%fused_computation.2 | loop fusion | flops 6266880 | bytes 12681216 | tf_op jit(solution)/shard_map/reduce_max | solution.py:13
  9.0 10.0 %divide_convert_fusion = bf16[8,32,96,128]{3,2,1,0:T(8,128)(2,1)} fusion(f32[8,32,96,128]{3,2,1,0:T(8,128)} %bitcast.5, f32[8,32,96]{2,1,0:T(8,128)S(1)} %convert_element_type.38), kind=kLoop, calls=%fused_computation.1 | loop fusion | flops 6291456 | bytes 18972672 | tf_op jit(solution)/shard_map/convert_element_type | solution.py:15
  19.0 16.6 %all_to_all.24 = bf16[8,32,96]{2,1,0:T(8,128)(2,1)S(1)} all-to-all(bf16[8,32,96]{2,1,0:T(8,128)(2,1)S(1)} %add_convert_fusion), channel_id=1, replica_groups=mesh['node'=8,'group'=32] {'node'}, dimensions={0} | all-to-all | bytes 98304 | tf_op jit(solution)/shard_map/all_to_all | solution.py:41
  35.6 4.7 %all-to-all-start = ((bf16[8,32,96,128]{3,2,1,0:T(8,128)(2,1)}), bf16[8,32,96,128]{3,2,1,0:T(8,128)(2,1)}, u32[]{:S(2)}, u32[]{:S(2)}) async-start(bf16[8,32,96,128]{3,2,1,0:T(8,128)(2,1)} %divide_convert_fusion), calls=%async_computation | async-start | bytes 12582912 | tf_op jit(solution)/shard_map/all_to_all | solution.py:40
  40.4 141.6 %all-to-all-done = bf16[8,32,96,128]{3,2,1,0:T(8,128)(2,1)} async-done(((bf16[8,32,96,128]{3,2,1,0:T(8,128)(2,1)}), bf16[8,32,96,128]{3,2,1,0:T(8,128)(2,1)}, u32[]{:S(2)}, u32[]{:S(2)}) %all-to-all-start) | async-done | bytes 6291488 | tf_op jit(solution)/shard_map/all_to_all | solution.py:40
  182.0 7.3 %multiply_reduce_fusion = f32[32,96,128]{2,1,0:T(8,128)S(1)} fusion(bf16[8,32,96,128]{3,2,1,0:T(8,128)(2,1)} %all-to-all-done, f32[8,32,96]{2,1,0:T(8,128)S(1)} %convert_element_type.41), kind=kLoop, calls=%fused_computation | loop fusion | flops 9043968 | bytes 7962624 | tf_op jit(solution)/shard_map/reduce_sum | solution.py:24
  189.3 0.6 abs_reduce_fusion.1
  189.9 1.4 divide_convert_fusion.1
  191.3 15.0 %all_to_all.25 = bf16[32,1,96]{2,1,0:T(2,128)(2,1)S(1)} all-to-all(bf16[32,1,96]{2,1,0:T(2,128)(2,1)S(1)} %copy.3), channel_id=1, replica_groups=mesh['node'=8,'group'=32] {'group'}, dimensions={0} | all-to-all | bytes 12288 | tf_op jit(solution)/shard_map/all_to_all | solution.py:47
  206.2 5.0 %all-to-all-start.2 = ((bf16[32,96,128]{2,1,0:T(8,128)(2,1)}), bf16[32,96,128]{2,1,0:T(8,128)(2,1)S(1)}, u32[]{:S(2)}, u32[]{:S(2)}) async-start(bf16[32,96,128]{2,1,0:T(8,128)(2,1)} %divide_convert_fusion.1), calls=%async_computation.2 | async-start | bytes 1572864 | tf_op jit(solution)/shard_map/all_to_all | solution.py:46
  211.3 11.3 %all-to-all-done.2 = bf16[32,96,128]{2,1,0:T(8,128)(2,1)S(1)} async-done(((bf16[32,96,128]{2,1,0:T(8,128)(2,1)}), bf16[32,96,128]{2,1,0:T(8,128)(2,1)S(1)}, u32[]{:S(2)}, u32[]{:S(2)}) %all-to-all-start.2) | async-done | bytes 786464 | tf_op jit(solution)/shard_map/all_to_all | solution.py:46
  222.6 1.1 multiply_reduce_fusion.1
  (7 shorter events, 0.1 us)
Async XLA Ops:
  35.6 146.4 %all-to-all-start = ((bf16[8,32,96,128]{3,2,1,0:T(8,128)(2,1)}), bf16[8,32,96,128]{3,2,1,0:T(8,128)(2,1)}, u32[]{:S(2)}, u32[]{:S(2)}) async-start(bf16[8,32,96,128]{3,2,1,0:T(8,128)(2,1)} %divide_convert_fusion), calls=%async_computation | async-start | bytes 12582912 | tf_op jit(solution)/shard_map/all_to_all | solution.py:40
  206.2 16.3 %all-to-all-start.2 = ((bf16[32,96,128]{2,1,0:T(8,128)(2,1)}), bf16[32,96,128]{2,1,0:T(8,128)(2,1)S(1)}, u32[]{:S(2)}, u32[]{:S(2)}) async-start(bf16[32,96,128]{2,1,0:T(8,128)(2,1)} %divide_convert_fusion.1), calls=%async_computation.2 | async-start | bytes 1572864 | tf_op jit(solution)/shard_map/all_to_all | solution.py:46
where the time goes:
time: 226 us; the launch traced here: 224 us
  waiting for transfers between devices  153 us (68%)
  blocking collectives  31.6 us (14%)
  other arithmetic  29.4 us (13%)
  starting transfers between devices  9.76 us (4%)
    all_to_all x1, waiting for transfers between devices, on_device(): lax.all_to_all(quant, 'node', split_axis=0, concat_axis=0, tiled=True)  142 us
    all_to_all x1, blocking collectives, on_device(): lax.all_to_all(scales, 'node', split_axis=0, concat_axis=0, tiled=True)  16.6 us
    all_to_all x1, blocking collectives, on_device(): lax.all_to_all(scales_two, 'group', split_axis=0, concat_axis=0, tiled=True)  15 us
    convert_element_type x2, other arithmetic, quantize(): (values / scales.astype(jnp.float32)[..., None]).astype(jnp.bfloat16)  11.3 us
    all_to_all x1, waiting for transfers between devices, on_device(): lax.all_to_all(quant_two, 'group', split_axis=0, concat_axis=0, tiled=True)  11.3 us
    reduce_max x2, other arithmetic, quantize(): scales = (jnp.max(jnp.abs(values), axis=-1) + EPS).astype(jnp.bfloat16)  9.58 us
    reduce_sum x1, other arithmetic, within_node(): partial_value = jnp.sum(expand(pieces[0], pieces[1]), axis=0)  7.26 us
    all_to_all x1, starting transfers between devices, on_device(): lax.all_to_all(quant_two, 'group', split_axis=0, concat_axis=0, tiled=True)  5.02 us
  transfers between devices with their start and end apart: 2, of which 2 were waited for; matrix products, arithmetic and copies ran while one was open for 0% of the time, Pallas kernels for 0%

commit v1 on v0

v1 whole, which is shorter than its diff:
```python
import functools

import jax
import jax.numpy as jnp
from jax import lax
from jax.experimental import pallas as pl
from jax.experimental.pallas import tpu as pltpu
from jax.sharding import PartitionSpec as P

QB = 128
ZH, CORE, X, Y, ZL = 4, 2, 4, 4, 2
RING = 4
BF16, F32 = jnp.bfloat16, jnp.float32


def flat(zh, c, x, y, zl):
    return (((zh * CORE + c) * X + x) * Y + y) * ZL + zl


def permutation(move):
    pairs = []
    for zh in range(ZH):
        for c in range(CORE):
            for x in range(X):
                for y in range(Y):
                    for zl in range(ZL):
                        pairs.append((flat(zh, c, x, y, zl), flat(*move(zh, c, x, y, zl))))
    return pairs


def to_other_core(values):
    return lax.ppermute(values, ("node", "group"), permutation(lambda zh, c, x, y, zl: (zh, 1 - c, x, y, zl)))


def along(values, shift, first):
    def move(zh, c, x, y, zl):
        if (c == 0) == first:
            return zh, c, (x + shift) % X, y, zl
        return zh, c, x, (y + shift) % Y, zl

    return lax.ppermute(values, ("node", "group"), permutation(move))


def z_groups():
    groups = []
    for c in range(CORE):
        for x in range(X):
            for y in range(Y):
                groups.append([flat(zh, c, x, y, zl) for zh in range(ZH) for zl in range(ZL)])
    return groups


def fetch(place, grads, held, sems):
    core, first = place[0], place[1]
    copies = []
    for zh in range(ZH):
        for other in range(RING):
            x = jnp.where(core == 0, first, other)
            y = jnp.where(core == 0, other, first)
            copy = pltpu.make_async_copy(grads.at[zh, core, x, y], held.at[zh, other], sems.at[zh, other])
            copy.start()
            copies.append((zh, other, copy))
    return copies


def cast_kernel(place, grads, out, held, sems):
    for zh, other, copy in fetch(place, grads, held, sems):
        copy.wait()
        out[zh, other] = held[zh, other].astype(BF16)


def add_kernel(place, grads, received, out, held, sems):
    for zh, other, copy in fetch(place, grads, held, sems):
        copy.wait()
        out[zh, other] = (held[zh, other] + received[zh, other].astype(F32)).astype(BF16)


def first_sum_kernel(place, grads, r0, p1, p2, p3, own, o1, o2, o3, held, sems):
    for zh, other, copy in fetch(place, grads, held, sems):
        copy.wait()
        total = held[zh, other] + r0[zh, other].astype(F32)
        total += p1[zh, other].astype(F32) + p2[zh, other].astype(F32) + p3[zh, other].astype(F32)
        held[zh, other] = total
    second = place[2]
    own[...] = held[:, second]
    for t, out in ((1, o1), (2, o2), (3, o3)):
        out[...] = held[:, lax.rem(second + t, RING)].astype(BF16)


def second_sum_kernel(own, u1, u2, u3, out):
    out[...] = (own[...] + u1[...].astype(F32) + u2[...].astype(F32) + u3[...].astype(F32)).astype(BF16)


def last_sum_kernel(pieces, out):
    out[...] = jnp.sum(pieces[...].astype(F32), axis=0)


VMEM = pl.BlockSpec(memory_space=pltpu.VMEM)


def call(kernel, out_shape, place, grads, *others):
    rows, lanes = grads.shape[-2:]
    return pl.pallas_call(
        kernel,
        out_shape=out_shape,
        in_specs=[pl.BlockSpec(memory_space=pltpu.SMEM), pl.BlockSpec(memory_space=pltpu.HBM)] + [VMEM] * len(others),
        out_specs=jax.tree.map(lambda _: VMEM, out_shape),
        scratch_shapes=[pltpu.VMEM((ZH, RING, rows, lanes), F32), pltpu.SemaphoreType.DMA((ZH, RING))],
        compiler_params=pltpu.CompilerParams(vmem_limit_bytes=32 * 1024 * 1024),
        cost_estimate=pl.CostEstimate(flops=ZH * RING * rows * lanes, bytes_accessed=ZH * RING * rows * lanes * 6, transcendentals=0),
    )(place, pltpu.with_memory_space_constraint(grads, pltpu.HBM), *others)


def on_device(grads):
    blocks = grads.shape[1] // (ZH * CORE * X * Y * ZL * QB)
    rows = ZL * blocks
    grads = grads.reshape(ZH, CORE, X, Y, rows, QB)
    node, group = lax.axis_index("node"), lax.axis_index("group")
    core = node % CORE
    x, y = group // (Y * ZL), (group // ZL) % Y
    first, second = jnp.where(core == 0, x, y), jnp.where(core == 0, y, x)

    def place_of(core, first, second):
        return jnp.stack([core, first, second]).astype(jnp.int32)

    quarter = jax.ShapeDtypeStruct((ZH, RING, rows, QB), BF16)
    crossed = {}
    for shift in (2, 1, 3, 0):
        mine = call(cast_kernel, quarter, place_of(1 - core, (second + shift) % RING, first), grads)
        crossed[shift] = to_other_core(mine)
    arrived = []
    for shift in (2, 1, 3):
        summed = call(add_kernel, quarter, place_of(core, (first + shift) % RING, second), grads, crossed[shift])
        arrived.append(along(summed, shift, True))
    piece = (ZH, rows, QB)
    own, *outs = call(
        first_sum_kernel,
        [jax.ShapeDtypeStruct(piece, F32)] + [jax.ShapeDtypeStruct(piece, BF16)] * 3,
        place_of(core, first, second),
        grads,
        crossed[0],
        *arrived,
    )
    got = {}
    for shift in (2, 1, 3):
        got[shift] = along(outs[shift - 1], shift, False)
    total = pl.pallas_call(second_sum_kernel, out_shape=jax.ShapeDtypeStruct(piece, BF16))(own, got[1], got[2], got[3])
    pieces = lax.all_to_all(
        total.reshape(ZH * ZL, blocks, QB), ("node", "group"), 0, 0, axis_index_groups=z_groups(), tiled=True
    )
    out = pl.pallas_call(last_sum_kernel, out_shape=jax.ShapeDtypeStruct((blocks, QB), F32))(pieces)
    return out.reshape(blocks * QB)


def solution(mesh):
    placed = (P(("node", "group"), None),)
    return jax.shard_map(
        on_device, mesh=mesh, in_specs=placed, out_specs=P(("node", "group")), check_vma=False
    )
```

time: 226 us -> 74.9 us (0.33)
  waiting for transfers between devices: 153 us -> 17.7 us
  other arithmetic: 29.4 us -> 0.6 us
  Pallas kernels: 0 us -> 24.5 us
  blocking collectives: 31.6 us -> 18.4 us
    all_to_all x2 -> x0, waiting for transfers between devices: 153 us -> none  [the longest x1 142 us: on_device(): lax.all_to_all(quant, 'node', split_axis=0, concat_axis=0, tiled=True)]
    pallas_call x0 -> x10, Pallas kernels: none -> 24.5 us  [the longest x8 21 us: call(): pl.pallas_call(kernel, out_shape=out_shape, in_specs=[pl.BlockSpec(memory...]
    ppermute x0 -> x10, waiting for transfers between devices: none -> 17.7 us  [the longest x6 17.7 us: along(): return lax.ppermute(values, ('node', 'group'), permutation(move))]
    all_to_all x2 -> x1, blocking collectives: 31.6 us -> 18.4 us  [on_device(): lax.all_to_all(total.reshape(ZH * ZL, blocks, QB), ('node', 'group'), 0,...]
    ppermute x0 -> x10, starting transfers between devices: none -> 11.6 us  [the longest x6 10.2 us: along(): return lax.ppermute(values, ('node', 'group'), permutation(move))]
    convert_element_type x8 -> x0, other arithmetic: 11.4 us -> none  [the longest x2 11.3 us: quantize(): (values / scales.astype(jnp.float32)[..., None]).astype(jnp.bfloat16)]
    all_to_all x2 -> x0, starting transfers between devices: 9.76 us -> none  [the longest x1 5.02 us: on_device(): lax.all_to_all(quant_two, 'group', split_axis=0, concat_axis=0, tiled=True)]
    reduce_max x2 -> x0, other arithmetic: 9.58 us -> none  [quantize(): scales = (jnp.max(jnp.abs(values), axis=-1) + EPS).astype(jnp.bfloat16)]
  transfers between devices with their start and end apart: 2 -> 10, of which waited for: 2 -> 4; matrix products, arithmetic and copies ran while one was open for 0% -> 1% of each run, Pallas kernels for 0% -> 21%
where the time goes in v1:
time: 74.9 us; the launch traced here: 74.3 us
  Pallas kernels  24.5 us (33%)
  blocking collectives  18.4 us (25%)
  waiting for transfers between devices  17.7 us (24%)
  starting transfers between devices  11.6 us (15%)
  local copies, waits for them, and re-layouts  1.48 us (2%)
    pallas_call x8, Pallas kernels, call(): pl.pallas_call(kernel, out_shape=out_shape, in_specs=[pl.BlockSpec(memory...  21 us
    all_to_all x1, blocking collectives, on_device(): lax.all_to_all(total.reshape(ZH * ZL, blocks, QB), ('node', 'group'), 0,...  18.4 us
    ppermute x6, waiting for transfers between devices, along(): return lax.ppermute(values, ('node', 'group'), permutation(move))  17.7 us
    ppermute x6, starting transfers between devices, along(): return lax.ppermute(values, ('node', 'group'), permutation(move))  10.2 us
    pallas_call x1, Pallas kernels, on_device(): pl.pallas_call(second_sum_kernel, out_shape=jax.ShapeDtypeStruct(piece, B...  1.96 us
    pallas_call x1, Pallas kernels, on_device(): pl.pallas_call(last_sum_kernel, out_shape=jax.ShapeDtypeStruct((blocks, Q...  1.57 us
  transfers between devices with their start and end apart: 10, of which 4 were waited for; matrix products, arithmetic and copies ran while one was open for 1% of the time, Pallas kernels for 21%

profile of v1, /device:TPU:2, one launch (start us, length us, event | category | flops | bytes accessed | tf_op | source)
XLA Modules:
  0.0 74.3 jit_solution(629072196979884838)
XLA Ops:
  0.2 3.1 %shard_map.18 = bf16[4,4,192,128]{3,2,1,0:T(8,128)(2,1)} custom-call(s32[3]{0:T(128)S(1)} %add_add_fusion.3.place, f32[4,2,4,4,192,128]{5,4,3,2,1,0:T(8,128)} %bitcast.14), custom_call_target="tpu_custom_call" | custom-call | flops 393216 | bytes 2359296 | tf_op jit(solution)/shard_map/pallas_call | solution.py:103
  3.3 3.1 %shard_map.20 = bf16[4,4,192,128]{3,2,1,0:T(8,128)(2,1)} custom-call(s32[3]{0:T(128)S(1)} %add_add_fusion.5.place, f32[4,2,4,4,192,128]{5,4,3,2,1,0:T(8,128)} %bitcast.15), custom_call_target="tpu_custom_call" | custom-call | flops 393216 | bytes 2359296 | tf_op jit(solution)/shard_map/pallas_call | solution.py:103
  6.4 0.6 collective-permute-start.3
  7.1 3.0 %shard_map.22 = bf16[4,4,192,128]{3,2,1,0:T(8,128)(2,1)} custom-call(s32[3]{0:T(128)S(1)} %add_add_fusion.7.place, f32[4,2,4,4,192,128]{5,4,3,2,1,0:T(8,128)} %bitcast.16), custom_call_target="tpu_custom_call" | custom-call | flops 393216 | bytes 2359296 | tf_op jit(solution)/shard_map/pallas_call | solution.py:103
  10.3 3.0 %shard_map.17 = bf16[4,4,192,128]{3,2,1,0:T(8,128)(2,1)} custom-call(s32[3]{0:T(128)S(1)} %add_add_fusion.1.place, f32[4,2,4,4,192,128]{5,4,3,2,1,0:T(8,128)} %bitcast.17), custom_call_target="tpu_custom_call" | custom-call | flops 393216 | bytes 2359296 | tf_op jit(solution)/shard_map/pallas_call | solution.py:103
  13.3 0.6 collective-permute-start
  14.1 2.2 %shard_map.19 = bf16[4,4,192,128]{3,2,1,0:T(8,128)(2,1)S(1)} custom-call(s32[3]{0:T(128)S(1)} %add_add_fusion.2.place, f32[4,2,4,4,192,128]{5,4,3,2,1,0:T(8,128)} %bitcast.18, bf16[4,4,192,128]{3,2,1,0:T(8,128)(2,1)S(1)} %collective-permute-done.1.received), custom_call_target="tpu_custom_call" | custom-call | flops 393216 | bytes 2359296 | tf_op jit(solution)/shard_map/pallas_call | solution.py:103
  16.3 2.2 %collective-permute-start.2 = (bf16[4,4,192,128]{3,2,1,0:T(8,128)(2,1)S(1)}, bf16[4,4,192,128]{3,2,1,0:T(8,128)(2,1)S(1)}, u32[]{:S(2)}, u32[]{:S(2)}) collective-permute-start(bf16[4,4,192,128]{3,2,1,0:T(8,128)(2,1)S(1)} %shard_map.19), channel_id=1, source_target_pairs={{0,16},{1,17},{2,18},{3,19},{4,20},{5,21},{6,22},{7,23},{8,24},{9,... | collective-permute-start | bytes 2359304 | tf_op jit(solution)/shard_map/ppermute | solution.py:41
  18.5 2.2 %shard_map.21 = bf16[4,4,192,128]{3,2,1,0:T(8,128)(2,1)S(1)} custom-call(s32[3]{0:T(128)S(1)} %add_add_fusion.4.place, f32[4,2,4,4,192,128]{5,4,3,2,1,0:T(8,128)} %bitcast.19, bf16[4,4,192,128]{3,2,1,0:T(8,128)(2,1)S(1)} %collective-permute-done.3.received), custom_call_target="tpu_custom_call" | custom-call | flops 393216 | bytes 2359296 | tf_op jit(solution)/shard_map/pallas_call | solution.py:103
  20.7 1.7 %collective-permute-start.4 = (bf16[4,4,192,128]{3,2,1,0:T(8,128)(2,1)S(1)}, bf16[4,4,192,128]{3,2,1,0:T(8,128)(2,1)S(1)}, u32[]{:S(2)}, u32[]{:S(2)}) collective-permute-start(bf16[4,4,192,128]{3,2,1,0:T(8,128)(2,1)S(1)} %shard_map.21), channel_id=1, source_target_pairs={{0,8},{1,9},{2,10},{3,11},{4,12},{5,13},{6,14},{7,15},{8,16},{9,17... | collective-permute-start | bytes 2359304 | tf_op jit(solution)/shard_map/ppermute | solution.py:41
  22.4 2.2 %shard_map.23 = bf16[4,4,192,128]{3,2,1,0:T(8,128)(2,1)S(1)} custom-call(s32[3]{0:T(128)S(1)} %add_add_fusion.6.place, f32[4,2,4,4,192,128]{5,4,3,2,1,0:T(8,128)} %bitcast.20, bf16[4,4,192,128]{3,2,1,0:T(8,128)(2,1)S(1)} %collective-permute-done.5.received), custom_call_target="tpu_custom_call" | custom-call | flops 393216 | bytes 2359296 | tf_op jit(solution)/shard_map/pallas_call | solution.py:103
  25.1 4.9 %collective-permute-done.2.p1 = bf16[4,4,192,128]{3,2,1,0:T(8,128)(2,1)S(1)} collective-permute-done((bf16[4,4,192,128]{3,2,1,0:T(8,128)(2,1)S(1)}, bf16[4,4,192,128]{3,2,1,0:T(8,128)(2,1)S(1)}, u32[]{:S(2)}, u32[]{:S(2)}) %collective-permute-start.2) | collective-permute-done | bytes 786464 | tf_op jit(solution)/shard_map/ppermute | solution.py:41
  30.0 8.4 %collective-permute-done.4.p2 = bf16[4,4,192,128]{3,2,1,0:T(8,128)(2,1)S(1)} collective-permute-done((bf16[4,4,192,128]{3,2,1,0:T(8,128)(2,1)S(1)}, bf16[4,4,192,128]{3,2,1,0:T(8,128)(2,1)S(1)}, u32[]{:S(2)}, u32[]{:S(2)}) %collective-permute-start.4) | collective-permute-done | bytes 786464 | tf_op jit(solution)/shard_map/ppermute | solution.py:41
  38.4 2.3 %shard_map.24 = (f32[4,192,128]{2,1,0:T(8,128)S(1)}, bf16[4,192,128]{2,1,0:T(8,128)(2,1)S(1)}, bf16[4,192,128]{2,1,0:T(8,128)(2,1)S(1)}, bf16[4,192,128]{2,1,0:T(8,128)(2,1)S(1)}) custom-call(s32[3]{0:T(128)S(1)} %add_add_fusion.place, f32[4,2,4,4,192,128]{5,4,3,2,1,0:T(8,128)} %bitcast.21, bf16[4,4,192,128]{3,2,1,0:T(8,128)(2,1)S(1)} %collective-permute-done.r0, ...), custom_call_target="tpu_custom_call" | custom-call | flops 393216 | bytes 2359296 | tf_op jit(solution)/shard_map/pallas_call | solution.py:103
  40.7 0.7 copy-done
  41.4 1.6 %collective-permute-start.7 = (bf16[4,192,128]{2,1,0:T(8,128)(2,1)S(1)}, bf16[4,192,128]{2,1,0:T(8,128)(2,1)S(1)}, u32[]{:S(2)}, u32[]{:S(2)}) collective-permute-start(bf16[4,192,128]{2,1,0:T(8,128)(2,1)S(1)} %get-tuple-element.10), channel_id=1, source_target_pairs={{0,2},{1,3},{2,4},{3,5},{4,6},{5,7},{6,0},{7,1},{8,10},{9,11},{10,... | collective-permute-start | bytes 589832 | tf_op jit(solution)/shard_map/ppermute | solution.py:41
  43.0 2.9 %collective-permute-start.8 = (bf16[4,192,128]{2,1,0:T(8,128)(2,1)S(1)}, bf16[4,192,128]{2,1,0:T(8,128)(2,1)S(1)}, u32[]{:S(2)}, u32[]{:S(2)}) collective-permute-start(bf16[4,192,128]{2,1,0:T(8,128)(2,1)S(1)} %get-tuple-element.11), channel_id=1, source_target_pairs={{0,4},{1,5},{2,6},{3,7},{4,0},{5,1},{6,2},{7,3},{8,12},{9,13},{10,... | collective-permute-start | bytes 589832 | tf_op jit(solution)/shard_map/ppermute | solution.py:41
  45.9 1.3 %collective-permute-start.9 = (bf16[4,192,128]{2,1,0:T(8,128)(2,1)S(1)}, bf16[4,192,128]{2,1,0:T(8,128)(2,1)S(1)}, u32[]{:S(2)}, u32[]{:S(2)}) collective-permute-start(bf16[4,192,128]{2,1,0:T(8,128)(2,1)S(1)} %get-tuple-element.12), channel_id=1, source_target_pairs={{0,6},{1,7},{2,0},{3,1},{4,2},{5,3},{6,4},{7,5},{8,14},{9,15},{10,... | collective-permute-start | bytes 589832 | tf_op jit(solution)/shard_map/ppermute | solution.py:41
  47.3 1.1 %collective-permute-done.7.u1 = bf16[4,192,128]{2,1,0:T(8,128)(2,1)S(1)} collective-permute-done((bf16[4,192,128]{2,1,0:T(8,128)(2,1)S(1)}, bf16[4,192,128]{2,1,0:T(8,128)(2,1)S(1)}, u32[]{:S(2)}, u32[]{:S(2)}) %collective-permute-start.7) | collective-permute-done | bytes 196640 | tf_op jit(solution)/shard_map/ppermute | solution.py:41
  48.3 3.3 %collective-permute-done.8.u2 = bf16[4,192,128]{2,1,0:T(8,128)(2,1)S(1)} collective-permute-done((bf16[4,192,128]{2,1,0:T(8,128)(2,1)S(1)}, bf16[4,192,128]{2,1,0:T(8,128)(2,1)S(1)}, u32[]{:S(2)}, u32[]{:S(2)}) %collective-permute-start.8) | collective-permute-done | bytes 196640 | tf_op jit(solution)/shard_map/ppermute | solution.py:41
  51.7 0.7 copy-done.2
  52.4 2.0 %shard_map.25 = bf16[4,192,128]{2,1,0:T(8,128)(2,1)} custom-call(f32[4,192,128]{2,1,0:T(8,128)} %copy-done, bf16[4,192,128]{2,1,0:T(8,128)(2,1)} %copy-done.1, bf16[4,192,128]{2,1,0:T(8,128)(2,1)} %copy-done.2, bf16[4,192,128]{2,1,0:T(8,128)(2,1)} %copy-done.3), custom_call_target="tpu_custom_call" | custom-call | tf_op jit(solution)/shard_map/pallas_call | solution.py:147
  54.4 18.4 %all_to_all.5.pieces = bf16[8,96,128]{2,1,0:T(8,128)(2,1)} all-to-all(bf16[8,96,128]{2,1,0:T(8,128)(2,1)} %bitcast.22), channel_id=1, replica_groups={{0,1,64,65,128,129,192,193},{2,3,66,67,130,131,194,195},{4,5,68,69,132,..., dimensions={0} | all-to-all | bytes 393216 | tf_op jit(solution)/shard_map/all_to_all | solution.py:148
  72.7 1.6 %shard_map.26 = f32[96,128]{1,0:T(8,128)} custom-call(bf16[8,96,128]{2,1,0:T(8,128)(2,1)} %all_to_all.5.pieces), custom_call_target="tpu_custom_call" | custom-call | tf_op jit(solution)/shard_map/pallas_call | solution.py:151
  (23 shorter events, 1.4 us)
Async XLA Ops:
  3.2 10.9 %collective-permute-start.1 = (bf16[4,4,192,128]{3,2,1,0:T(8,128)(2,1)}, bf16[4,4,192,128]{3,2,1,0:T(8,128)(2,1)S(1)}, u32[]{:S(2)}, u32[]{:S(2)}) collective-permute-start(bf16[4,4,192,128]{3,2,1,0:T(8,128)(2,1)} %shard_map.18), channel_id=1, source_target_pairs={{0,32},{1,33},{2,34},{3,35},{4,36},{5,37},{6,38},{7,39},{8,40},{9,... | collective-permute-start | bytes 2359304 | tf_op jit(solution)/shard_map/ppermute | solution.py:32
  6.4 12.1 %collective-permute-start.3 = (bf16[4,4,192,128]{3,2,1,0:T(8,128)(2,1)}, bf16[4,4,192,128]{3,2,1,0:T(8,128)(2,1)S(1)}, u32[]{:S(2)}, u32[]{:S(2)}) collective-permute-start(bf16[4,4,192,128]{3,2,1,0:T(8,128)(2,1)} %shard_map.20), channel_id=1, source_target_pairs={{0,32},{1,33},{2,34},{3,35},{4,36},{5,37},{6,38},{7,39},{8,40},{9,... | collective-permute-start | bytes 2359304 | tf_op jit(solution)/shard_map/ppermute | solution.py:32
  10.1 12.3 %collective-permute-start.5 = (bf16[4,4,192,128]{3,2,1,0:T(8,128)(2,1)}, bf16[4,4,192,128]{3,2,1,0:T(8,128)(2,1)S(1)}, u32[]{:S(2)}, u32[]{:S(2)}) collective-permute-start(bf16[4,4,192,128]{3,2,1,0:T(8,128)(2,1)} %shard_map.22), channel_id=1, source_target_pairs={{0,32},{1,33},{2,34},{3,35},{4,36},{5,37},{6,38},{7,39},{8,40},{9,... | collective-permute-start | bytes 2359304 | tf_op jit(solution)/shard_map/ppermute | solution.py:32
  13.3 11.8 %collective-permute-start = (bf16[4,4,192,128]{3,2,1,0:T(8,128)(2,1)}, bf16[4,4,192,128]{3,2,1,0:T(8,128)(2,1)S(1)}, u32[]{:S(2)}, u32[]{:S(2)}) collective-permute-start(bf16[4,4,192,128]{3,2,1,0:T(8,128)(2,1)} %shard_map.17), channel_id=1, source_target_pairs={{0,32},{1,33},{2,34},{3,35},{4,36},{5,37},{6,38},{7,39},{8,40},{9,... | collective-permute-start | bytes 2359304 | tf_op jit(solution)/shard_map/ppermute | solution.py:32
  16.3 13.7 %collective-permute-start.2 = (bf16[4,4,192,128]{3,2,1,0:T(8,128)(2,1)S(1)}, bf16[4,4,192,128]{3,2,1,0:T(8,128)(2,1)S(1)}, u32[]{:S(2)}, u32[]{:S(2)}) collective-permute-start(bf16[4,4,192,128]{3,2,1,0:T(8,128)(2,1)S(1)} %shard_map.19), channel_id=1, source_target_pairs={{0,16},{1,17},{2,18},{3,19},{4,20},{5,21},{6,22},{7,23},{8,24},{9,... | collective-permute-start | bytes 2359304 | tf_op jit(solution)/shard_map/ppermute | solution.py:41
  20.7 17.7 %collective-permute-start.4 = (bf16[4,4,192,128]{3,2,1,0:T(8,128)(2,1)S(1)}, bf16[4,4,192,128]{3,2,1,0:T(8,128)(2,1)S(1)}, u32[]{:S(2)}, u32[]{:S(2)}) collective-permute-start(bf16[4,4,192,128]{3,2,1,0:T(8,128)(2,1)S(1)} %shard_map.21), channel_id=1, source_target_pairs={{0,8},{1,9},{2,10},{3,11},{4,12},{5,13},{6,14},{7,15},{8,16},{9,17... | collective-permute-start | bytes 2359304 | tf_op jit(solution)/shard_map/ppermute | solution.py:41
  24.5 13.9 %collective-permute-start.6 = (bf16[4,4,192,128]{3,2,1,0:T(8,128)(2,1)S(1)}, bf16[4,4,192,128]{3,2,1,0:T(8,128)(2,1)S(1)}, u32[]{:S(2)}, u32[]{:S(2)}) collective-permute-start(bf16[4,4,192,128]{3,2,1,0:T(8,128)(2,1)S(1)} %shard_map.23), channel_id=1, source_target_pairs={{0,24},{1,25},{2,26},{3,27},{4,28},{5,29},{6,30},{7,31},{8,0},{9,1... | collective-permute-start | bytes 2359304 | tf_op jit(solution)/shard_map/ppermute | solution.py:41
  40.7 0.7 copy-start
  41.4 6.9 %collective-permute-start.7 = (bf16[4,192,128]{2,1,0:T(8,128)(2,1)S(1)}, bf16[4,192,128]{2,1,0:T(8,128)(2,1)S(1)}, u32[]{:S(2)}, u32[]{:S(2)}) collective-permute-start(bf16[4,192,128]{2,1,0:T(8,128)(2,1)S(1)} %get-tuple-element.10), channel_id=1, source_target_pairs={{0,2},{1,3},{2,4},{3,5},{4,6},{5,7},{6,0},{7,1},{8,10},{9,11},{10,... | collective-permute-start | bytes 589832 | tf_op jit(solution)/shard_map/ppermute | solution.py:41
  43.0 8.7 %collective-permute-start.8 = (bf16[4,192,128]{2,1,0:T(8,128)(2,1)S(1)}, bf16[4,192,128]{2,1,0:T(8,128)(2,1)S(1)}, u32[]{:S(2)}, u32[]{:S(2)}) collective-permute-start(bf16[4,192,128]{2,1,0:T(8,128)(2,1)S(1)} %get-tuple-element.11), channel_id=1, source_target_pairs={{0,4},{1,5},{2,6},{3,7},{4,0},{5,1},{6,2},{7,3},{8,12},{9,13},{10,... | collective-permute-start | bytes 589832 | tf_op jit(solution)/shard_map/ppermute | solution.py:41
  45.9 5.8 %collective-permute-start.9 = (bf16[4,192,128]{2,1,0:T(8,128)(2,1)S(1)}, bf16[4,192,128]{2,1,0:T(8,128)(2,1)S(1)}, u32[]{:S(2)}, u32[]{:S(2)}) collective-permute-start(bf16[4,192,128]{2,1,0:T(8,128)(2,1)S(1)} %get-tuple-element.12), channel_id=1, source_target_pairs={{0,6},{1,7},{2,0},{3,1},{4,2},{5,3},{6,4},{7,5},{8,14},{9,15},{10,... | collective-permute-start | bytes 589832 | tf_op jit(solution)/shard_map/ppermute | solution.py:41
  48.3 3.4 %copy-start.1 = (bf16[4,192,128]{2,1,0:T(8,128)(2,1)}, bf16[4,192,128]{2,1,0:T(8,128)(2,1)S(1)}, u32[]{:S(2)}) copy-start(bf16[4,192,128]{2,1,0:T(8,128)(2,1)S(1)} %collective-permute-done.7.u1) | copy-start | bytes 589828
  51.7 0.7 copy-start.2
  51.7 0.7 %copy-start.3 = (bf16[4,192,128]{2,1,0:T(8,128)(2,1)}, bf16[4,192,128]{2,1,0:T(8,128)(2,1)S(1)}, u32[]{:S(2)}) copy-start(bf16[4,192,128]{2,1,0:T(8,128)(2,1)S(1)} %collective-permute-done.9.u3) | copy-start | bytes 589828

commit v2 on v0

v2 whole, which is shorter than its diff:
```python
import functools

import jax
import jax.numpy as jnp
from jax import lax
from jax.experimental import pallas as pl
from jax.experimental.pallas import tpu as pltpu
from jax.sharding import PartitionSpec as P

QB = 128
ZH, CORE, X, Y, ZL = 4, 2, 4, 4, 2
RING = 4
COST = 0
AXES = ("node", "group")
BF16, F32 = jnp.bfloat16, jnp.float32


def flat(zh, c, x, y, zl):
    return (((zh * CORE + c) * X + x) * Y + y) * ZL + zl


def permuted(values, move):
    pairs = []
    for zh in range(ZH):
        for c in range(CORE):
            for x in range(X):
                for y in range(Y):
                    for zl in range(ZL):
                        pairs.append((flat(zh, c, x, y, zl), flat(*move(zh, c, x, y, zl))))
    return lax.ppermute(values, AXES, pairs)


def to_other_core(values):
    return permuted(values, lambda zh, c, x, y, zl: (zh, 1 - c, x, y, zl))


def along(values, shift, first):
    def move(zh, c, x, y, zl):
        if (c == 0) == first:
            return zh, c, (x + shift) % X, y, zl
        return zh, c, x, (y + shift) % Y, zl

    return permuted(values, move)


def z_groups():
    groups = []
    for c in range(CORE):
        for x in range(X):
            for y in range(Y):
                groups.append([flat(zh, c, x, y, zl) for zh in range(ZH) for zl in range(ZL)])
    return groups


def place():
    node, group = lax.axis_index("node"), lax.axis_index("group")
    core = lax.rem(node, CORE)
    x, y = lax.div(group, Y * ZL), lax.rem(lax.div(group, ZL), Y)
    return core, jnp.where(core == 0, x, y), jnp.where(core == 0, y, x)


def steps_kernel(steps, grads, *refs):
    n_received = sum(added for _, added in steps)
    received, outs = list(refs[:n_received]), refs[n_received : n_received + len(steps)]
    held, sems = refs[n_received + len(steps) :]
    core, first, second = place()
    copies = []
    for k, (shift, added) in enumerate(steps):
        half = core if added else 1 - core
        at = lax.rem((first if added else second) + shift, RING)
        for zh in range(ZH):
            for other in range(RING):
                x, y = jnp.where(half == 0, at, other), jnp.where(half == 0, other, at)
                copy = pltpu.make_async_copy(grads.at[zh, half, x, y], held.at[k, zh, other], sems.at[k, zh, other])
                copy.start()
                copies.append(copy)
    copies = iter(copies)
    for k, (_, added) in enumerate(steps):
        source = received.pop(0) if added else None
        for zh in range(ZH):
            for other in range(RING):
                next(copies).wait()
                value = held[k, zh, other]
                if added:
                    value += source[zh, other].astype(F32)
                outs[k][zh, other] = value.astype(outs[k].dtype)


VMEM = pl.BlockSpec(memory_space=pltpu.VMEM)


def run_steps(grads, steps, received=(), dtype=BF16):
    rows, lanes = grads.shape[-2:]
    size = len(steps) * ZH * RING * rows * lanes
    return pl.pallas_call(
        functools.partial(steps_kernel, steps),
        out_shape=[pltpu.VMEM((ZH, RING, rows, lanes), dtype)] * len(steps),
        in_specs=[pl.BlockSpec(memory_space=pltpu.HBM)] + [VMEM] * len(received),
        out_specs=[VMEM] * len(steps),
        scratch_shapes=[
            pltpu.VMEM((len(steps), ZH, RING, rows, lanes), F32),
            pltpu.SemaphoreType.DMA((len(steps), ZH, RING)),
        ],
        compiler_params=pltpu.CompilerParams(vmem_limit_bytes=10 * 1024 * 1024),
        cost_estimate=pl.CostEstimate(flops=COST, bytes_accessed=COST, transcendentals=0),
    )(pltpu.with_memory_space_constraint(grads, pltpu.HBM), *received)


def on_device(grads):
    blocks = grads.shape[1] // (ZH * CORE * X * Y * ZL * QB)
    grads = grads.reshape(ZH, CORE, X, Y, ZL * blocks, QB)
    second = place()[2]

    (c2,) = run_steps(grads, ((2, False),))
    later = lax.optimization_barrier((grads, c2))[0]
    c1, c3, c0 = run_steps(later, ((1, False), (3, False), (0, False)))
    c2, c1, c3, c0 = [to_other_core(c) for c in (c2, c1, c3, c0)]
    (s2,) = run_steps(grads, ((2, True),), (c2,))
    p2 = along(s2, 2, True)
    grads = lax.optimization_barrier((grads, s2))[0]
    (s1,) = run_steps(grads, ((1, True),), (c1,))
    p1 = along(s1, 1, True)
    grads = lax.optimization_barrier((grads, s1))[0]
    (s3,) = run_steps(grads, ((3, True),), (c3,))
    p3 = along(s3, 3, True)
    grads = lax.optimization_barrier((grads, s3))[0]
    (s0,) = run_steps(grads, ((0, True),), (c0,), F32)

    total = s0 + p1.astype(F32) + p2.astype(F32) + p3.astype(F32)

    def piece(shift):
        return lax.dynamic_index_in_dim(total, lax.rem(second + shift, RING), 1, keepdims=False)

    summed = piece(0)
    for shift in (2, 1, 3):
        summed += along(piece(shift).astype(BF16), shift, False).astype(F32)
    pieces = summed.astype(BF16).reshape(ZH * ZL, blocks, QB)
    pieces = lax.all_to_all(pieces, AXES, 0, 0, axis_index_groups=z_groups(), tiled=True)
    return jnp.sum(pieces.astype(F32), axis=0).reshape(blocks * QB)


def solution(mesh):
    placed = (P(("node", "group"), None),)
    return jax.shard_map(
        on_device, mesh=mesh, in_specs=placed, out_specs=P(("node", "group")), check_vma=False
    )
```

time: 226 us -> 62.9 us (0.28)
  waiting for transfers between devices: 153 us -> 18.9 us
  other arithmetic: 29.4 us -> 2.78 us
  blocking collectives: 31.6 us -> 18 us
  Pallas kernels: 0 us -> 11.7 us
    all_to_all x2 -> x0, waiting for transfers between devices: 153 us -> none  [the longest x1 142 us: on_device(): lax.all_to_all(quant, 'node', split_axis=0, concat_axis=0, tiled=True)]
    ppermute x0 -> x10, waiting for transfers between devices: none -> 18.9 us  [permuted(): return lax.ppermute(values, AXES, pairs)]
    all_to_all x2 -> x1, blocking collectives: 31.6 us -> 18 us  [on_device(): lax.all_to_all(pieces, AXES, 0, 0, axis_index_groups=z_groups(), tiled=True)]
    pallas_call x0 -> x6, Pallas kernels: none -> 11.7 us  [run_steps(): pl.pallas_call(functools.partial(steps_kernel, steps), out_shape=[pltpu.V...]
    convert_element_type x8 -> x1, other arithmetic: 11.4 us -> 0.1 us  [on_device(): pieces = summed.astype(BF16).reshape(ZH * ZL, blocks, QB)]
    ppermute x0 -> x10, starting transfers between devices: none -> 10.9 us  [permuted(): return lax.ppermute(values, AXES, pairs)]
    all_to_all x2 -> x0, starting transfers between devices: 9.76 us -> none  [the longest x1 5.02 us: on_device(): lax.all_to_all(quant_two, 'group', split_axis=0, concat_axis=0, tiled=True)]
    reduce_max x2 -> x0, other arithmetic: 9.58 us -> none  [quantize(): scales = (jnp.max(jnp.abs(values), axis=-1) + EPS).astype(jnp.bfloat16)]
  transfers between devices with their start and end apart: 2 -> 10, of which waited for: 2 -> 5; matrix products, arithmetic and copies ran while one was open for 0% -> 0% of each run, Pallas kernels for 0% -> 16%
where the time goes in v2:
time: 62.9 us; the launch traced here: 62.5 us
  waiting for transfers between devices  18.9 us (30%)
  blocking collectives  18 us (29%)
  Pallas kernels  11.7 us (19%)
  starting transfers between devices  10.9 us (17%)
  other arithmetic  2.78 us (4%)
    ppermute x10, waiting for transfers between devices, permuted(): return lax.ppermute(values, AXES, pairs)  18.9 us
    all_to_all x1, blocking collectives, on_device(): lax.all_to_all(pieces, AXES, 0, 0, axis_index_groups=z_groups(), tiled=True)  18 us
    pallas_call x6, Pallas kernels, run_steps(): pl.pallas_call(functools.partial(steps_kernel, steps), out_shape=[pltpu.V...  11.7 us
    ppermute x10, starting transfers between devices, permuted(): return lax.ppermute(values, AXES, pairs)  10.9 us
    add x1, other arithmetic, on_device(): total = s0 + p1.astype(F32) + p2.astype(F32) + p3.astype(F32)  2.04 us
  transfers between devices with their start and end apart: 10, of which 5 were waited for; matrix products, arithmetic and copies ran while one was open for 0% of the time, Pallas kernels for 16%

profile of v2, /device:TPU:2, one launch (start us, length us, event | category | flops | bytes accessed | tf_op | source)
XLA Modules:
  0.0 62.5 jit_solution(17755482798522167725)
XLA Ops:
  0.0 1.6 %shard_map.17 = bf16[4,4,192,128]{3,2,1,0:T(8,128)(2,1)S(1)} custom-call(f32[4,2,4,4,192,128]{5,4,3,2,1,0:T(8,128)} %bitcast.25), custom_call_target="tpu_custom_call" | custom-call | tf_op jit(solution)/shard_map/pallas_call | solution.py:95
  1.7 3.7 %shard_map.19 = (bf16[4,4,192,128]{3,2,1,0:T(8,128)(2,1)S(1)}, bf16[4,4,192,128]{3,2,1,0:T(8,128)(2,1)S(1)}, bf16[4,4,192,128]{3,2,1,0:T(8,128)(2,1)}) custom-call(f32[4,2,4,4,192,128]{5,4,3,2,1,0:T(8,128)} %bitcast.26), custom_call_target="tpu_custom_call" | custom-call | tf_op jit(solution)/shard_map/pallas_call | solution.py:95
  5.5 0.6 collective-permute-start.1
  6.0 0.1 collective-permute-start.2
  6.1 0.4 collective-permute-start.3
  6.5 1.6 %shard_map.18 = bf16[4,4,192,128]{3,2,1,0:T(8,128)(2,1)S(1)} custom-call(f32[4,2,4,4,192,128]{5,4,3,2,1,0:T(8,128)} %bitcast.27, bf16[4,4,192,128]{3,2,1,0:T(8,128)(2,1)S(1)} %collective-permute-done.refs_0_), custom_call_target="tpu_custom_call" | custom-call | tf_op jit(solution)/shard_map/pallas_call | solution.py:95
  8.1 2.2 %collective-permute-start.5 = (bf16[4,4,192,128]{3,2,1,0:T(8,128)(2,1)S(1)}, bf16[4,4,192,128]{3,2,1,0:T(8,128)(2,1)}, u32[]{:S(2)}, u32[]{:S(2)}) collective-permute-start(bf16[4,4,192,128]{3,2,1,0:T(8,128)(2,1)S(1)} %shard_map.18), channel_id=1, source_target_pairs={{0,16},{1,17},{2,18},{3,19},{4,20},{5,21},{6,22},{7,23},{8,24},{9,... | collective-permute-start | bytes 2359304 | tf_op jit(solution)/shard_map/ppermute | solution.py:30
  10.3 1.6 %shard_map.20 = bf16[4,4,192,128]{3,2,1,0:T(8,128)(2,1)S(1)} custom-call(f32[4,2,4,4,192,128]{5,4,3,2,1,0:T(8,128)} %bitcast.28, bf16[4,4,192,128]{3,2,1,0:T(8,128)(2,1)S(1)} %collective-permute-done.1.refs_0_), custom_call_target="tpu_custom_call" | custom-call | tf_op jit(solution)/shard_map/pallas_call | solution.py:95
  12.0 1.7 %collective-permute-start.4 = (bf16[4,4,192,128]{3,2,1,0:T(8,128)(2,1)S(1)}, bf16[4,4,192,128]{3,2,1,0:T(8,128)(2,1)}, u32[]{:S(2)}, u32[]{:S(2)}) collective-permute-start(bf16[4,4,192,128]{3,2,1,0:T(8,128)(2,1)S(1)} %shard_map.20), channel_id=1, source_target_pairs={{0,8},{1,9},{2,10},{3,11},{4,12},{5,13},{6,14},{7,15},{8,16},{9,17... | collective-permute-start | bytes 2359304 | tf_op jit(solution)/shard_map/ppermute | solution.py:30
  13.6 1.6 %shard_map.21 = bf16[4,4,192,128]{3,2,1,0:T(8,128)(2,1)S(1)} custom-call(f32[4,2,4,4,192,128]{5,4,3,2,1,0:T(8,128)} %bitcast.29, bf16[4,4,192,128]{3,2,1,0:T(8,128)(2,1)S(1)} %collective-permute-done.2.refs_0_), custom_call_target="tpu_custom_call" | custom-call | tf_op jit(solution)/shard_map/pallas_call | solution.py:95
  15.3 0.5 collective-permute-start.6
  15.7 1.6 %shard_map.22 = f32[4,4,192,128]{3,2,1,0:T(8,128)S(1)} custom-call(f32[4,2,4,4,192,128]{5,4,3,2,1,0:T(8,128)} %bitcast.30, bf16[4,4,192,128]{3,2,1,0:T(8,128)(2,1)S(1)} %collective-permute-done.3.refs_0_), custom_call_target="tpu_custom_call" | custom-call | tf_op jit(solution)/shard_map/pallas_call | solution.py:95
  17.4 4.6 %collective-permute-done.5 = bf16[4,4,192,128]{3,2,1,0:T(8,128)(2,1)} collective-permute-done((bf16[4,4,192,128]{3,2,1,0:T(8,128)(2,1)S(1)}, bf16[4,4,192,128]{3,2,1,0:T(8,128)(2,1)}, u32[]{:S(2)}, u32[]{:S(2)}) %collective-permute-start.5) | collective-permute-done | bytes 786464 | tf_op jit(solution)/shard_map/ppermute | solution.py:30
  21.9 8.4 %collective-permute-done.4 = bf16[4,4,192,128]{3,2,1,0:T(8,128)(2,1)} collective-permute-done((bf16[4,4,192,128]{3,2,1,0:T(8,128)(2,1)S(1)}, bf16[4,4,192,128]{3,2,1,0:T(8,128)(2,1)}, u32[]{:S(2)}, u32[]{:S(2)}) %collective-permute-start.4) | collective-permute-done | bytes 786464 | tf_op jit(solution)/shard_map/ppermute | solution.py:30
  30.3 2.0 %convert_add_fusion = f32[4,4,192,128]{3,2,1,0:T(8,128)S(1)} fusion(bf16[4,4,192,128]{3,2,1,0:T(8,128)(2,1)} %collective-permute-done.6, bf16[4,4,192,128]{3,2,1,0:T(8,128)(2,1)} %collective-permute-done.5, f32[4,4,192,128]{3,2,1,0:T(8,128)S(1)} %shard_map.22, bf16[4,4,192,128]{3,2,1,0:T(8,128)(2,1)} %collective-permute-done.4), kind=kLoop, calls=%fused_computation | loop fusion | flops 2359296 | bytes 5505024 | tf_op jit(solution)/shard_map/add | solution.py:129
  32.4 0.1 fusion.4
  32.5 3.3 %collective-permute-start.7 = (bf16[4,192,128]{2,1,0:T(8,128)(2,1)S(1)}, bf16[4,192,128]{2,1,0:T(8,128)(2,1)S(1)}, u32[]{:S(2)}, u32[]{:S(2)}) collective-permute-start(bf16[4,192,128]{2,1,0:T(8,128)(2,1)S(1)} %get-tuple-element.19), channel_id=1, source_target_pairs={{0,4},{1,5},{2,6},{3,7},{4,0},{5,1},{6,2},{7,3},{8,12},{9,13},{10,... | collective-permute-start | bytes 589832 | tf_op jit(solution)/shard_map/ppermute | solution.py:30
  35.8 1.1 %collective-permute-start.9 = (bf16[4,192,128]{2,1,0:T(8,128)(2,1)S(1)}, bf16[4,192,128]{2,1,0:T(8,128)(2,1)S(1)}, u32[]{:S(2)}, u32[]{:S(2)}) collective-permute-start(bf16[4,192,128]{2,1,0:T(8,128)(2,1)S(1)} %get-tuple-element.20), channel_id=1, source_target_pairs={{0,6},{1,7},{2,0},{3,1},{4,2},{5,3},{6,4},{7,5},{8,14},{9,15},{10,... | collective-permute-start | bytes 589832 | tf_op jit(solution)/shard_map/ppermute | solution.py:30
  36.8 1.0 %collective-permute-start.8 = (bf16[4,192,128]{2,1,0:T(8,128)(2,1)S(1)}, bf16[4,192,128]{2,1,0:T(8,128)(2,1)S(1)}, u32[]{:S(2)}, u32[]{:S(2)}) collective-permute-start(bf16[4,192,128]{2,1,0:T(8,128)(2,1)S(1)} %get-tuple-element.21), channel_id=1, source_target_pairs={{0,2},{1,3},{2,4},{3,5},{4,6},{5,7},{6,0},{7,1},{8,10},{9,11},{10,... | collective-permute-start | bytes 589832 | tf_op jit(solution)/shard_map/ppermute | solution.py:30
  37.8 2.0 %collective-permute-done.7 = bf16[4,192,128]{2,1,0:T(8,128)(2,1)S(1)} collective-permute-done((bf16[4,192,128]{2,1,0:T(8,128)(2,1)S(1)}, bf16[4,192,128]{2,1,0:T(8,128)(2,1)S(1)}, u32[]{:S(2)}, u32[]{:S(2)}) %collective-permute-start.7) | collective-permute-done | bytes 196640 | tf_op jit(solution)/shard_map/ppermute | solution.py:30
  39.7 2.4 %collective-permute-done.9 = bf16[4,192,128]{2,1,0:T(8,128)(2,1)S(1)} collective-permute-done((bf16[4,192,128]{2,1,0:T(8,128)(2,1)S(1)}, bf16[4,192,128]{2,1,0:T(8,128)(2,1)S(1)}, u32[]{:S(2)}, u32[]{:S(2)}) %collective-permute-start.9) | collective-permute-done | bytes 196640 | tf_op jit(solution)/shard_map/ppermute | solution.py:30
  42.2 1.5 %collective-permute-done.8 = bf16[4,192,128]{2,1,0:T(8,128)(2,1)S(1)} collective-permute-done((bf16[4,192,128]{2,1,0:T(8,128)(2,1)S(1)}, bf16[4,192,128]{2,1,0:T(8,128)(2,1)S(1)}, u32[]{:S(2)}, u32[]{:S(2)}) %collective-permute-start.8) | collective-permute-done | bytes 196640 | tf_op jit(solution)/shard_map/ppermute | solution.py:30
  43.8 18.0 %all_to_all.5 = bf16[8,96,128]{2,1,0:T(8,128)(2,1)S(1)} all-to-all(bf16[8,96,128]{2,1,0:T(8,128)(2,1)S(1)} %bitcast.31), channel_id=1, replica_groups={{0,1,64,65,128,129,192,193},{2,3,66,67,130,131,194,195},{4,5,68,69,132,..., dimensions={0} | all-to-all | bytes 393216 | tf_op jit(solution)/shard_map/all_to_all | solution.py:138
  61.8 0.6 %convert_reduce_fusion = f32[96,128]{1,0:T(8,128)} fusion(bf16[8,96,128]{2,1,0:T(8,128)(2,1)S(1)} %all_to_all.5), kind=kLoop, calls=%fused_computation.7 | loop fusion | flops 184320 | bytes 245760 | tf_op jit(solution)/shard_map/reduce_sum | solution.py:139
  (7 shorter events, 0.2 us)
Async XLA Ops:
  1.6 4.9 %collective-permute-start = (bf16[4,4,192,128]{3,2,1,0:T(8,128)(2,1)S(1)}, bf16[4,4,192,128]{3,2,1,0:T(8,128)(2,1)S(1)}, u32[]{:S(2)}, u32[]{:S(2)}) collective-permute-start(bf16[4,4,192,128]{3,2,1,0:T(8,128)(2,1)S(1)} %shard_map.17), channel_id=1, source_target_pairs={{0,32},{1,33},{2,34},{3,35},{4,36},{5,37},{6,38},{7,39},{8,40},{9,... | collective-permute-start | bytes 2359304 | tf_op jit(solution)/shard_map/ppermute | solution.py:30
  5.5 4.9 %collective-permute-start.1 = (bf16[4,4,192,128]{3,2,1,0:T(8,128)(2,1)S(1)}, bf16[4,4,192,128]{3,2,1,0:T(8,128)(2,1)S(1)}, u32[]{:S(2)}, u32[]{:S(2)}) collective-permute-start(bf16[4,4,192,128]{3,2,1,0:T(8,128)(2,1)S(1)} %get-tuple-element.14), channel_id=1, source_target_pairs={{0,32},{1,33},{2,34},{3,35},{4,36},{5,37},{6,38},{7,39},{8,40},{9,... | collective-permute-start | bytes 2359304 | tf_op jit(solution)/shard_map/ppermute | solution.py:30
  6.0 7.6 %collective-permute-start.2 = (bf16[4,4,192,128]{3,2,1,0:T(8,128)(2,1)S(1)}, bf16[4,4,192,128]{3,2,1,0:T(8,128)(2,1)S(1)}, u32[]{:S(2)}, u32[]{:S(2)}) collective-permute-start(bf16[4,4,192,128]{3,2,1,0:T(8,128)(2,1)S(1)} %get-tuple-element.16), channel_id=1, source_target_pairs={{0,32},{1,33},{2,34},{3,35},{4,36},{5,37},{6,38},{7,39},{8,40},{9,... | collective-permute-start | bytes 2359304 | tf_op jit(solution)/shard_map/ppermute | solution.py:30
  6.1 9.6 %collective-permute-start.3 = (bf16[4,4,192,128]{3,2,1,0:T(8,128)(2,1)}, bf16[4,4,192,128]{3,2,1,0:T(8,128)(2,1)S(1)}, u32[]{:S(2)}, u32[]{:S(2)}) collective-permute-start(bf16[4,4,192,128]{3,2,1,0:T(8,128)(2,1)} %get-tuple-element.18), channel_id=1, source_target_pairs={{0,32},{1,33},{2,34},{3,35},{4,36},{5,37},{6,38},{7,39},{8,40},{9,... | collective-permute-start | bytes 2359304 | tf_op jit(solution)/shard_map/ppermute | solution.py:30
  8.1 13.8 %collective-permute-start.5 = (bf16[4,4,192,128]{3,2,1,0:T(8,128)(2,1)S(1)}, bf16[4,4,192,128]{3,2,1,0:T(8,128)(2,1)}, u32[]{:S(2)}, u32[]{:S(2)}) collective-permute-start(bf16[4,4,192,128]{3,2,1,0:T(8,128)(2,1)S(1)} %shard_map.18), channel_id=1, source_target_pairs={{0,16},{1,17},{2,18},{3,19},{4,20},{5,21},{6,22},{7,23},{8,24},{9,... | collective-permute-start | bytes 2359304 | tf_op jit(solution)/shard_map/ppermute | solution.py:30
  12.0 18.4 %collective-permute-start.4 = (bf16[4,4,192,128]{3,2,1,0:T(8,128)(2,1)S(1)}, bf16[4,4,192,128]{3,2,1,0:T(8,128)(2,1)}, u32[]{:S(2)}, u32[]{:S(2)}) collective-permute-start(bf16[4,4,192,128]{3,2,1,0:T(8,128)(2,1)S(1)} %shard_map.20), channel_id=1, source_target_pairs={{0,8},{1,9},{2,10},{3,11},{4,12},{5,13},{6,14},{7,15},{8,16},{9,17... | collective-permute-start | bytes 2359304 | tf_op jit(solution)/shard_map/ppermute | solution.py:30
  15.3 15.1 %collective-permute-start.6 = (bf16[4,4,192,128]{3,2,1,0:T(8,128)(2,1)S(1)}, bf16[4,4,192,128]{3,2,1,0:T(8,128)(2,1)}, u32[]{:S(2)}, u32[]{:S(2)}) collective-permute-start(bf16[4,4,192,128]{3,2,1,0:T(8,128)(2,1)S(1)} %shard_map.21), channel_id=1, source_target_pairs={{0,24},{1,25},{2,26},{3,27},{4,28},{5,29},{6,30},{7,31},{8,0},{9,1... | collective-permute-start | bytes 2359304 | tf_op jit(solution)/shard_map/ppermute | solution.py:30
  32.5 7.3 %collective-permute-start.7 = (bf16[4,192,128]{2,1,0:T(8,128)(2,1)S(1)}, bf16[4,192,128]{2,1,0:T(8,128)(2,1)S(1)}, u32[]{:S(2)}, u32[]{:S(2)}) collective-permute-start(bf16[4,192,128]{2,1,0:T(8,128)(2,1)S(1)} %get-tuple-element.19), channel_id=1, source_target_pairs={{0,4},{1,5},{2,6},{3,7},{4,0},{5,1},{6,2},{7,3},{8,12},{9,13},{10,... | collective-permute-start | bytes 589832 | tf_op jit(solution)/shard_map/ppermute | solution.py:30
  35.8 6.4 %collective-permute-start.9 = (bf16[4,192,128]{2,1,0:T(8,128)(2,1)S(1)}, bf16[4,192,128]{2,1,0:T(8,128)(2,1)S(1)}, u32[]{:S(2)}, u32[]{:S(2)}) collective-permute-start(bf16[4,192,128]{2,1,0:T(8,128)(2,1)S(1)} %get-tuple-element.20), channel_id=1, source_target_pairs={{0,6},{1,7},{2,0},{3,1},{4,2},{5,3},{6,4},{7,5},{8,14},{9,15},{10,... | collective-permute-start | bytes 589832 | tf_op jit(solution)/shard_map/ppermute | solution.py:30
  36.8 6.9 %collective-permute-start.8 = (bf16[4,192,128]{2,1,0:T(8,128)(2,1)S(1)}, bf16[4,192,128]{2,1,0:T(8,128)(2,1)S(1)}, u32[]{:S(2)}, u32[]{:S(2)}) collective-permute-start(bf16[4,192,128]{2,1,0:T(8,128)(2,1)S(1)} %get-tuple-element.21), channel_id=1, source_target_pairs={{0,2},{1,3},{2,4},{3,5},{4,6},{5,7},{6,0},{7,1},{8,10},{9,11},{10,... | collective-permute-start | bytes 589832 | tf_op jit(solution)/shard_map/ppermute | solution.py:30

commit v3 on v2

v3 whole, which is shorter than its diff:
```python
import functools

import jax
import jax.numpy as jnp
from jax import lax
from jax.experimental import pallas as pl
from jax.experimental.pallas import tpu as pltpu
from jax.sharding import PartitionSpec as P

QB = 128
ZH, CORE, X, Y, ZL = 4, 2, 4, 4, 2
RING = 4
AXES = ("node", "group")
BF16, F32 = jnp.bfloat16, jnp.float32


def flat(zh, c, x, y, zl):
    return (((zh * CORE + c) * X + x) * Y + y) * ZL + zl


def permuted(values, move):
    pairs = []
    for zh in range(ZH):
        for c in range(CORE):
            for x in range(X):
                for y in range(Y):
                    for zl in range(ZL):
                        pairs.append((flat(zh, c, x, y, zl), flat(*move(zh, c, x, y, zl))))
    return lax.ppermute(values, AXES, pairs)


def to_other_core(values):
    return permuted(values, lambda zh, c, x, y, zl: (zh, 1 - c, x, y, zl))


def along(values, shift, first):
    def move(zh, c, x, y, zl):
        if (c == 0) == first:
            return zh, c, (x + shift) % X, y, zl
        return zh, c, x, (y + shift) % Y, zl

    return permuted(values, move)


def z_groups():
    groups = []
    for c in range(CORE):
        for x in range(X):
            for y in range(Y):
                groups.append([flat(zh, c, x, y, zl) for zh in range(ZH) for zl in range(ZL)])
    return groups


def place():
    node, group = lax.axis_index("node"), lax.axis_index("group")
    core = lax.rem(node, CORE)
    x, y = lax.div(group, Y * ZL), lax.rem(lax.div(group, ZL), Y)
    return core, jnp.where(core == 0, x, y), jnp.where(core == 0, y, x)


def steps_kernel(steps, grads, *refs):
    n_received = sum(added for _, _, added in steps)
    received, outs = list(refs[:n_received]), refs[n_received : n_received + len(steps)]
    held, sems = refs[n_received + len(steps) :]
    core, first, second = place()
    copies = []
    for k, (shift, (begin, end), added) in enumerate(steps):
        half = core if added else 1 - core
        at = lax.rem((first if added else second) + shift, RING)
        for zh in range(begin, end):
            target, sem = held.at[k, zh - begin], sems.at[k, zh - begin]
            along_x = pltpu.make_async_copy(grads.at[zh, half, at], target, sem)
            along_y = pltpu.make_async_copy(grads.at[zh, half, :, at], target, sem)
            pl.when(half == 0)(along_x.start)
            pl.when(half != 0)(along_y.start)
            copies.append(along_x)
    copies = iter(copies)
    for k, (_, (begin, end), added) in enumerate(steps):
        source = received.pop(0) if added else None
        for zh in range(end - begin):
            next(copies).wait()
            for other in range(RING):
                value = held[k, zh, other]
                if added:
                    value += source[zh, other].astype(F32)
                outs[k][zh, other] = value.astype(outs[k].dtype)


VMEM = pl.BlockSpec(memory_space=pltpu.VMEM)
PARAMS = pltpu.CompilerParams(vmem_limit_bytes=10 * 1024 * 1024)
COST = pl.CostEstimate(flops=0, bytes_accessed=0, transcendentals=0)


def run_steps(grads, steps, received=(), dtype=BF16):
    rows, lanes = grads.shape[-2:]
    longest = max(end - begin for _, (begin, end), _ in steps)
    return pl.pallas_call(
        functools.partial(steps_kernel, steps),
        out_shape=[pltpu.VMEM((end - begin, RING, rows, lanes), dtype) for _, (begin, end), _ in steps],
        in_specs=[pl.BlockSpec(memory_space=pltpu.HBM)] + [VMEM] * len(received),
        out_specs=[VMEM] * len(steps),
        scratch_shapes=[
            pltpu.VMEM((len(steps), longest, RING, rows, lanes), F32),
            pltpu.SemaphoreType.DMA((len(steps), longest)),
        ],
        compiler_params=PARAMS,
        cost_estimate=COST,
    )(pltpu.with_memory_space_constraint(grads, pltpu.HBM), *received)


def sum_kernel(parts, own, *refs):
    arrived, outs = refs[: len(parts)], refs[len(parts) :]
    second = place()[2]
    for shift, out in enumerate(outs):
        other = lax.rem(second + shift, RING)
        for zh in range(ZH):
            value = own[zh, other]
            for (begin, end), part in zip(parts, arrived):
                if begin <= zh < end:
                    value += part[zh - begin, other].astype(F32)
            out[zh] = value.astype(out.dtype)


def run_sum(own, parts, arrived):
    rows, lanes = own.shape[-2:]
    return pl.pallas_call(
        functools.partial(sum_kernel, parts),
        out_shape=[pltpu.VMEM((ZH, rows, lanes), BF16 if shift else F32) for shift in range(RING)],
        in_specs=[VMEM] * (1 + len(arrived)),
        out_specs=[VMEM] * RING,
        compiler_params=PARAMS,
        cost_estimate=COST,
    )(own, *[pltpu.with_memory_space_constraint(part, pltpu.VMEM) for part in arrived])


def on_device(grads):
    blocks = grads.shape[1] // (ZH * CORE * X * Y * ZL * QB)
    grads = grads.reshape(ZH, CORE, X, Y, ZL * blocks, QB)
    whole, low, high = (0, ZH), (0, ZH // 2), (ZH // 2, ZH)
    order = (
        ((2, whole, False),),
        ((1, whole, False), (3, whole, False), (0, whole, False)),
        ((2, whole, True),),
        ((1, whole, True),),
        ((3, whole, True),),
        ((0, whole, True),),
    )
    crossed, arrived, own = {}, {}, None
    for steps in order:
        received = [crossed[shift, part] for shift, part, added in steps if added]
        outs = run_steps(grads, steps, received, BF16 if steps[0] != (0, whole, True) else F32)
        grads = lax.optimization_barrier((grads, *outs))[0]
        for (shift, part, added), out in zip(steps, outs):
            if not added:
                crossed[shift, part] = to_other_core(out)
            elif shift:
                arrived[shift, part] = along(out, shift, True)
            else:
                own = out

    pieces = run_sum(own, [part for _, part in arrived], list(arrived.values()))
    summed = pieces[0]
    for shift in (2, 1, 3):
        summed += along(pieces[shift], shift, False).astype(F32)
    pieces = summed.astype(BF16).reshape(ZH * ZL, blocks, QB)
    pieces = lax.all_to_all(pieces, AXES, 0, 0, axis_index_groups=z_groups(), tiled=True)
    return jnp.sum(pieces.astype(F32), axis=0).reshape(blocks * QB)


def solution(mesh):
    placed = (P(("node", "group"), None),)
    return jax.shard_map(
        on_device, mesh=mesh, in_specs=placed, out_specs=P(("node", "group")), check_vma=False
    )
```

time: 62.9 us -> 58.4 us (0.928)
  other arithmetic: 2.78 us -> 0.74 us
  Pallas kernels: 11.7 us -> 9.86 us
  waiting for transfers between devices: 18.9 us -> 17.1 us
  starting transfers between devices: 10.9 us -> 12.1 us
    pallas_call x6, Pallas kernels: 11.7 us -> 9.53 us  [run_steps(): pl.pallas_call(functools.partial(steps_kernel, steps), out_shape=[pltpu.V...]
    add x1 -> x0, other arithmetic: 2.04 us -> none  [on_device(): total = s0 + p1.astype(F32) + p2.astype(F32) + p3.astype(F32)]
    ppermute x10, waiting for transfers between devices: 18.9 us -> 17.1 us  [permuted(): return lax.ppermute(values, AXES, pairs)]
    ppermute x10, starting transfers between devices: 10.9 us -> 12.1 us  [permuted(): return lax.ppermute(values, AXES, pairs)]
  transfers between devices with their start and end apart: 10 -> 10, of which waited for: 5 -> 4; matrix products, arithmetic and copies ran while one was open for 0% -> 0% of each run, Pallas kernels for 16% -> 14%
where the time goes in v3:
time: 58.4 us; the launch traced here: 57.8 us
  blocking collectives  18 us (31%)
  waiting for transfers between devices  17.1 us (29%)
  starting transfers between devices  12.1 us (21%)
  Pallas kernels  9.86 us (17%)
  other arithmetic  0.74 us (1%)
    all_to_all x1, blocking collectives, on_device(): lax.all_to_all(pieces, AXES, 0, 0, axis_index_groups=z_groups(), tiled=True)  18 us
    ppermute x10, waiting for transfers between devices, permuted(): return lax.ppermute(values, AXES, pairs)  17.1 us
    ppermute x10, starting transfers between devices, permuted(): return lax.ppermute(values, AXES, pairs)  12.1 us
    pallas_call x6, Pallas kernels, run_steps(): pl.pallas_call(functools.partial(steps_kernel, steps), out_shape=[pltpu.V...  9.53 us
  transfers between devices with their start and end apart: 10, of which 4 were waited for; matrix products, arithmetic and copies ran while one was open for 0% of the time, Pallas kernels for 14%

profile of v3, /device:TPU:2, one launch (start us, length us, event | category | flops | bytes accessed | tf_op | source)
XLA Modules:
  0.0 57.8 jit_solution(14126648772057285179)
XLA Ops:
  0.0 1.4 %shard_map.17 = bf16[4,4,192,128]{3,2,1,0:T(8,128)(2,1)S(1)} custom-call(f32[4,2,4,4,192,128]{5,4,3,2,1,0:T(8,128)} %bitcast.3), custom_call_target="tpu_custom_call" | custom-call | tf_op jit(solution)/shard_map/pallas_call | solution.py:97
  1.4 0.1 collective-permute-start
  1.5 2.5 %shard_map.18 = (bf16[4,4,192,128]{3,2,1,0:T(8,128)(2,1)S(1)}, bf16[4,4,192,128]{3,2,1,0:T(8,128)(2,1)S(1)}, bf16[4,4,192,128]{3,2,1,0:T(8,128)(2,1)S(1)}) custom-call(f32[4,2,4,4,192,128]{5,4,3,2,1,0:T(8,128)} %bitcast.4), custom_call_target="tpu_custom_call" | custom-call | tf_op jit(solution)/shard_map/pallas_call | solution.py:97
  4.0 0.6 collective-permute-start.1
  4.5 0.1 collective-permute-start.2
  4.6 0.4 collective-permute-start.3
  5.0 1.4 %shard_map.19 = bf16[4,4,192,128]{3,2,1,0:T(8,128)(2,1)S(1)} custom-call(f32[4,2,4,4,192,128]{5,4,3,2,1,0:T(8,128)} %bitcast.5, bf16[4,4,192,128]{3,2,1,0:T(8,128)(2,1)S(1)} %collective-permute-done.refs_0_), custom_call_target="tpu_custom_call" | custom-call | tf_op jit(solution)/shard_map/pallas_call | solution.py:97
  6.5 2.2 %collective-permute-start.4 = (bf16[4,4,192,128]{3,2,1,0:T(8,128)(2,1)S(1)}, bf16[4,4,192,128]{3,2,1,0:T(8,128)(2,1)S(1)}, u32[]{:S(2)}, u32[]{:S(2)}) collective-permute-start(bf16[4,4,192,128]{3,2,1,0:T(8,128)(2,1)S(1)} %shard_map.19), channel_id=1, source_target_pairs={{0,16},{1,17},{2,18},{3,19},{4,20},{5,21},{6,22},{7,23},{8,24},{9,... | collective-permute-start | bytes 2359304 | tf_op jit(solution)/shard_map/ppermute | solution.py:29
  8.7 1.4 %shard_map.20 = bf16[4,4,192,128]{3,2,1,0:T(8,128)(2,1)S(1)} custom-call(f32[4,2,4,4,192,128]{5,4,3,2,1,0:T(8,128)} %bitcast.6, bf16[4,4,192,128]{3,2,1,0:T(8,128)(2,1)S(1)} %collective-permute-done.1.refs_0_), custom_call_target="tpu_custom_call" | custom-call | tf_op jit(solution)/shard_map/pallas_call | solution.py:97
  10.1 1.7 %collective-permute-start.5 = (bf16[4,4,192,128]{3,2,1,0:T(8,128)(2,1)S(1)}, bf16[4,4,192,128]{3,2,1,0:T(8,128)(2,1)S(1)}, u32[]{:S(2)}, u32[]{:S(2)}) collective-permute-start(bf16[4,4,192,128]{3,2,1,0:T(8,128)(2,1)S(1)} %shard_map.20), channel_id=1, source_target_pairs={{0,8},{1,9},{2,10},{3,11},{4,12},{5,13},{6,14},{7,15},{8,16},{9,17... | collective-permute-start | bytes 2359304 | tf_op jit(solution)/shard_map/ppermute | solution.py:29
  11.8 1.4 %shard_map.21 = bf16[4,4,192,128]{3,2,1,0:T(8,128)(2,1)S(1)} custom-call(f32[4,2,4,4,192,128]{5,4,3,2,1,0:T(8,128)} %bitcast.7, bf16[4,4,192,128]{3,2,1,0:T(8,128)(2,1)S(1)} %collective-permute-done.2.refs_0_), custom_call_target="tpu_custom_call" | custom-call | tf_op jit(solution)/shard_map/pallas_call | solution.py:97
  13.2 0.5 collective-permute-start.6
  13.7 1.4 %shard_map.22.own = f32[4,4,192,128]{3,2,1,0:T(8,128)S(1)} custom-call(f32[4,2,4,4,192,128]{5,4,3,2,1,0:T(8,128)} %bitcast.8, bf16[4,4,192,128]{3,2,1,0:T(8,128)(2,1)S(1)} %collective-permute-done.3.refs_0_), custom_call_target="tpu_custom_call" | custom-call | tf_op jit(solution)/shard_map/pallas_call | solution.py:97
  15.1 5.0 %collective-permute-done.4.refs_0_ = bf16[4,4,192,128]{3,2,1,0:T(8,128)(2,1)S(1)} collective-permute-done((bf16[4,4,192,128]{3,2,1,0:T(8,128)(2,1)S(1)}, bf16[4,4,192,128]{3,2,1,0:T(8,128)(2,1)S(1)}, u32[]{:S(2)}, u32[]{:S(2)}) %collective-permute-start.4) | collective-permute-done | bytes 786464 | tf_op jit(solution)/shard_map/ppermute | solution.py:29
  20.2 8.4 %collective-permute-done.5.refs_1_ = bf16[4,4,192,128]{3,2,1,0:T(8,128)(2,1)S(1)} collective-permute-done((bf16[4,4,192,128]{3,2,1,0:T(8,128)(2,1)S(1)}, bf16[4,4,192,128]{3,2,1,0:T(8,128)(2,1)S(1)}, u32[]{:S(2)}, u32[]{:S(2)}) %collective-permute-start.5) | collective-permute-done | bytes 786464 | tf_op jit(solution)/shard_map/ppermute | solution.py:29
  28.5 0.3 shard_map.23
  28.9 3.3 %collective-permute-start.7 = (bf16[4,192,128]{2,1,0:T(8,128)(2,1)S(1)}, bf16[4,192,128]{2,1,0:T(8,128)(2,1)S(1)}, u32[]{:S(2)}, u32[]{:S(2)}) collective-permute-start(bf16[4,192,128]{2,1,0:T(8,128)(2,1)S(1)} %get-tuple-element.26), channel_id=1, source_target_pairs={{0,4},{1,5},{2,6},{3,7},{4,0},{5,1},{6,2},{7,3},{8,12},{9,13},{10,... | collective-permute-start | bytes 589832 | tf_op jit(solution)/shard_map/ppermute | solution.py:29
  32.2 0.7 %collective-permute-start.8 = (bf16[4,192,128]{2,1,0:T(8,128)(2,1)S(1)}, bf16[4,192,128]{2,1,0:T(8,128)(2,1)S(1)}, u32[]{:S(2)}, u32[]{:S(2)}) collective-permute-start(bf16[4,192,128]{2,1,0:T(8,128)(2,1)S(1)} %get-tuple-element.27), channel_id=1, source_target_pairs={{0,2},{1,3},{2,4},{3,5},{4,6},{5,7},{6,0},{7,1},{8,10},{9,11},{10,... | collective-permute-start | bytes 589832 | tf_op jit(solution)/shard_map/ppermute | solution.py:29
  32.8 2.6 %collective-permute-start.9 = (bf16[4,192,128]{2,1,0:T(8,128)(2,1)S(1)}, bf16[4,192,128]{2,1,0:T(8,128)(2,1)S(1)}, u32[]{:S(2)}, u32[]{:S(2)}) collective-permute-start(bf16[4,192,128]{2,1,0:T(8,128)(2,1)S(1)} %get-tuple-element.28), channel_id=1, source_target_pairs={{0,6},{1,7},{2,0},{3,1},{4,2},{5,3},{6,4},{7,5},{8,14},{9,15},{10,... | collective-permute-start | bytes 589832 | tf_op jit(solution)/shard_map/ppermute | solution.py:29
  35.4 0.7 %collective-permute-done.7 = bf16[4,192,128]{2,1,0:T(8,128)(2,1)S(1)} collective-permute-done((bf16[4,192,128]{2,1,0:T(8,128)(2,1)S(1)}, bf16[4,192,128]{2,1,0:T(8,128)(2,1)S(1)}, u32[]{:S(2)}, u32[]{:S(2)}) %collective-permute-start.7) | collective-permute-done | bytes 196640 | tf_op jit(solution)/shard_map/ppermute | solution.py:29
  36.1 2.9 %collective-permute-done.8 = bf16[4,192,128]{2,1,0:T(8,128)(2,1)S(1)} collective-permute-done((bf16[4,192,128]{2,1,0:T(8,128)(2,1)S(1)}, bf16[4,192,128]{2,1,0:T(8,128)(2,1)S(1)}, u32[]{:S(2)}, u32[]{:S(2)}) %collective-permute-start.8) | collective-permute-done | bytes 196640 | tf_op jit(solution)/shard_map/ppermute | solution.py:29
  39.0 0.1 add_convert_fusion
  39.1 18.0 %all_to_all.5 = bf16[8,96,128]{2,1,0:T(8,128)(2,1)S(1)} all-to-all(bf16[8,96,128]{2,1,0:T(8,128)(2,1)S(1)} %bitcast.9), channel_id=1, replica_groups={{0,1,64,65,128,129,192,193},{2,3,66,67,130,131,194,195},{4,5,68,69,132,..., dimensions={0} | all-to-all | bytes 393216 | tf_op jit(solution)/shard_map/all_to_all | solution.py:166
  57.2 0.6 %convert_reduce_fusion = f32[96,128]{1,0:T(8,128)} fusion(bf16[8,96,128]{2,1,0:T(8,128)(2,1)S(1)} %all_to_all.5), kind=kLoop, calls=%fused_computation | loop fusion | flops 184320 | bytes 245760 | tf_op jit(solution)/shard_map/reduce_sum | solution.py:167
  (6 shorter events, 0.0 us)
Async XLA Ops:
  1.4 3.6 %collective-permute-start = (bf16[4,4,192,128]{3,2,1,0:T(8,128)(2,1)S(1)}, bf16[4,4,192,128]{3,2,1,0:T(8,128)(2,1)S(1)}, u32[]{:S(2)}, u32[]{:S(2)}) collective-permute-start(bf16[4,4,192,128]{3,2,1,0:T(8,128)(2,1)S(1)} %shard_map.17), channel_id=1, source_target_pairs={{0,32},{1,33},{2,34},{3,35},{4,36},{5,37},{6,38},{7,39},{8,40},{9,... | collective-permute-start | bytes 2359304 | tf_op jit(solution)/shard_map/ppermute | solution.py:29
  4.0 4.7 %collective-permute-start.1 = (bf16[4,4,192,128]{3,2,1,0:T(8,128)(2,1)S(1)}, bf16[4,4,192,128]{3,2,1,0:T(8,128)(2,1)S(1)}, u32[]{:S(2)}, u32[]{:S(2)}) collective-permute-start(bf16[4,4,192,128]{3,2,1,0:T(8,128)(2,1)S(1)} %get-tuple-element.18), channel_id=1, source_target_pairs={{0,32},{1,33},{2,34},{3,35},{4,36},{5,37},{6,38},{7,39},{8,40},{9,... | collective-permute-start | bytes 2359304 | tf_op jit(solution)/shard_map/ppermute | solution.py:29
  4.5 7.3 %collective-permute-start.2 = (bf16[4,4,192,128]{3,2,1,0:T(8,128)(2,1)S(1)}, bf16[4,4,192,128]{3,2,1,0:T(8,128)(2,1)S(1)}, u32[]{:S(2)}, u32[]{:S(2)}) collective-permute-start(bf16[4,4,192,128]{3,2,1,0:T(8,128)(2,1)S(1)} %get-tuple-element.19), channel_id=1, source_target_pairs={{0,32},{1,33},{2,34},{3,35},{4,36},{5,37},{6,38},{7,39},{8,40},{9,... | collective-permute-start | bytes 2359304 | tf_op jit(solution)/shard_map/ppermute | solution.py:29
  4.6 9.1 %collective-permute-start.3 = (bf16[4,4,192,128]{3,2,1,0:T(8,128)(2,1)S(1)}, bf16[4,4,192,128]{3,2,1,0:T(8,128)(2,1)S(1)}, u32[]{:S(2)}, u32[]{:S(2)}) collective-permute-start(bf16[4,4,192,128]{3,2,1,0:T(8,128)(2,1)S(1)} %get-tuple-element.20), channel_id=1, source_target_pairs={{0,32},{1,33},{2,34},{3,35},{4,36},{5,37},{6,38},{7,39},{8,40},{9,... | collective-permute-start | bytes 2359304 | tf_op jit(solution)/shard_map/ppermute | solution.py:29
  6.5 13.7 %collective-permute-start.4 = (bf16[4,4,192,128]{3,2,1,0:T(8,128)(2,1)S(1)}, bf16[4,4,192,128]{3,2,1,0:T(8,128)(2,1)S(1)}, u32[]{:S(2)}, u32[]{:S(2)}) collective-permute-start(bf16[4,4,192,128]{3,2,1,0:T(8,128)(2,1)S(1)} %shard_map.19), channel_id=1, source_target_pairs={{0,16},{1,17},{2,18},{3,19},{4,20},{5,21},{6,22},{7,23},{8,24},{9,... | collective-permute-start | bytes 2359304 | tf_op jit(solution)/shard_map/ppermute | solution.py:29
  10.1 18.4 %collective-permute-start.5 = (bf16[4,4,192,128]{3,2,1,0:T(8,128)(2,1)S(1)}, bf16[4,4,192,128]{3,2,1,0:T(8,128)(2,1)S(1)}, u32[]{:S(2)}, u32[]{:S(2)}) collective-permute-start(bf16[4,4,192,128]{3,2,1,0:T(8,128)(2,1)S(1)} %shard_map.20), channel_id=1, source_target_pairs={{0,8},{1,9},{2,10},{3,11},{4,12},{5,13},{6,14},{7,15},{8,16},{9,17... | collective-permute-start | bytes 2359304 | tf_op jit(solution)/shard_map/ppermute | solution.py:29
  13.2 15.3 %collective-permute-start.6 = (bf16[4,4,192,128]{3,2,1,0:T(8,128)(2,1)S(1)}, bf16[4,4,192,128]{3,2,1,0:T(8,128)(2,1)S(1)}, u32[]{:S(2)}, u32[]{:S(2)}) collective-permute-start(bf16[4,4,192,128]{3,2,1,0:T(8,128)(2,1)S(1)} %shard_map.21), channel_id=1, source_target_pairs={{0,24},{1,25},{2,26},{3,27},{4,28},{5,29},{6,30},{7,31},{8,0},{9,1... | collective-permute-start | bytes 2359304 | tf_op jit(solution)/shard_map/ppermute | solution.py:29
  28.9 7.3 %collective-permute-start.7 = (bf16[4,192,128]{2,1,0:T(8,128)(2,1)S(1)}, bf16[4,192,128]{2,1,0:T(8,128)(2,1)S(1)}, u32[]{:S(2)}, u32[]{:S(2)}) collective-permute-start(bf16[4,192,128]{2,1,0:T(8,128)(2,1)S(1)} %get-tuple-element.26), channel_id=1, source_target_pairs={{0,4},{1,5},{2,6},{3,7},{4,0},{5,1},{6,2},{7,3},{8,12},{9,13},{10,... | collective-permute-start | bytes 589832 | tf_op jit(solution)/shard_map/ppermute | solution.py:29
  32.2 6.9 %collective-permute-start.8 = (bf16[4,192,128]{2,1,0:T(8,128)(2,1)S(1)}, bf16[4,192,128]{2,1,0:T(8,128)(2,1)S(1)}, u32[]{:S(2)}, u32[]{:S(2)}) collective-permute-start(bf16[4,192,128]{2,1,0:T(8,128)(2,1)S(1)} %get-tuple-element.27), channel_id=1, source_target_pairs={{0,2},{1,3},{2,4},{3,5},{4,6},{5,7},{6,0},{7,1},{8,10},{9,11},{10,... | collective-permute-start | bytes 589832 | tf_op jit(solution)/shard_map/ppermute | solution.py:29
  32.8 6.2 %collective-permute-start.9 = (bf16[4,192,128]{2,1,0:T(8,128)(2,1)S(1)}, bf16[4,192,128]{2,1,0:T(8,128)(2,1)S(1)}, u32[]{:S(2)}, u32[]{:S(2)}) collective-permute-start(bf16[4,192,128]{2,1,0:T(8,128)(2,1)S(1)} %get-tuple-element.28), channel_id=1, source_target_pairs={{0,6},{1,7},{2,0},{3,1},{4,2},{5,3},{6,4},{7,5},{8,14},{9,15},{10,... | collective-permute-start | bytes 589832 | tf_op jit(solution)/shard_map/ppermute | solution.py:29

commit v4 on v3

v4 whole, which is shorter than its diff:
```python
import functools

import jax
import jax.numpy as jnp
from jax import lax
from jax.experimental import pallas as pl
from jax.experimental.pallas import tpu as pltpu
from jax.sharding import PartitionSpec as P

QB = 128
ZH, CORE, X, Y, ZL = 4, 2, 4, 4, 2
RING = 4
AXES = ("node", "group")
BF16, F32 = jnp.bfloat16, jnp.float32
SLABS, PLAIN = 6, 4


def flat(zh, c, x, y, zl):
    return (((zh * CORE + c) * X + x) * Y + y) * ZL + zl


def permuted(values, move):
    pairs = []
    for zh in range(ZH):
        for c in range(CORE):
            for x in range(X):
                for y in range(Y):
                    for zl in range(ZL):
                        pairs.append((flat(zh, c, x, y, zl), flat(*move(zh, c, x, y, zl))))
    return lax.ppermute(values, AXES, pairs)


def to_other_core(values):
    return permuted(values, lambda zh, c, x, y, zl: (zh, 1 - c, x, y, zl))


def along(values, shift, first):
    def move(zh, c, x, y, zl):
        if (c == 0) == first:
            return zh, c, (x + shift) % X, y, zl
        return zh, c, x, (y + shift) % Y, zl

    return permuted(values, move)


def to_z_partner(values):
    def move(zh, c, x, y, zl):
        step = 1 if (zl == 0) == (c == 0) else -1
        z = (zh * ZL + zl + step) % (ZH * ZL)
        return z // ZL, c, x, y, z % ZL

    return permuted(values, move)


def z_groups():
    groups = []
    for c in range(CORE):
        for x in range(X):
            for y in range(Y):
                groups.append([flat(zh, c, x, y, zl) for zh in range(ZH) for zl in range(ZL)])
    return groups


def place():
    node, group = lax.axis_index("node"), lax.axis_index("group")
    core = lax.rem(node, CORE)
    x, y = lax.div(group, Y * ZL), lax.rem(lax.div(group, ZL), Y)
    return core, jnp.where(core == 0, x, y), jnp.where(core == 0, y, x), lax.rem(group, ZL)


PAIR, SENT, KEPT = "pair", "sent", "kept"


def shape_of(what, rows):
    if what == PAIR:
        return (ZH, X, Y, ZL, SLABS - PLAIN, rows, QB)
    if what in (SENT, KEPT):
        return (ZH, X, Y, ZL, rows, QB)
    return (ZH, RING, ZL, PLAIN, rows, QB)


def steps_kernel(steps, grads, *refs):
    n_received = sum(added for _, added in steps)
    received, outs = list(refs[:n_received]), refs[n_received : n_received + len(steps)]
    helds, sems = refs[n_received + len(steps) : -1], refs[-1]
    core, first, second, zl = place()
    copies = []
    for k, (what, added) in enumerate(steps):
        half = core if added else 1 - core
        for zh in range(ZH):
            target, sem = helds[k].at[zh], sems.at[k, zh]
            if what == PAIR:
                copy = pltpu.make_async_copy(grads.at[zh, half, :, :, :, pl.ds(PLAIN, SLABS - PLAIN)], target, sem)
                copy.start()
            elif what in (SENT, KEPT):
                slab = PLAIN + (1 - zl if what == SENT else zl)
                copy = pltpu.make_async_copy(grads.at[zh, half, :, :, :, slab], target, sem)
                copy.start()
            else:
                at = lax.rem((first if added else second) + what, RING)
                copy = pltpu.make_async_copy(grads.at[zh, half, at, :, :, pl.ds(0, PLAIN)], target, sem)
                along_y = pltpu.make_async_copy(grads.at[zh, half, :, at, :, pl.ds(0, PLAIN)], target, sem)
                pl.when(half == 0)(copy.start)
                pl.when(half != 0)(along_y.start)
            copies.append(copy)
    copies = iter(copies)
    for k, (what, added) in enumerate(steps):
        source = received.pop(0) if added else None
        for zh in range(ZH):
            next(copies).wait()
            value = helds[k][zh]
            if added and what in (SENT, KEPT):
                value += source[zh, :, :, :, 1 - zl if what == SENT else zl].astype(F32)
            elif added:
                value += source[zh].astype(F32)
            outs[k][zh] = value.astype(outs[k].dtype)


VMEM = pl.BlockSpec(memory_space=pltpu.VMEM)
PARAMS = pltpu.CompilerParams(vmem_limit_bytes=10 * 1024 * 1024)
COST = pl.CostEstimate(flops=0, bytes_accessed=0, transcendentals=0)


def in_vmem(values):
    return pltpu.with_memory_space_constraint(values, pltpu.VMEM)


def run_steps(grads, steps, received):
    rows = grads.shape[-2]
    shapes = [shape_of(what, rows) for what, _ in steps]
    types = [F32 if added and what in (0, KEPT) else BF16 for what, added in steps]
    return pl.pallas_call(
        functools.partial(steps_kernel, steps),
        out_shape=[pltpu.VMEM(shape, dtype) for shape, dtype in zip(shapes, types)],
        in_specs=[pl.BlockSpec(memory_space=pltpu.HBM)] + [VMEM] * len(received),
        out_specs=[VMEM] * len(steps),
        scratch_shapes=[pltpu.VMEM(shape, F32) for shape in shapes] + [pltpu.SemaphoreType.DMA((len(steps), ZH))],
        compiler_params=PARAMS,
        cost_estimate=COST,
    )(pltpu.with_memory_space_constraint(grads, pltpu.HBM), *received)


def paired_kernel(kept, arrived, *outs):
    core, first, _, _ = place()
    for shift, out in enumerate(outs):
        at = lax.rem(first + shift, RING)
        for zh in range(ZH):
            for other in range(RING):
                x, y = jnp.where(core == 0, at, other), jnp.where(core == 0, other, at)
                out[zh, other] = (kept[zh, x, y] + arrived[zh, x, y].astype(F32)).astype(out.dtype)


def run_paired(kept, arrived):
    rows = kept.shape[-2]
    return pl.pallas_call(
        paired_kernel,
        out_shape=[pltpu.VMEM((ZH, RING, ZL, rows, QB), BF16 if shift else F32) for shift in range(RING)],
        in_specs=[VMEM] * 2,
        out_specs=[VMEM] * RING,
        compiler_params=PARAMS,
        cost_estimate=COST,
    )(kept, in_vmem(arrived))


def plain_kernel(own, p1, p2, p3, out):
    for zh in range(ZH):
        out[zh] = own[zh] + p1[zh].astype(F32) + p2[zh].astype(F32) + p3[zh].astype(F32)


def run_plain(own, arrived):
    return pl.pallas_call(
        plain_kernel,
        out_shape=pltpu.VMEM(own.shape, F32),
        in_specs=[VMEM] * 4,
        out_specs=VMEM,
        compiler_params=PARAMS,
        cost_estimate=COST,
    )(own, *map(in_vmem, arrived))


def pieces_kernel(plain, own, p1, p2, p3, *outs):
    second = place()[2]
    for shift, out in enumerate(outs):
        other = lax.rem(second + shift, RING)
        for zh in range(ZH):
            paired = own[zh, other] + p1[zh, other].astype(F32) + p2[zh, other].astype(F32) + p3[zh, other].astype(F32)
            out[zh, :, 0:PLAIN] = plain[zh, other].astype(out.dtype)
            out[zh, :, PLAIN] = paired.astype(out.dtype)


def run_pieces(plain, own, arrived):
    rows = own.shape[-2]
    return pl.pallas_call(
        pieces_kernel,
        out_shape=[pltpu.VMEM((ZH, ZL, PLAIN + 1, rows, QB), BF16 if shift else F32) for shift in range(RING)],
        in_specs=[VMEM] * 5,
        out_specs=[VMEM] * RING,
        compiler_params=PARAMS,
        cost_estimate=COST,
    )(plain, own, *map(in_vmem, arrived))


def on_device(grads):
    rows = grads.shape[1] // (ZH * CORE * X * Y * ZL * SLABS * QB)
    grads = grads.reshape(ZH, CORE, X, Y, ZL, SLABS, rows, QB)
    order = (
        ((2, False), (PAIR, False)),
        ((1, False), (3, False), (0, False)),
        ((2, True), (SENT, True)),
        ((1, True),),
        ((3, True),),
        ((0, True), (KEPT, True)),
    )
    crossed, arrived, own = {}, {}, {}
    for steps in order:
        received = [crossed[PAIR if what in (SENT, KEPT) else what] for what, added in steps if added]
        outs = run_steps(grads, steps, received)
        grads = lax.optimization_barrier((grads, *outs))[0]
        for (what, added), out in zip(steps, outs):
            if not added:
                crossed[what] = to_other_core(out)
            elif what == SENT:
                arrived[what] = to_z_partner(out)
            elif what in (0, KEPT):
                own[what] = out
            else:
                arrived[what] = along(out, what, True)

    paired = run_paired(own[KEPT], arrived[SENT])
    paired_arrived = {shift: along(paired[shift], shift, True) for shift in (2, 1, 3)}
    plain = run_plain(own[0], [arrived[shift] for shift in (2, 1, 3)])
    pieces = run_pieces(plain, paired[0], [paired_arrived[shift] for shift in (2, 1, 3)])
    summed = pieces[0]
    for shift in (2, 1, 3):
        summed += along(pieces[shift], shift, False).astype(F32)
    pieces = summed.astype(BF16).reshape(ZH * ZL, PLAIN + 1, rows, QB)
    pieces = lax.all_to_all(pieces, AXES, 0, 0, axis_index_groups=z_groups(), tiled=True).astype(F32)
    of_plain = jnp.sum(pieces[:, :PLAIN], axis=0)
    of_paired = jnp.sum(pieces[:, PLAIN].reshape(ZH, ZL, rows, QB), axis=0)
    return jnp.concatenate([of_plain, of_paired]).reshape(SLABS * rows * QB)


def solution(mesh):
    placed = (P(("node", "group"), None),)
    return jax.shard_map(
        on_device, mesh=mesh, in_specs=placed, out_specs=P(("node", "group")), check_vma=False
    )
```

time: 58.4 us -> 56.4 us (0.966)
  waiting for transfers between devices: 17.1 us -> 9.81 us
  starting transfers between devices: 12.1 us -> 18.3 us
  blocking collectives: 18 us -> 16.8 us
    ppermute x10 -> x15, waiting for transfers between devices: 17.1 us -> 9.81 us  [permuted(): return lax.ppermute(values, AXES, pairs)]
    ppermute x10 -> x15, starting transfers between devices: 12.1 us -> 18.3 us  [permuted(): return lax.ppermute(values, AXES, pairs)]
    all_to_all x1, blocking collectives: 18 us -> 16.8 us  [on_device(): lax.all_to_all(pieces, AXES, 0, 0, axis_index_groups=z_groups(), tiled=True)]
    concatenate x0 -> x1, other arithmetic: none -> 0.62 us  [on_device(): return jnp.concatenate([of_plain, of_paired]).reshape(SLABS * rows * QB)]
    reduce_sum x1 -> x2, other arithmetic: 0.65 us -> 0.03 us  [the longest x1 0.02 us: on_device(): of_plain = jnp.sum(pieces[:, :PLAIN], axis=0)]
  transfers between devices with their start and end apart: 10 -> 15, of which waited for: 4 -> 6; matrix products, arithmetic and copies ran while one was open for 0% -> 0% of each run, Pallas kernels for 14% -> 14%
where the time goes in v4:
time: 56.4 us; the launch traced here: 55.8 us
  starting transfers between devices  18.3 us (32%)
  blocking collectives  16.8 us (30%)
  Pallas kernels  10 us (18%)
  waiting for transfers between devices  9.81 us (17%)
  other arithmetic  0.77 us (1%)
    ppermute x15, starting transfers between devices, permuted(): return lax.ppermute(values, AXES, pairs)  18.3 us
    all_to_all x1, blocking collectives, on_device(): lax.all_to_all(pieces, AXES, 0, 0, axis_index_groups=z_groups(), tiled=True)  16.8 us
    ppermute x15, waiting for transfers between devices, permuted(): return lax.ppermute(values, AXES, pairs)  9.81 us
    pallas_call x6, Pallas kernels, run_steps(): pl.pallas_call(functools.partial(steps_kernel, steps), out_shape=[pltpu.V...  9.61 us
  transfers between devices with their start and end apart: 15, of which 6 were waited for; matrix products, arithmetic and copies ran while one was open for 0% of the time, Pallas kernels for 14%

profile of v4, /device:TPU:2, one launch (start us, length us, event | category | flops | bytes accessed | tf_op | source)
XLA Modules:
  0.0 55.8 jit_solution(6717719342646691361)
XLA Ops:
  0.0 1.9 %shard_map.17 = (bf16[4,4,2,4,16,128]{5,4,3,2,1,0:T(8,128)(2,1)S(1)}, bf16[4,4,4,2,2,16,128]{6,5,4,3,2,1,0:T(8,128)(2,1)S(1)}) custom-call(f32[4,2,4,4,2,6,16,128]{7,6,5,4,3,2,1,0:T(8,128)} %bitcast.6), custom_call_target="tpu_custom_call" | custom-call | tf_op jit(solution)/shard_map/pallas_call | solution.py:132
  2.0 0.5 collective-permute-start
  2.5 1.9 %shard_map.18 = (bf16[4,4,2,4,16,128]{5,4,3,2,1,0:T(8,128)(2,1)S(1)}, bf16[4,4,2,4,16,128]{5,4,3,2,1,0:T(8,128)(2,1)S(1)}, bf16[4,4,2,4,16,128]{5,4,3,2,1,0:T(8,128)(2,1)S(1)}) custom-call(f32[4,2,4,4,2,6,16,128]{7,6,5,4,3,2,1,0:T(8,128)} %bitcast.7), custom_call_target="tpu_custom_call" | custom-call | tf_op jit(solution)/shard_map/pallas_call | solution.py:132
  4.7 0.4 collective-permute-start.3
  5.2 0.3 collective-permute-done.refs_0_
  5.4 1.6 %shard_map.19 = (bf16[4,4,2,4,16,128]{5,4,3,2,1,0:T(8,128)(2,1)S(1)}, bf16[4,4,4,2,16,128]{5,4,3,2,1,0:T(8,128)(2,1)S(1)}) custom-call(f32[4,2,4,4,2,6,16,128]{7,6,5,4,3,2,1,0:T(8,128)} %bitcast.8, bf16[4,4,2,4,16,128]{5,4,3,2,1,0:T(8,128)(2,1)S(1)} %collective-permute-done.refs_0_, bf16[4,4,4,2,2,16,128]{6,5,4,3,2,1,0:T(8,128)(2,1)S(1)} %collective-permute-done.1.refs_1_), custom_call_target="tpu_custom_call" | custom-call | tf_op jit(solution)/shard_map/pallas_call | solution.py:132
  7.1 2.0 %collective-permute-start.8 = (bf16[4,4,4,2,16,128]{5,4,3,2,1,0:T(8,128)(2,1)S(1)}, bf16[4,4,4,2,16,128]{5,4,3,2,1,0:T(8,128)(2,1)S(1)}, u32[]{:S(2)}, u32[]{:S(2)}) collective-permute-start(bf16[4,4,4,2,16,128]{5,4,3,2,1,0:T(8,128)(2,1)S(1)} %get-tuple-element.35), channel_id=1, source_target_pairs={{0,1},{1,0},{2,3},{3,2},{4,5},{5,4},{6,7},{7,6},{8,9},{9,8},{10,11... | collective-permute-start | bytes 1572872 | tf_op jit(solution)/shard_map/ppermute | solution.py:30
  9.1 2.1 %collective-permute-start.5 = (bf16[4,4,2,4,16,128]{5,4,3,2,1,0:T(8,128)(2,1)S(1)}, bf16[4,4,2,4,16,128]{5,4,3,2,1,0:T(8,128)(2,1)S(1)}, u32[]{:S(2)}, u32[]{:S(2)}) collective-permute-start(bf16[4,4,2,4,16,128]{5,4,3,2,1,0:T(8,128)(2,1)S(1)} %get-tuple-element.34), channel_id=1, source_target_pairs={{0,16},{1,17},{2,18},{3,19},{4,20},{5,21},{6,22},{7,23},{8,24},{9,... | collective-permute-start | bytes 1572872 | tf_op jit(solution)/shard_map/ppermute | solution.py:30
  11.2 1.2 %shard_map.20 = bf16[4,4,2,4,16,128]{5,4,3,2,1,0:T(8,128)(2,1)S(1)} custom-call(f32[4,2,4,4,2,6,16,128]{7,6,5,4,3,2,1,0:T(8,128)} %bitcast.9, bf16[4,4,2,4,16,128]{5,4,3,2,1,0:T(8,128)(2,1)S(1)} %collective-permute-done.2.refs_0_), custom_call_target="tpu_custom_call" | custom-call | tf_op jit(solution)/shard_map/pallas_call | solution.py:132
  12.5 1.3 %shard_map.21 = bf16[4,4,2,4,16,128]{5,4,3,2,1,0:T(8,128)(2,1)S(1)} custom-call(f32[4,2,4,4,2,6,16,128]{7,6,5,4,3,2,1,0:T(8,128)} %bitcast.10, bf16[4,4,2,4,16,128]{5,4,3,2,1,0:T(8,128)(2,1)S(1)} %collective-permute-done.3.refs_0_), custom_call_target="tpu_custom_call" | custom-call | tf_op jit(solution)/shard_map/pallas_call | solution.py:132
  13.8 2.1 %collective-permute-start.7 = (bf16[4,4,2,4,16,128]{5,4,3,2,1,0:T(8,128)(2,1)S(1)}, bf16[4,4,2,4,16,128]{5,4,3,2,1,0:T(8,128)(2,1)S(1)}, u32[]{:S(2)}, u32[]{:S(2)}) collective-permute-start(bf16[4,4,2,4,16,128]{5,4,3,2,1,0:T(8,128)(2,1)S(1)} %shard_map.21), channel_id=1, source_target_pairs={{0,24},{1,25},{2,26},{3,27},{4,28},{5,29},{6,30},{7,31},{8,0},{9,1... | collective-permute-start | bytes 1572872 | tf_op jit(solution)/shard_map/ppermute | solution.py:30
  15.9 1.6 %shard_map.22 = (f32[4,4,2,4,16,128]{5,4,3,2,1,0:T(8,128)S(1)}, f32[4,4,4,2,16,128]{5,4,3,2,1,0:T(8,128)S(1)}) custom-call(f32[4,2,4,4,2,6,16,128]{7,6,5,4,3,2,1,0:T(8,128)} %bitcast.11, bf16[4,4,2,4,16,128]{5,4,3,2,1,0:T(8,128)(2,1)S(1)} %collective-permute-done.4.refs_0_, bf16[4,4,4,2,2,16,128]{6,5,4,3,2,1,0:T(8,128)(2,1)S(1)} %collective-permute-done.1.refs_1_), custom_call_target="tpu_custom_call" | custom-call | tf_op jit(solution)/shard_map/pallas_call | solution.py:132
  17.6 1.6 %collective-permute-start.9 = (bf16[4,4,2,16,128]{4,3,2,1,0:T(8,128)(2,1)S(1)}, bf16[4,4,2,16,128]{4,3,2,1,0:T(8,128)(2,1)S(1)}, u32[]{:S(2)}, u32[]{:S(2)}) collective-permute-start(bf16[4,4,2,16,128]{4,3,2,1,0:T(8,128)(2,1)S(1)} %get-tuple-element.42), channel_id=1, source_target_pairs={{0,16},{1,17},{2,18},{3,19},{4,20},{5,21},{6,22},{7,23},{8,24},{9,... | collective-permute-start | bytes 393224 | tf_op jit(solution)/shard_map/ppermute | solution.py:30
  19.2 2.6 %collective-permute-start.10 = (bf16[4,4,2,16,128]{4,3,2,1,0:T(8,128)(2,1)S(1)}, bf16[4,4,2,16,128]{4,3,2,1,0:T(8,128)(2,1)S(1)}, u32[]{:S(2)}, u32[]{:S(2)}) collective-permute-start(bf16[4,4,2,16,128]{4,3,2,1,0:T(8,128)(2,1)S(1)} %get-tuple-element.43), channel_id=1, source_target_pairs={{0,8},{1,9},{2,10},{3,11},{4,12},{5,13},{6,14},{7,15},{8,16},{9,17... | collective-permute-start | bytes 393224 | tf_op jit(solution)/shard_map/ppermute | solution.py:30
  21.8 3.6 %collective-permute-done.6.p2 = bf16[4,4,2,4,16,128]{5,4,3,2,1,0:T(8,128)(2,1)S(1)} collective-permute-done((bf16[4,4,2,4,16,128]{5,4,3,2,1,0:T(8,128)(2,1)S(1)}, bf16[4,4,2,4,16,128]{5,4,3,2,1,0:T(8,128)(2,1)S(1)}, u32[]{:S(2)}, u32[]{:S(2)}) %collective-permute-start.6) | collective-permute-done | bytes 524320 | tf_op jit(solution)/shard_map/ppermute | solution.py:30
  25.6 1.3 %collective-permute-done.9.p1 = bf16[4,4,2,16,128]{4,3,2,1,0:T(8,128)(2,1)S(1)} collective-permute-done((bf16[4,4,2,16,128]{4,3,2,1,0:T(8,128)(2,1)S(1)}, bf16[4,4,2,16,128]{4,3,2,1,0:T(8,128)(2,1)S(1)}, u32[]{:S(2)}, u32[]{:S(2)}) %collective-permute-start.9) | collective-permute-done | bytes 131104 | tf_op jit(solution)/shard_map/ppermute | solution.py:30
  26.9 1.4 %collective-permute-done.10.p2 = bf16[4,4,2,16,128]{4,3,2,1,0:T(8,128)(2,1)S(1)} collective-permute-done((bf16[4,4,2,16,128]{4,3,2,1,0:T(8,128)(2,1)S(1)}, bf16[4,4,2,16,128]{4,3,2,1,0:T(8,128)(2,1)S(1)}, u32[]{:S(2)}, u32[]{:S(2)}) %collective-permute-start.10) | collective-permute-done | bytes 131104 | tf_op jit(solution)/shard_map/ppermute | solution.py:30
  28.4 3.3 %collective-permute-start.12 = (bf16[4,2,5,16,128]{4,3,2,1,0:T(8,128)(2,1)S(1)}, bf16[4,2,5,16,128]{4,3,2,1,0:T(8,128)(2,1)S(1)}, u32[]{:S(2)}, u32[]{:S(2)}) collective-permute-start(bf16[4,2,5,16,128]{4,3,2,1,0:T(8,128)(2,1)S(1)} %get-tuple-element.46), channel_id=1, source_target_pairs={{0,4},{1,5},{2,6},{3,7},{4,0},{5,1},{6,2},{7,3},{8,12},{9,13},{10,... | collective-permute-start | bytes 491528 | tf_op jit(solution)/shard_map/ppermute | solution.py:30
  31.7 0.7 %collective-permute-start.13 = (bf16[4,2,5,16,128]{4,3,2,1,0:T(8,128)(2,1)S(1)}, bf16[4,2,5,16,128]{4,3,2,1,0:T(8,128)(2,1)S(1)}, u32[]{:S(2)}, u32[]{:S(2)}) collective-permute-start(bf16[4,2,5,16,128]{4,3,2,1,0:T(8,128)(2,1)S(1)} %get-tuple-element.47), channel_id=1, source_target_pairs={{0,2},{1,3},{2,4},{3,5},{4,6},{5,7},{6,0},{7,1},{8,10},{9,11},{10,... | collective-permute-start | bytes 491528 | tf_op jit(solution)/shard_map/ppermute | solution.py:30
  32.4 2.6 %collective-permute-start.14 = (bf16[4,2,5,16,128]{4,3,2,1,0:T(8,128)(2,1)S(1)}, bf16[4,2,5,16,128]{4,3,2,1,0:T(8,128)(2,1)S(1)}, u32[]{:S(2)}, u32[]{:S(2)}) collective-permute-start(bf16[4,2,5,16,128]{4,3,2,1,0:T(8,128)(2,1)S(1)} %get-tuple-element.48), channel_id=1, source_target_pairs={{0,6},{1,7},{2,0},{3,1},{4,2},{5,3},{6,4},{7,5},{8,14},{9,15},{10,... | collective-permute-start | bytes 491528 | tf_op jit(solution)/shard_map/ppermute | solution.py:30
  34.9 0.4 collective-permute-done.12
  35.3 2.9 %collective-permute-done.13 = bf16[4,2,5,16,128]{4,3,2,1,0:T(8,128)(2,1)S(1)} collective-permute-done((bf16[4,2,5,16,128]{4,3,2,1,0:T(8,128)(2,1)S(1)}, bf16[4,2,5,16,128]{4,3,2,1,0:T(8,128)(2,1)S(1)}, u32[]{:S(2)}, u32[]{:S(2)}) %collective-permute-start.13) | collective-permute-done | bytes 163872 | tf_op jit(solution)/shard_map/ppermute | solution.py:30
  38.3 16.8 %all_to_all.5 = bf16[8,5,16,128]{3,2,1,0:T(8,128)(2,1)S(1)} all-to-all(bf16[8,5,16,128]{3,2,1,0:T(8,128)(2,1)S(1)} %bitcast.12), channel_id=1, replica_groups={{0,1,64,65,128,129,192,193},{2,3,66,67,130,131,194,195},{4,5,68,69,132,..., dimensions={0} | all-to-all | bytes 327680 | tf_op jit(solution)/shard_map/all_to_all | solution.py:237
  55.2 0.6 %pad_maximum_fusion = f32[6,16,128]{2,1,0:T(8,128)} fusion(f32[2,16,128]{2,1,0:T(8,128)S(1)} %bitcast_reduce_fusion, f32[4,16,128]{2,1,0:T(8,128)S(1)} %slice_reduce_fusion), kind=kLoop, calls=%fused_computation.3 | loop fusion | flops 12288 | bytes 98304 | tf_op jit(solution)/shard_map/concatenate | solution.py:240
  (22 shorter events, 1.1 us)
Async XLA Ops:
  1.9 3.5 %collective-permute-start.1 = (bf16[4,4,4,2,2,16,128]{6,5,4,3,2,1,0:T(8,128)(2,1)S(1)}, bf16[4,4,4,2,2,16,128]{6,5,4,3,2,1,0:T(8,128)(2,1)S(1)}, u32[]{:S(2)}, u32[]{:S(2)}) collective-permute-start(bf16[4,4,4,2,2,16,128]{6,5,4,3,2,1,0:T(8,128)(2,1)S(1)} %get-tuple-element.28), channel_id=1, source_target_pairs={{0,32},{1,33},{2,34},{3,35},{4,36},{5,37},{6,38},{7,39},{8,40},{9,... | collective-permute-start | bytes 3145736 | tf_op jit(solution)/shard_map/ppermute | solution.py:30
  2.0 3.4 %collective-permute-start = (bf16[4,4,2,4,16,128]{5,4,3,2,1,0:T(8,128)(2,1)S(1)}, bf16[4,4,2,4,16,128]{5,4,3,2,1,0:T(8,128)(2,1)S(1)}, u32[]{:S(2)}, u32[]{:S(2)}) collective-permute-start(bf16[4,4,2,4,16,128]{5,4,3,2,1,0:T(8,128)(2,1)S(1)} %get-tuple-element.27), channel_id=1, source_target_pairs={{0,32},{1,33},{2,34},{3,35},{4,36},{5,37},{6,38},{7,39},{8,40},{9,... | collective-permute-start | bytes 1572872 | tf_op jit(solution)/shard_map/ppermute | solution.py:30
  4.5 6.7 %collective-permute-start.2 = (bf16[4,4,2,4,16,128]{5,4,3,2,1,0:T(8,128)(2,1)S(1)}, bf16[4,4,2,4,16,128]{5,4,3,2,1,0:T(8,128)(2,1)S(1)}, u32[]{:S(2)}, u32[]{:S(2)}) collective-permute-start(bf16[4,4,2,4,16,128]{5,4,3,2,1,0:T(8,128)(2,1)S(1)} %get-tuple-element.30), channel_id=1, source_target_pairs={{0,32},{1,33},{2,34},{3,35},{4,36},{5,37},{6,38},{7,39},{8,40},{9,... | collective-permute-start | bytes 1572872 | tf_op jit(solution)/shard_map/ppermute | solution.py:30
  4.7 7.9 %collective-permute-start.3 = (bf16[4,4,2,4,16,128]{5,4,3,2,1,0:T(8,128)(2,1)S(1)}, bf16[4,4,2,4,16,128]{5,4,3,2,1,0:T(8,128)(2,1)S(1)}, u32[]{:S(2)}, u32[]{:S(2)}) collective-permute-start(bf16[4,4,2,4,16,128]{5,4,3,2,1,0:T(8,128)(2,1)S(1)} %get-tuple-element.31), channel_id=1, source_target_pairs={{0,32},{1,33},{2,34},{3,35},{4,36},{5,37},{6,38},{7,39},{8,40},{9,... | collective-permute-start | bytes 1572872 | tf_op jit(solution)/shard_map/ppermute | solution.py:30
  5.1 10.8 %collective-permute-start.4 = (bf16[4,4,2,4,16,128]{5,4,3,2,1,0:T(8,128)(2,1)S(1)}, bf16[4,4,2,4,16,128]{5,4,3,2,1,0:T(8,128)(2,1)S(1)}, u32[]{:S(2)}, u32[]{:S(2)}) collective-permute-start(bf16[4,4,2,4,16,128]{5,4,3,2,1,0:T(8,128)(2,1)S(1)} %get-tuple-element.32), channel_id=1, source_target_pairs={{0,32},{1,33},{2,34},{3,35},{4,36},{5,37},{6,38},{7,39},{8,40},{9,... | collective-permute-start | bytes 1572872 | tf_op jit(solution)/shard_map/ppermute | solution.py:30
  7.1 10.4 %collective-permute-start.8 = (bf16[4,4,4,2,16,128]{5,4,3,2,1,0:T(8,128)(2,1)S(1)}, bf16[4,4,4,2,16,128]{5,4,3,2,1,0:T(8,128)(2,1)S(1)}, u32[]{:S(2)}, u32[]{:S(2)}) collective-permute-start(bf16[4,4,4,2,16,128]{5,4,3,2,1,0:T(8,128)(2,1)S(1)} %get-tuple-element.35), channel_id=1, source_target_pairs={{0,1},{1,0},{2,3},{3,2},{4,5},{5,4},{6,7},{7,6},{8,9},{9,8},{10,11... | collective-permute-start | bytes 1572872 | tf_op jit(solution)/shard_map/ppermute | solution.py:30
  9.1 12.8 %collective-permute-start.5 = (bf16[4,4,2,4,16,128]{5,4,3,2,1,0:T(8,128)(2,1)S(1)}, bf16[4,4,2,4,16,128]{5,4,3,2,1,0:T(8,128)(2,1)S(1)}, u32[]{:S(2)}, u32[]{:S(2)}) collective-permute-start(bf16[4,4,2,4,16,128]{5,4,3,2,1,0:T(8,128)(2,1)S(1)} %get-tuple-element.34), channel_id=1, source_target_pairs={{0,16},{1,17},{2,18},{3,19},{4,20},{5,21},{6,22},{7,23},{8,24},{9,... | collective-permute-start | bytes 1572872 | tf_op jit(solution)/shard_map/ppermute | solution.py:30
  12.4 13.0 %collective-permute-start.6 = (bf16[4,4,2,4,16,128]{5,4,3,2,1,0:T(8,128)(2,1)S(1)}, bf16[4,4,2,4,16,128]{5,4,3,2,1,0:T(8,128)(2,1)S(1)}, u32[]{:S(2)}, u32[]{:S(2)}) collective-permute-start(bf16[4,4,2,4,16,128]{5,4,3,2,1,0:T(8,128)(2,1)S(1)} %shard_map.20), channel_id=1, source_target_pairs={{0,8},{1,9},{2,10},{3,11},{4,12},{5,13},{6,14},{7,15},{8,16},{9,17... | collective-permute-start | bytes 1572872 | tf_op jit(solution)/shard_map/ppermute | solution.py:30
  13.8 11.6 %collective-permute-start.7 = (bf16[4,4,2,4,16,128]{5,4,3,2,1,0:T(8,128)(2,1)S(1)}, bf16[4,4,2,4,16,128]{5,4,3,2,1,0:T(8,128)(2,1)S(1)}, u32[]{:S(2)}, u32[]{:S(2)}) collective-permute-start(bf16[4,4,2,4,16,128]{5,4,3,2,1,0:T(8,128)(2,1)S(1)} %shard_map.21), channel_id=1, source_target_pairs={{0,24},{1,25},{2,26},{3,27},{4,28},{5,29},{6,30},{7,31},{8,0},{9,1... | collective-permute-start | bytes 1572872 | tf_op jit(solution)/shard_map/ppermute | solution.py:30
  17.6 9.3 %collective-permute-start.9 = (bf16[4,4,2,16,128]{4,3,2,1,0:T(8,128)(2,1)S(1)}, bf16[4,4,2,16,128]{4,3,2,1,0:T(8,128)(2,1)S(1)}, u32[]{:S(2)}, u32[]{:S(2)}) collective-permute-start(bf16[4,4,2,16,128]{4,3,2,1,0:T(8,128)(2,1)S(1)} %get-tuple-element.42), channel_id=1, source_target_pairs={{0,16},{1,17},{2,18},{3,19},{4,20},{5,21},{6,22},{7,23},{8,24},{9,... | collective-permute-start | bytes 393224 | tf_op jit(solution)/shard_map/ppermute | solution.py:30
  19.2 9.0 %collective-permute-start.10 = (bf16[4,4,2,16,128]{4,3,2,1,0:T(8,128)(2,1)S(1)}, bf16[4,4,2,16,128]{4,3,2,1,0:T(8,128)(2,1)S(1)}, u32[]{:S(2)}, u32[]{:S(2)}) collective-permute-start(bf16[4,4,2,16,128]{4,3,2,1,0:T(8,128)(2,1)S(1)} %get-tuple-element.43), channel_id=1, source_target_pairs={{0,8},{1,9},{2,10},{3,11},{4,12},{5,13},{6,14},{7,15},{8,16},{9,17... | collective-permute-start | bytes 393224 | tf_op jit(solution)/shard_map/ppermute | solution.py:30
  21.8 6.5 %collective-permute-start.11 = (bf16[4,4,2,16,128]{4,3,2,1,0:T(8,128)(2,1)S(1)}, bf16[4,4,2,16,128]{4,3,2,1,0:T(8,128)(2,1)S(1)}, u32[]{:S(2)}, u32[]{:S(2)}) collective-permute-start(bf16[4,4,2,16,128]{4,3,2,1,0:T(8,128)(2,1)S(1)} %get-tuple-element.44), channel_id=1, source_target_pairs={{0,24},{1,25},{2,26},{3,27},{4,28},{5,29},{6,30},{7,31},{8,0},{9,1... | collective-permute-start | bytes 393224 | tf_op jit(solution)/shard_map/ppermute | solution.py:30
  28.4 6.9 %collective-permute-start.12 = (bf16[4,2,5,16,128]{4,3,2,1,0:T(8,128)(2,1)S(1)}, bf16[4,2,5,16,128]{4,3,2,1,0:T(8,128)(2,1)S(1)}, u32[]{:S(2)}, u32[]{:S(2)}) collective-permute-start(bf16[4,2,5,16,128]{4,3,2,1,0:T(8,128)(2,1)S(1)} %get-tuple-element.46), channel_id=1, source_target_pairs={{0,4},{1,5},{2,6},{3,7},{4,0},{5,1},{6,2},{7,3},{8,12},{9,13},{10,... | collective-permute-start | bytes 491528 | tf_op jit(solution)/shard_map/ppermute | solution.py:30
  31.7 6.5 %collective-permute-start.13 = (bf16[4,2,5,16,128]{4,3,2,1,0:T(8,128)(2,1)S(1)}, bf16[4,2,5,16,128]{4,3,2,1,0:T(8,128)(2,1)S(1)}, u32[]{:S(2)}, u32[]{:S(2)}) collective-permute-start(bf16[4,2,5,16,128]{4,3,2,1,0:T(8,128)(2,1)S(1)} %get-tuple-element.47), channel_id=1, source_target_pairs={{0,2},{1,3},{2,4},{3,5},{4,6},{5,7},{6,0},{7,1},{8,10},{9,11},{10,... | collective-permute-start | bytes 491528 | tf_op jit(solution)/shard_map/ppermute | solution.py:30
  32.4 5.9 %collective-permute-start.14 = (bf16[4,2,5,16,128]{4,3,2,1,0:T(8,128)(2,1)S(1)}, bf16[4,2,5,16,128]{4,3,2,1,0:T(8,128)(2,1)S(1)}, u32[]{:S(2)}, u32[]{:S(2)}) collective-permute-start(bf16[4,2,5,16,128]{4,3,2,1,0:T(8,128)(2,1)S(1)} %get-tuple-element.48), channel_id=1, source_target_pairs={{0,6},{1,7},{2,0},{3,1},{4,2},{5,3},{6,4},{7,5},{8,14},{9,15},{10,... | collective-permute-start | bytes 491528 | tf_op jit(solution)/shard_map/ppermute | solution.py:30

commit v5 on v4

--- a/solution.py
+++ b/solution.py
@@ -68,52 +68,69 @@
     return core, jnp.where(core == 0, x, y), jnp.where(core == 0, y, x), lax.rem(group, ZL)
 
 
-PAIR, SENT, KEPT = "pair", "sent", "kept"
+SENT, KEPT = "sent", "kept"
 
 
 def shape_of(what, rows):
-    if what == PAIR:
-        return (ZH, X, Y, ZL, SLABS - PLAIN, rows, QB)
     if what in (SENT, KEPT):
         return (ZH, X, Y, ZL, rows, QB)
     return (ZH, RING, ZL, PLAIN, rows, QB)
 
 
-def steps_kernel(steps, grads, *refs):
-    n_received = sum(added for _, added in steps)
-    received, outs = list(refs[:n_received]), refs[n_received : n_received + len(steps)]
-    helds, sems = refs[n_received + len(steps) : -1], refs[-1]
-    core, first, second, zl = place()
+def slabs_of(what):
+    return X * Y * ZL if what in (SENT, KEPT) else RING * ZL * PLAIN
+
+
+def fetch(grads, what, half, at, zl, zh, target, sem):
+    if what in (SENT, KEPT):
+        slab = PLAIN + (1 - zl if what == SENT else zl)
+        copy = pltpu.make_async_copy(grads.at[zh, half, :, :, :, slab], target, sem)
+        copy.start()
+        return copy
+    copy = pltpu.make_async_copy(grads.at[zh, half, at, :, :, pl.ds(0, PLAIN)], target, sem)
+    along_y = pltpu.make_async_copy(grads.at[zh, half, :, at, :, pl.ds(0, PLAIN)], target, sem)
+    pl.when(half == 0)(copy.start)
+    pl.when(half != 0)(along_y.start)
+    return copy
+
+
+def fetch_all(grads, steps, half, first, zl, helds, sems):
     copies = []
-    for k, (what, added) in enumerate(steps):
-        half = core if added else 1 - core
-        for zh in range(ZH):
-            target, sem = helds[k].at[zh], sems.at[k, zh]
-            if what == PAIR:
-                copy = pltpu.make_async_copy(grads.at[zh, half, :, :, :, pl.ds(PLAIN, SLABS - PLAIN)], target, sem)
-                copy.start()
-            elif what in (SENT, KEPT):
-                slab = PLAIN + (1 - zl if what == SENT else zl)
-                copy = pltpu.make_async_copy(grads.at[zh, half, :, :, :, slab], target, sem)
-                copy.start()
-            else:
-                at = lax.rem((first if added else second) + what, RING)
-                copy = pltpu.make_async_copy(grads.at[zh, half, at, :, :, pl.ds(0, PLAIN)], target, sem)
-                along_y = pltpu.make_async_copy(grads.at[zh, half, :, at, :, pl.ds(0, PLAIN)], target, sem)
-                pl.when(half == 0)(copy.start)
-                pl.when(half != 0)(along_y.start)
-            copies.append(copy)
-    copies = iter(copies)
-    for k, (what, added) in enumerate(steps):
-        source = received.pop(0) if added else None
+    for k, what in enumerate(steps):
+        at = first if what in (SENT, KEPT) else lax.rem(first + what, RING)
+        for zh in range(ZH):
+            copies.append(fetch(grads, what, half, at, zl, zh, helds[k].at[zh], sems.at[k, zh]))
+    return copies
+
+
+def cast_kernel(groups, grads, *refs):
+    outs, helds, sems = refs[: len(groups)], refs[len(groups) : -1], refs[-1]
+    core, _, second, zl = place()
+    steps = [what for group in groups for what in group]
+    copies = iter(fetch_all(grads, steps, 1 - core, second, zl, helds, sems))
+    helds = iter(helds)
+    for group, out in zip(groups, outs):
+        begin = 0
+        for what in group:
+            held, end = next(helds), begin + slabs_of(what)
+            for zh in range(ZH):
+                next(copies).wait()
+                out[zh, begin:end] = held[zh].reshape(end - begin, *held.shape[-2:]).astype(out.dtype)
+            begin = end
+
+
+def add_kernel(group, grads, received, *refs):
+    outs, helds, sems = refs[: len(group)], refs[len(group) : -1], refs[-1]
+    core, first, _, zl = place()
+    copies = iter(fetch_all(grads, group, core, first, zl, helds, sems))
+    begin = 0
+    for what, out, held in zip(group, outs, helds):
+        end = begin + slabs_of(what)
         for zh in range(ZH):
             next(copies).wait()
-            value = helds[k][zh]
-            if added and what in (SENT, KEPT):
-                value += source[zh, :, :, :, 1 - zl if what == SENT else zl].astype(F32)
-            elif added:
-                value += source[zh].astype(F32)
-            outs[k][zh] = value.astype(outs[k].dtype)
+            value = held[zh] + received[zh, begin:end].reshape(held.shape[1:]).astype(F32)
+            out[zh] = value.astype(out.dtype)
+        begin = end
 
 
 VMEM = pl.BlockSpec(memory_space=pltpu.VMEM)
@@ -125,19 +142,31 @@
     return pltpu.with_memory_space_constraint(values, pltpu.VMEM)
 
 
-def run_steps(grads, steps, received):
+def run_on_grads(kernel, grads, steps, out_shape, received=()):
     rows = grads.shape[-2]
-    shapes = [shape_of(what, rows) for what, _ in steps]
-    types = [F32 if added and what in (0, KEPT) else BF16 for what, added in steps]
-    return pl.pallas_call(
-        functools.partial(steps_kernel, steps),
-        out_shape=[pltpu.VMEM(shape, dtype) for shape, dtype in zip(shapes, types)],
+    return pl.pallas_call(
+        kernel,
+        out_shape=out_shape,
         in_specs=[pl.BlockSpec(memory_space=pltpu.HBM)] + [VMEM] * len(received),
-        out_specs=[VMEM] * len(steps),
-        scratch_shapes=[pltpu.VMEM(shape, F32) for shape in shapes] + [pltpu.SemaphoreType.DMA((len(steps), ZH))],
+        out_specs=[VMEM] * len(out_shape),
+        scratch_shapes=[pltpu.VMEM(shape_of(what, rows), F32) for what in steps]
+        + [pltpu.SemaphoreType.DMA((len(steps), ZH))],
         compiler_params=PARAMS,
         cost_estimate=COST,
     )(pltpu.with_memory_space_constraint(grads, pltpu.HBM), *received)
+
+
+def run_cast(grads, groups):
+    rows = grads.shape[-2]
+    out_shape = [pltpu.VMEM((ZH, sum(map(slabs_of, group)), rows, QB), BF16) for group in groups]
+    steps = [what for group in groups for what in group]
+    return run_on_grads(functools.partial(cast_kernel, groups), grads, steps, out_shape)
+
+
+def run_add(grads, group, received):
+    rows = grads.shape[-2]
+    out_shape = [pltpu.VMEM(shape_of(what, rows), F32 if what in (0, KEPT) else BF16) for what in group]
+    return run_on_grads(functools.partial(add_kernel, group), grads, group, out_shape, [received])
 
 
 def paired_kernel(kept, arrived, *outs):
@@ -203,23 +232,18 @@
 def on_device(grads):
     rows = grads.shape[1] // (ZH * CORE * X * Y * ZL * SLABS * QB)
     grads = grads.reshape(ZH, CORE, X, Y, ZL, SLABS, rows, QB)
-    order = (
-        ((2, False), (PAIR, False)),
-        ((1, False), (3, False), (0, False)),
-        ((2, True), (SENT, True)),
-        ((1, True),),
-        ((3, True),),
-        ((0, True), (KEPT, True)),
-    )
-    crossed, arrived, own = {}, {}, {}
-    for steps in order:
-        received = [crossed[PAIR if what in (SENT, KEPT) else what] for what, added in steps if added]
-        outs = run_steps(grads, steps, received)
+    groups = ((2, SENT), (1, 3), (0, KEPT))
+    crossed = []
+    for some in (groups[:1], groups[1:]):
+        outs = run_cast(grads, some)
         grads = lax.optimization_barrier((grads, *outs))[0]
-        for (what, added), out in zip(steps, outs):
-            if not added:
-                crossed[what] = to_other_core(out)
-            elif what == SENT:
+        crossed += [to_other_core(out) for out in outs]
+    arrived, own = {}, {}
+    for group, received in zip(groups, crossed):
+        outs = run_add(grads, group, received)
+        grads = lax.optimization_barrier((grads, *outs))[0]
+        for what, out in zip(group, outs):
+            if what == SENT:
                 arrived[what] = to_z_partner(out)
             elif what in (0, KEPT):
                 own[what] = out

time: 56.4 us -> 55.5 us (0.984)
  Pallas kernels: 10 us -> 9.17 us
  waiting for transfers between devices: 9.81 us -> 10.5 us
  starting transfers between devices: 18.3 us -> 17.7 us
    pallas_call x6 -> x5, Pallas kernels: 9.61 us -> 8.73 us  [run_on_grads(): pl.pallas_call(kernel, out_shape=out_shape, in_specs=[pl.BlockSpec(memory...]
    ppermute x15 -> x13, waiting for transfers between devices: 9.81 us -> 10.5 us  [permuted(): return lax.ppermute(values, AXES, pairs)]
    ppermute x15 -> x13, starting transfers between devices: 18.3 us -> 17.7 us  [permuted(): return lax.ppermute(values, AXES, pairs)]
  transfers between devices with their start and end apart: 15 -> 13, of which waited for: 6 -> 5; matrix products, arithmetic and copies ran while one was open for 0% -> 0% of each run, Pallas kernels for 14% -> 14%
where the time goes in v5:
time: 55.5 us; the launch traced here: 55.1 us
  starting transfers between devices  17.7 us (32%)
  blocking collectives  16.8 us (30%)
  waiting for transfers between devices  10.5 us (19%)
  Pallas kernels  9.17 us (17%)
  other arithmetic  0.77 us (1%)
    ppermute x13, starting transfers between devices, permuted(): return lax.ppermute(values, AXES, pairs)  17.7 us
    all_to_all x1, blocking collectives, on_device(): lax.all_to_all(pieces, AXES, 0, 0, axis_index_groups=z_groups(), tiled=True)  16.8 us
    ppermute x13, waiting for transfers between devices, permuted(): return lax.ppermute(values, AXES, pairs)  10.5 us
    pallas_call x5, Pallas kernels, run_on_grads(): pl.pallas_call(kernel, out_shape=out_shape, in_specs=[pl.BlockSpec(memory...  8.73 us
  transfers between devices with their start and end apart: 13, of which 5 were waited for; matrix products, arithmetic and copies ran while one was open for 0% of the time, Pallas kernels for 14%

profile of v5, /device:TPU:2, one launch (start us, length us, event | category | flops | bytes accessed | tf_op | source)
XLA Modules:
  0.0 55.1 jit_solution(6742227839224934838)
XLA Ops:
  0.0 1.6 %shard_map.17 = bf16[4,64,16,128]{3,2,1,0:T(8,128)(2,1)S(1)} custom-call(f32[4,2,4,4,2,6,16,128]{7,6,5,4,3,2,1,0:T(8,128)} %bitcast.6), custom_call_target="tpu_custom_call" | custom-call | tf_op jit(solution)/shard_map/pallas_call | solution.py:147
  1.7 2.3 %shard_map.18 = (bf16[4,64,16,128]{3,2,1,0:T(8,128)(2,1)S(1)}, bf16[4,64,16,128]{3,2,1,0:T(8,128)(2,1)S(1)}) custom-call(f32[4,2,4,4,2,6,16,128]{7,6,5,4,3,2,1,0:T(8,128)} %bitcast.7), custom_call_target="tpu_custom_call" | custom-call | tf_op jit(solution)/shard_map/pallas_call | solution.py:147
  4.1 0.5 collective-permute-start.1
  4.7 1.6 %shard_map.19 = (bf16[4,4,2,4,16,128]{5,4,3,2,1,0:T(8,128)(2,1)S(1)}, bf16[4,4,4,2,16,128]{5,4,3,2,1,0:T(8,128)(2,1)S(1)}) custom-call(f32[4,2,4,4,2,6,16,128]{7,6,5,4,3,2,1,0:T(8,128)} %bitcast.8, bf16[4,64,16,128]{3,2,1,0:T(8,128)(2,1)S(1)} %collective-permute-done.received), custom_call_target="tpu_custom_call" | custom-call | tf_op jit(solution)/shard_map/pallas_call | solution.py:147
  6.3 2.0 %collective-permute-start.6 = (bf16[4,4,4,2,16,128]{5,4,3,2,1,0:T(8,128)(2,1)S(1)}, bf16[4,4,4,2,16,128]{5,4,3,2,1,0:T(8,128)(2,1)S(1)}, u32[]{:S(2)}, u32[]{:S(2)}) collective-permute-start(bf16[4,4,4,2,16,128]{5,4,3,2,1,0:T(8,128)(2,1)S(1)} %get-tuple-element.30), channel_id=1, source_target_pairs={{0,1},{1,0},{2,3},{3,2},{4,5},{5,4},{6,7},{7,6},{8,9},{9,8},{10,11... | collective-permute-start | bytes 1572872 | tf_op jit(solution)/shard_map/ppermute | solution.py:30
  8.3 2.1 %collective-permute-start.3 = (bf16[4,4,2,4,16,128]{5,4,3,2,1,0:T(8,128)(2,1)S(1)}, bf16[4,4,2,4,16,128]{5,4,3,2,1,0:T(8,128)(2,1)S(1)}, u32[]{:S(2)}, u32[]{:S(2)}) collective-permute-start(bf16[4,4,2,4,16,128]{5,4,3,2,1,0:T(8,128)(2,1)S(1)} %get-tuple-element.29), channel_id=1, source_target_pairs={{0,16},{1,17},{2,18},{3,19},{4,20},{5,21},{6,22},{7,23},{8,24},{9,... | collective-permute-start | bytes 1572872 | tf_op jit(solution)/shard_map/ppermute | solution.py:30
  10.4 1.6 %shard_map.20 = (bf16[4,4,2,4,16,128]{5,4,3,2,1,0:T(8,128)(2,1)S(1)}, bf16[4,4,2,4,16,128]{5,4,3,2,1,0:T(8,128)(2,1)S(1)}) custom-call(f32[4,2,4,4,2,6,16,128]{7,6,5,4,3,2,1,0:T(8,128)} %bitcast.9, bf16[4,64,16,128]{3,2,1,0:T(8,128)(2,1)S(1)} %collective-permute-done.1.received), custom_call_target="tpu_custom_call" | custom-call | tf_op jit(solution)/shard_map/pallas_call | solution.py:147
  12.1 2.0 %collective-permute-start.5 = (bf16[4,4,2,4,16,128]{5,4,3,2,1,0:T(8,128)(2,1)S(1)}, bf16[4,4,2,4,16,128]{5,4,3,2,1,0:T(8,128)(2,1)S(1)}, u32[]{:S(2)}, u32[]{:S(2)}) collective-permute-start(bf16[4,4,2,4,16,128]{5,4,3,2,1,0:T(8,128)(2,1)S(1)} %get-tuple-element.33), channel_id=1, source_target_pairs={{0,24},{1,25},{2,26},{3,27},{4,28},{5,29},{6,30},{7,31},{8,0},{9,1... | collective-permute-start | bytes 1572872 | tf_op jit(solution)/shard_map/ppermute | solution.py:30
  14.1 1.6 %shard_map.21 = (f32[4,4,2,4,16,128]{5,4,3,2,1,0:T(8,128)S(1)}, f32[4,4,4,2,16,128]{5,4,3,2,1,0:T(8,128)S(1)}) custom-call(f32[4,2,4,4,2,6,16,128]{7,6,5,4,3,2,1,0:T(8,128)} %bitcast.10, bf16[4,64,16,128]{3,2,1,0:T(8,128)(2,1)S(1)} %collective-permute-done.2.received), custom_call_target="tpu_custom_call" | custom-call | tf_op jit(solution)/shard_map/pallas_call | solution.py:147
  15.8 0.1 shard_map.23
  15.9 2.0 %collective-permute-start.7 = (bf16[4,4,2,16,128]{4,3,2,1,0:T(8,128)(2,1)S(1)}, bf16[4,4,2,16,128]{4,3,2,1,0:T(8,128)(2,1)S(1)}, u32[]{:S(2)}, u32[]{:S(2)}) collective-permute-start(bf16[4,4,2,16,128]{4,3,2,1,0:T(8,128)(2,1)S(1)} %get-tuple-element.38), channel_id=1, source_target_pairs={{0,16},{1,17},{2,18},{3,19},{4,20},{5,21},{6,22},{7,23},{8,24},{9,... | collective-permute-start | bytes 393224 | tf_op jit(solution)/shard_map/ppermute | solution.py:30
  17.9 2.2 %collective-permute-start.8 = (bf16[4,4,2,16,128]{4,3,2,1,0:T(8,128)(2,1)S(1)}, bf16[4,4,2,16,128]{4,3,2,1,0:T(8,128)(2,1)S(1)}, u32[]{:S(2)}, u32[]{:S(2)}) collective-permute-start(bf16[4,4,2,16,128]{4,3,2,1,0:T(8,128)(2,1)S(1)} %get-tuple-element.39), channel_id=1, source_target_pairs={{0,8},{1,9},{2,10},{3,11},{4,12},{5,13},{6,14},{7,15},{8,16},{9,17... | collective-permute-start | bytes 393224 | tf_op jit(solution)/shard_map/ppermute | solution.py:30
  20.1 4.6 %collective-permute-done.4.p2 = bf16[4,4,2,4,16,128]{5,4,3,2,1,0:T(8,128)(2,1)S(1)} collective-permute-done((bf16[4,4,2,4,16,128]{5,4,3,2,1,0:T(8,128)(2,1)S(1)}, bf16[4,4,2,4,16,128]{5,4,3,2,1,0:T(8,128)(2,1)S(1)}, u32[]{:S(2)}, u32[]{:S(2)}) %collective-permute-start.4) | collective-permute-done | bytes 524320 | tf_op jit(solution)/shard_map/ppermute | solution.py:30
  24.7 0.2 shard_map.22.plain
  24.9 1.3 %collective-permute-done.7.p1 = bf16[4,4,2,16,128]{4,3,2,1,0:T(8,128)(2,1)S(1)} collective-permute-done((bf16[4,4,2,16,128]{4,3,2,1,0:T(8,128)(2,1)S(1)}, bf16[4,4,2,16,128]{4,3,2,1,0:T(8,128)(2,1)S(1)}, u32[]{:S(2)}, u32[]{:S(2)}) %collective-permute-start.7) | collective-permute-done | bytes 131104 | tf_op jit(solution)/shard_map/ppermute | solution.py:30
  26.2 1.4 %collective-permute-done.8.p2 = bf16[4,4,2,16,128]{4,3,2,1,0:T(8,128)(2,1)S(1)} collective-permute-done((bf16[4,4,2,16,128]{4,3,2,1,0:T(8,128)(2,1)S(1)}, bf16[4,4,2,16,128]{4,3,2,1,0:T(8,128)(2,1)S(1)}, u32[]{:S(2)}, u32[]{:S(2)}) %collective-permute-start.8) | collective-permute-done | bytes 131104 | tf_op jit(solution)/shard_map/ppermute | solution.py:30
  27.5 0.1 shard_map.24
  27.6 3.3 %collective-permute-start.10 = (bf16[4,2,5,16,128]{4,3,2,1,0:T(8,128)(2,1)S(1)}, bf16[4,2,5,16,128]{4,3,2,1,0:T(8,128)(2,1)S(1)}, u32[]{:S(2)}, u32[]{:S(2)}) collective-permute-start(bf16[4,2,5,16,128]{4,3,2,1,0:T(8,128)(2,1)S(1)} %get-tuple-element.42), channel_id=1, source_target_pairs={{0,4},{1,5},{2,6},{3,7},{4,0},{5,1},{6,2},{7,3},{8,12},{9,13},{10,... | collective-permute-start | bytes 491528 | tf_op jit(solution)/shard_map/ppermute | solution.py:30
  30.9 0.7 %collective-permute-start.11 = (bf16[4,2,5,16,128]{4,3,2,1,0:T(8,128)(2,1)S(1)}, bf16[4,2,5,16,128]{4,3,2,1,0:T(8,128)(2,1)S(1)}, u32[]{:S(2)}, u32[]{:S(2)}) collective-permute-start(bf16[4,2,5,16,128]{4,3,2,1,0:T(8,128)(2,1)S(1)} %get-tuple-element.43), channel_id=1, source_target_pairs={{0,2},{1,3},{2,4},{3,5},{4,6},{5,7},{6,0},{7,1},{8,10},{9,11},{10,... | collective-permute-start | bytes 491528 | tf_op jit(solution)/shard_map/ppermute | solution.py:30
  31.6 2.6 %collective-permute-start.12 = (bf16[4,2,5,16,128]{4,3,2,1,0:T(8,128)(2,1)S(1)}, bf16[4,2,5,16,128]{4,3,2,1,0:T(8,128)(2,1)S(1)}, u32[]{:S(2)}, u32[]{:S(2)}) collective-permute-start(bf16[4,2,5,16,128]{4,3,2,1,0:T(8,128)(2,1)S(1)} %get-tuple-element.44), channel_id=1, source_target_pairs={{0,6},{1,7},{2,0},{3,1},{4,2},{5,3},{6,4},{7,5},{8,14},{9,15},{10,... | collective-permute-start | bytes 491528 | tf_op jit(solution)/shard_map/ppermute | solution.py:30
  34.2 0.4 collective-permute-done.10
  34.6 2.9 %collective-permute-done.11 = bf16[4,2,5,16,128]{4,3,2,1,0:T(8,128)(2,1)S(1)} collective-permute-done((bf16[4,2,5,16,128]{4,3,2,1,0:T(8,128)(2,1)S(1)}, bf16[4,2,5,16,128]{4,3,2,1,0:T(8,128)(2,1)S(1)}, u32[]{:S(2)}, u32[]{:S(2)}) %collective-permute-start.11) | collective-permute-done | bytes 163872 | tf_op jit(solution)/shard_map/ppermute | solution.py:30
  37.6 16.8 %all_to_all.5 = bf16[8,5,16,128]{3,2,1,0:T(8,128)(2,1)S(1)} all-to-all(bf16[8,5,16,128]{3,2,1,0:T(8,128)(2,1)S(1)} %bitcast.11), channel_id=1, replica_groups={{0,1,64,65,128,129,192,193},{2,3,66,67,130,131,194,195},{4,5,68,69,132,..., dimensions={0} | all-to-all | bytes 327680 | tf_op jit(solution)/shard_map/all_to_all | solution.py:261
  54.4 0.6 %pad_maximum_fusion = f32[6,16,128]{2,1,0:T(8,128)} fusion(f32[2,16,128]{2,1,0:T(8,128)S(1)} %bitcast_reduce_fusion, f32[4,16,128]{2,1,0:T(8,128)S(1)} %slice_reduce_fusion), kind=kLoop, calls=%fused_computation.3 | loop fusion | flops 12288 | bytes 98304 | tf_op jit(solution)/shard_map/concatenate | solution.py:264
  (17 shorter events, 0.5 us)
Async XLA Ops:
  1.6 3.1 %collective-permute-start = (bf16[4,64,16,128]{3,2,1,0:T(8,128)(2,1)S(1)}, bf16[4,64,16,128]{3,2,1,0:T(8,128)(2,1)S(1)}, u32[]{:S(2)}, u32[]{:S(2)}) collective-permute-start(bf16[4,64,16,128]{3,2,1,0:T(8,128)(2,1)S(1)} %shard_map.17), channel_id=1, source_target_pairs={{0,32},{1,33},{2,34},{3,35},{4,36},{5,37},{6,38},{7,39},{8,40},{9,... | collective-permute-start | bytes 3145736 | tf_op jit(solution)/shard_map/ppermute | solution.py:30
  4.1 6.4 %collective-permute-start.1 = (bf16[4,64,16,128]{3,2,1,0:T(8,128)(2,1)S(1)}, bf16[4,64,16,128]{3,2,1,0:T(8,128)(2,1)S(1)}, u32[]{:S(2)}, u32[]{:S(2)}) collective-permute-start(bf16[4,64,16,128]{3,2,1,0:T(8,128)(2,1)S(1)} %get-tuple-element.26), channel_id=1, source_target_pairs={{0,32},{1,33},{2,34},{3,35},{4,36},{5,37},{6,38},{7,39},{8,40},{9,... | collective-permute-start | bytes 3145736 | tf_op jit(solution)/shard_map/ppermute | solution.py:30
  4.6 9.6 %collective-permute-start.2 = (bf16[4,64,16,128]{3,2,1,0:T(8,128)(2,1)S(1)}, bf16[4,64,16,128]{3,2,1,0:T(8,128)(2,1)S(1)}, u32[]{:S(2)}, u32[]{:S(2)}) collective-permute-start(bf16[4,64,16,128]{3,2,1,0:T(8,128)(2,1)S(1)} %get-tuple-element.27), channel_id=1, source_target_pairs={{0,32},{1,33},{2,34},{3,35},{4,36},{5,37},{6,38},{7,39},{8,40},{9,... | collective-permute-start | bytes 3145736 | tf_op jit(solution)/shard_map/ppermute | solution.py:30
  6.3 9.5 %collective-permute-start.6 = (bf16[4,4,4,2,16,128]{5,4,3,2,1,0:T(8,128)(2,1)S(1)}, bf16[4,4,4,2,16,128]{5,4,3,2,1,0:T(8,128)(2,1)S(1)}, u32[]{:S(2)}, u32[]{:S(2)}) collective-permute-start(bf16[4,4,4,2,16,128]{5,4,3,2,1,0:T(8,128)(2,1)S(1)} %get-tuple-element.30), channel_id=1, source_target_pairs={{0,1},{1,0},{2,3},{3,2},{4,5},{5,4},{6,7},{7,6},{8,9},{9,8},{10,11... | collective-permute-start | bytes 1572872 | tf_op jit(solution)/shard_map/ppermute | solution.py:30
  8.3 11.8 %collective-permute-start.3 = (bf16[4,4,2,4,16,128]{5,4,3,2,1,0:T(8,128)(2,1)S(1)}, bf16[4,4,2,4,16,128]{5,4,3,2,1,0:T(8,128)(2,1)S(1)}, u32[]{:S(2)}, u32[]{:S(2)}) collective-permute-start(bf16[4,4,2,4,16,128]{5,4,3,2,1,0:T(8,128)(2,1)S(1)} %get-tuple-element.29), channel_id=1, source_target_pairs={{0,16},{1,17},{2,18},{3,19},{4,20},{5,21},{6,22},{7,23},{8,24},{9,... | collective-permute-start | bytes 1572872 | tf_op jit(solution)/shard_map/ppermute | solution.py:30
  12.0 12.7 %collective-permute-start.4 = (bf16[4,4,2,4,16,128]{5,4,3,2,1,0:T(8,128)(2,1)S(1)}, bf16[4,4,2,4,16,128]{5,4,3,2,1,0:T(8,128)(2,1)S(1)}, u32[]{:S(2)}, u32[]{:S(2)}) collective-permute-start(bf16[4,4,2,4,16,128]{5,4,3,2,1,0:T(8,128)(2,1)S(1)} %get-tuple-element.32), channel_id=1, source_target_pairs={{0,8},{1,9},{2,10},{3,11},{4,12},{5,13},{6,14},{7,15},{8,16},{9,17... | collective-permute-start | bytes 1572872 | tf_op jit(solution)/shard_map/ppermute | solution.py:30
  12.1 12.6 %collective-permute-start.5 = (bf16[4,4,2,4,16,128]{5,4,3,2,1,0:T(8,128)(2,1)S(1)}, bf16[4,4,2,4,16,128]{5,4,3,2,1,0:T(8,128)(2,1)S(1)}, u32[]{:S(2)}, u32[]{:S(2)}) collective-permute-start(bf16[4,4,2,4,16,128]{5,4,3,2,1,0:T(8,128)(2,1)S(1)} %get-tuple-element.33), channel_id=1, source_target_pairs={{0,24},{1,25},{2,26},{3,27},{4,28},{5,29},{6,30},{7,31},{8,0},{9,1... | collective-permute-start | bytes 1572872 | tf_op jit(solution)/shard_map/ppermute | solution.py:30
  15.9 10.3 %collective-permute-start.7 = (bf16[4,4,2,16,128]{4,3,2,1,0:T(8,128)(2,1)S(1)}, bf16[4,4,2,16,128]{4,3,2,1,0:T(8,128)(2,1)S(1)}, u32[]{:S(2)}, u32[]{:S(2)}) collective-permute-start(bf16[4,4,2,16,128]{4,3,2,1,0:T(8,128)(2,1)S(1)} %get-tuple-element.38), channel_id=1, source_target_pairs={{0,16},{1,17},{2,18},{3,19},{4,20},{5,21},{6,22},{7,23},{8,24},{9,... | collective-permute-start | bytes 393224 | tf_op jit(solution)/shard_map/ppermute | solution.py:30
  17.9 9.6 %collective-permute-start.8 = (bf16[4,4,2,16,128]{4,3,2,1,0:T(8,128)(2,1)S(1)}, bf16[4,4,2,16,128]{4,3,2,1,0:T(8,128)(2,1)S(1)}, u32[]{:S(2)}, u32[]{:S(2)}) collective-permute-start(bf16[4,4,2,16,128]{4,3,2,1,0:T(8,128)(2,1)S(1)} %get-tuple-element.39), channel_id=1, source_target_pairs={{0,8},{1,9},{2,10},{3,11},{4,12},{5,13},{6,14},{7,15},{8,16},{9,17... | collective-permute-start | bytes 393224 | tf_op jit(solution)/shard_map/ppermute | solution.py:30
  20.1 7.4 %collective-permute-start.9 = (bf16[4,4,2,16,128]{4,3,2,1,0:T(8,128)(2,1)S(1)}, bf16[4,4,2,16,128]{4,3,2,1,0:T(8,128)(2,1)S(1)}, u32[]{:S(2)}, u32[]{:S(2)}) collective-permute-start(bf16[4,4,2,16,128]{4,3,2,1,0:T(8,128)(2,1)S(1)} %get-tuple-element.40), channel_id=1, source_target_pairs={{0,24},{1,25},{2,26},{3,27},{4,28},{5,29},{6,30},{7,31},{8,0},{9,1... | collective-permute-start | bytes 393224 | tf_op jit(solution)/shard_map/ppermute | solution.py:30
  27.6 6.9 %collective-permute-start.10 = (bf16[4,2,5,16,128]{4,3,2,1,0:T(8,128)(2,1)S(1)}, bf16[4,2,5,16,128]{4,3,2,1,0:T(8,128)(2,1)S(1)}, u32[]{:S(2)}, u32[]{:S(2)}) collective-permute-start(bf16[4,2,5,16,128]{4,3,2,1,0:T(8,128)(2,1)S(1)} %get-tuple-element.42), channel_id=1, source_target_pairs={{0,4},{1,5},{2,6},{3,7},{4,0},{5,1},{6,2},{7,3},{8,12},{9,13},{10,... | collective-permute-start | bytes 491528 | tf_op jit(solution)/shard_map/ppermute | solution.py:30
  30.9 6.5 %collective-permute-start.11 = (bf16[4,2,5,16,128]{4,3,2,1,0:T(8,128)(2,1)S(1)}, bf16[4,2,5,16,128]{4,3,2,1,0:T(8,128)(2,1)S(1)}, u32[]{:S(2)}, u32[]{:S(2)}) collective-permute-start(bf16[4,2,5,16,128]{4,3,2,1,0:T(8,128)(2,1)S(1)} %get-tuple-element.43), channel_id=1, source_target_pairs={{0,2},{1,3},{2,4},{3,5},{4,6},{5,7},{6,0},{7,1},{8,10},{9,11},{10,... | collective-permute-start | bytes 491528 | tf_op jit(solution)/shard_map/ppermute | solution.py:30
  31.6 5.9 %collective-permute-start.12 = (bf16[4,2,5,16,128]{4,3,2,1,0:T(8,128)(2,1)S(1)}, bf16[4,2,5,16,128]{4,3,2,1,0:T(8,128)(2,1)S(1)}, u32[]{:S(2)}, u32[]{:S(2)}) collective-permute-start(bf16[4,2,5,16,128]{4,3,2,1,0:T(8,128)(2,1)S(1)} %get-tuple-element.44), channel_id=1, source_target_pairs={{0,6},{1,7},{2,0},{3,1},{4,2},{5,3},{6,4},{7,5},{8,14},{9,15},{10,... | collective-permute-start | bytes 491528 | tf_op jit(solution)/shard_map/ppermute | solution.py:30

commit v6 on v5

--- a/solution.py
+++ b/solution.py
@@ -94,20 +94,24 @@
     return copy
 
 
-def fetch_all(grads, steps, half, first, zl, helds, sems):
+def fetch_all(grads, steps, half, first, zl, helds, sems, skip=0):
     copies = []
     for k, what in enumerate(steps):
         at = first if what in (SENT, KEPT) else lax.rem(first + what, RING)
         for zh in range(ZH):
-            copies.append(fetch(grads, what, half, at, zl, zh, helds[k].at[zh], sems.at[k, zh]))
+            copies.append(fetch(grads, what, half, at, zl, zh, helds[k].at[zh], sems.at[skip + k, zh]))
     return copies
 
 
-def cast_kernel(groups, grads, *refs):
-    outs, helds, sems = refs[: len(groups)], refs[len(groups) : -1], refs[-1]
-    core, _, second, zl = place()
+def cast_kernel(groups, kept, grads, *refs):
+    outs, refs = refs[: len(groups)], refs[len(groups) :]
+    keeps, helds, sems = refs[: len(kept)], refs[len(kept) : -1], refs[-1]
+    core, first, second, zl = place()
     steps = [what for group in groups for what in group]
-    copies = iter(fetch_all(grads, steps, 1 - core, second, zl, helds, sems))
+    copies = iter(
+        fetch_all(grads, steps, 1 - core, second, zl, helds, sems)
+        + fetch_all(grads, kept, core, first, zl, keeps, sems, len(steps))
+    )
     helds = iter(helds)
     for group, out in zip(groups, outs):
         begin = 0
@@ -117,6 +121,18 @@
                 next(copies).wait()
                 out[zh, begin:end] = held[zh].reshape(end - begin, *held.shape[-2:]).astype(out.dtype)
             begin = end
+    for copy in copies:
+        copy.wait()
+
+
+def add_kept_kernel(group, received, *refs):
+    keeps, outs = refs[: len(group)], refs[len(group) :]
+    begin = 0
+    for what, kept, out in zip(group, keeps, outs):
+        end = begin + slabs_of(what)
+        for zh in range(ZH):
+            out[zh] = (kept[zh] + received[zh, begin:end].reshape(kept.shape[1:]).astype(F32)).astype(out.dtype)
+        begin = end
 
 
 def add_kernel(group, grads, received, *refs):
@@ -142,7 +158,7 @@
     return pltpu.with_memory_space_constraint(values, pltpu.VMEM)
 
 
-def run_on_grads(kernel, grads, steps, out_shape, received=()):
+def run_on_grads(kernel, grads, steps, out_shape, received=(), kept=()):
     rows = grads.shape[-2]
     return pl.pallas_call(
         kernel,
@@ -150,23 +166,37 @@
         in_specs=[pl.BlockSpec(memory_space=pltpu.HBM)] + [VMEM] * len(received),
         out_specs=[VMEM] * len(out_shape),
         scratch_shapes=[pltpu.VMEM(shape_of(what, rows), F32) for what in steps]
-        + [pltpu.SemaphoreType.DMA((len(steps), ZH))],
+        + [pltpu.SemaphoreType.DMA((len(steps) + len(kept), ZH))],
         compiler_params=PARAMS,
         cost_estimate=COST,
     )(pltpu.with_memory_space_constraint(grads, pltpu.HBM), *received)
 
 
-def run_cast(grads, groups):
+def run_cast(grads, groups, kept):
     rows = grads.shape[-2]
     out_shape = [pltpu.VMEM((ZH, sum(map(slabs_of, group)), rows, QB), BF16) for group in groups]
+    out_shape += [pltpu.VMEM(shape_of(what, rows), F32) for what in kept]
     steps = [what for group in groups for what in group]
-    return run_on_grads(functools.partial(cast_kernel, groups), grads, steps, out_shape)
+    return run_on_grads(functools.partial(cast_kernel, groups, kept), grads, steps, out_shape, kept=kept)
+
+
+def add_shape(group, rows):
+    return [pltpu.VMEM(shape_of(what, rows), F32 if what in (0, KEPT) else BF16) for what in group]
 
 
 def run_add(grads, group, received):
-    rows = grads.shape[-2]
-    out_shape = [pltpu.VMEM(shape_of(what, rows), F32 if what in (0, KEPT) else BF16) for what in group]
-    return run_on_grads(functools.partial(add_kernel, group), grads, group, out_shape, [received])
+    return run_on_grads(functools.partial(add_kernel, group), grads, group, add_shape(group, grads.shape[-2]), [received])
+
+
+def run_add_kept(group, received, keeps):
+    return pl.pallas_call(
+        functools.partial(add_kept_kernel, group),
+        out_shape=add_shape(group, received.shape[-2]),
+        in_specs=[VMEM] * (1 + len(keeps)),
+        out_specs=[VMEM] * len(group),
+        compiler_params=PARAMS,
+        cost_estimate=COST,
+    )(received, *keeps)
 
 
 def paired_kernel(kept, arrived, *outs):
@@ -233,16 +263,17 @@
     rows = grads.shape[1] // (ZH * CORE * X * Y * ZL * SLABS * QB)
     grads = grads.reshape(ZH, CORE, X, Y, ZL, SLABS, rows, QB)
     groups = ((2, SENT), (1, 3), (0, KEPT))
-    crossed = []
-    for some in (groups[:1], groups[1:]):
-        outs = run_cast(grads, some)
-        grads = lax.optimization_barrier((grads, *outs))[0]
-        crossed += [to_other_core(out) for out in outs]
+    outs = run_cast(grads, groups[:1], ())
+    grads = lax.optimization_barrier((grads, *outs))[0]
+    crossed = [to_other_core(out) for out in outs]
+    outs = run_cast(grads, groups[1:], groups[0])
+    grads = lax.optimization_barrier((grads, *outs))[0]
+    crossed += [to_other_core(out) for out in outs[:2]]
     arrived, own = {}, {}
     for group, received in zip(groups, crossed):
-        outs = run_add(grads, group, received)
-        grads = lax.optimization_barrier((grads, *outs))[0]
-        for what, out in zip(group, outs):
+        summed = run_add(grads, group, received) if group != groups[0] else run_add_kept(group, received, outs[2:])
+        grads = lax.optimization_barrier((grads, *summed))[0]
+        for what, out in zip(group, summed):
             if what == SENT:
                 arrived[what] = to_z_partner(out)
             elif what in (0, KEPT):

time: 55.5 us -> 54.7 us (0.986)
  Pallas kernels: 9.17 us -> 8.44 us
    pallas_call x5 -> x4, Pallas kernels: 8.73 us -> 7.83 us  [run_on_grads(): pl.pallas_call(kernel, out_shape=out_shape, in_specs=[pl.BlockSpec(memory...]
  transfers between devices with their start and end apart: 13 -> 13, of which waited for: 5 -> 5; matrix products, arithmetic and copies ran while one was open for 0% -> 0% of each run, Pallas kernels for 14% -> 12%
where the time goes in v6:
time: 54.7 us; the launch traced here: 54.3 us
  starting transfers between devices  17.7 us (32%)
  blocking collectives  16.8 us (31%)
  waiting for transfers between devices  10.5 us (19%)
  Pallas kernels  8.44 us (15%)
  other arithmetic  0.77 us (1%)
    ppermute x13, starting transfers between devices, permuted(): return lax.ppermute(values, AXES, pairs)  17.7 us
    all_to_all x1, blocking collectives, on_device(): lax.all_to_all(pieces, AXES, 0, 0, axis_index_groups=z_groups(), tiled=True)  16.8 us
    ppermute x13, waiting for transfers between devices, permuted(): return lax.ppermute(values, AXES, pairs)  10.5 us
    pallas_call x4, Pallas kernels, run_on_grads(): pl.pallas_call(kernel, out_shape=out_shape, in_specs=[pl.BlockSpec(memory...  7.83 us
  transfers between devices with their start and end apart: 13, of which 5 were waited for; matrix products, arithmetic and copies ran while one was open for 0% of the time, Pallas kernels for 12%

profile of v6, /device:TPU:2, one launch (start us, length us, event | category | flops | bytes accessed | tf_op | source)
XLA Modules:
  0.0 54.3 jit_solution(6598527311349716603)
XLA Ops:
  0.0 1.6 %shard_map.17 = bf16[4,64,16,128]{3,2,1,0:T(8,128)(2,1)S(1)} custom-call(f32[4,2,4,4,2,6,16,128]{7,6,5,4,3,2,1,0:T(8,128)} %bitcast.6), custom_call_target="tpu_custom_call" | custom-call | tf_op jit(solution)/shard_map/pallas_call | solution.py:163
  1.7 3.0 %shard_map.18 = (bf16[4,64,16,128]{3,2,1,0:T(8,128)(2,1)S(1)}, bf16[4,64,16,128]{3,2,1,0:T(8,128)(2,1)S(1)}, f32[4,4,2,4,16,128]{5,4,3,2,1,0:T(8,128)S(1)}, f32[4,4,4,2,16,128]{5,4,3,2,1,0:T(8,128)S(1)}) custom-call(f32[4,2,4,4,2,6,16,128]{7,6,5,4,3,2,1,0:T(8,128)} %bitcast.7), custom_call_target="tpu_custom_call" | custom-call | tf_op jit(solution)/shard_map/pallas_call | solution.py:163
  4.8 0.5 collective-permute-start.1
  5.4 0.2 shard_map.19
  5.6 2.0 %collective-permute-start.6 = (bf16[4,4,4,2,16,128]{5,4,3,2,1,0:T(8,128)(2,1)S(1)}, bf16[4,4,4,2,16,128]{5,4,3,2,1,0:T(8,128)(2,1)S(1)}, u32[]{:S(2)}, u32[]{:S(2)}) collective-permute-start(bf16[4,4,4,2,16,128]{5,4,3,2,1,0:T(8,128)(2,1)S(1)} %get-tuple-element.34), channel_id=1, source_target_pairs={{0,1},{1,0},{2,3},{3,2},{4,5},{5,4},{6,7},{7,6},{8,9},{9,8},{10,11... | collective-permute-start | bytes 1572872 | tf_op jit(solution)/shard_map/ppermute | solution.py:30
  7.6 2.1 %collective-permute-start.3 = (bf16[4,4,2,4,16,128]{5,4,3,2,1,0:T(8,128)(2,1)S(1)}, bf16[4,4,2,4,16,128]{5,4,3,2,1,0:T(8,128)(2,1)S(1)}, u32[]{:S(2)}, u32[]{:S(2)}) collective-permute-start(bf16[4,4,2,4,16,128]{5,4,3,2,1,0:T(8,128)(2,1)S(1)} %get-tuple-element.33), channel_id=1, source_target_pairs={{0,16},{1,17},{2,18},{3,19},{4,20},{5,21},{6,22},{7,23},{8,24},{9,... | collective-permute-start | bytes 1572872 | tf_op jit(solution)/shard_map/ppermute | solution.py:30
  9.7 1.6 %shard_map.20 = (bf16[4,4,2,4,16,128]{5,4,3,2,1,0:T(8,128)(2,1)S(1)}, bf16[4,4,2,4,16,128]{5,4,3,2,1,0:T(8,128)(2,1)S(1)}) custom-call(f32[4,2,4,4,2,6,16,128]{7,6,5,4,3,2,1,0:T(8,128)} %bitcast.8, bf16[4,64,16,128]{3,2,1,0:T(8,128)(2,1)S(1)} %collective-permute-done.1.received), custom_call_target="tpu_custom_call" | custom-call | tf_op jit(solution)/shard_map/pallas_call | solution.py:163
  11.4 2.0 %collective-permute-start.5 = (bf16[4,4,2,4,16,128]{5,4,3,2,1,0:T(8,128)(2,1)S(1)}, bf16[4,4,2,4,16,128]{5,4,3,2,1,0:T(8,128)(2,1)S(1)}, u32[]{:S(2)}, u32[]{:S(2)}) collective-permute-start(bf16[4,4,2,4,16,128]{5,4,3,2,1,0:T(8,128)(2,1)S(1)} %get-tuple-element.37), channel_id=1, source_target_pairs={{0,24},{1,25},{2,26},{3,27},{4,28},{5,29},{6,30},{7,31},{8,0},{9,1... | collective-permute-start | bytes 1572872 | tf_op jit(solution)/shard_map/ppermute | solution.py:30
  13.4 1.6 %shard_map.21 = (f32[4,4,2,4,16,128]{5,4,3,2,1,0:T(8,128)S(1)}, f32[4,4,4,2,16,128]{5,4,3,2,1,0:T(8,128)S(1)}) custom-call(f32[4,2,4,4,2,6,16,128]{7,6,5,4,3,2,1,0:T(8,128)} %bitcast.9, bf16[4,64,16,128]{3,2,1,0:T(8,128)(2,1)S(1)} %collective-permute-done.2.received), custom_call_target="tpu_custom_call" | custom-call | tf_op jit(solution)/shard_map/pallas_call | solution.py:163
  15.0 0.1 shard_map.23
  15.2 2.0 %collective-permute-start.7 = (bf16[4,4,2,16,128]{4,3,2,1,0:T(8,128)(2,1)S(1)}, bf16[4,4,2,16,128]{4,3,2,1,0:T(8,128)(2,1)S(1)}, u32[]{:S(2)}, u32[]{:S(2)}) collective-permute-start(bf16[4,4,2,16,128]{4,3,2,1,0:T(8,128)(2,1)S(1)} %get-tuple-element.42), channel_id=1, source_target_pairs={{0,16},{1,17},{2,18},{3,19},{4,20},{5,21},{6,22},{7,23},{8,24},{9,... | collective-permute-start | bytes 393224 | tf_op jit(solution)/shard_map/ppermute | solution.py:30
  17.1 2.2 %collective-permute-start.8 = (bf16[4,4,2,16,128]{4,3,2,1,0:T(8,128)(2,1)S(1)}, bf16[4,4,2,16,128]{4,3,2,1,0:T(8,128)(2,1)S(1)}, u32[]{:S(2)}, u32[]{:S(2)}) collective-permute-start(bf16[4,4,2,16,128]{4,3,2,1,0:T(8,128)(2,1)S(1)} %get-tuple-element.43), channel_id=1, source_target_pairs={{0,8},{1,9},{2,10},{3,11},{4,12},{5,13},{6,14},{7,15},{8,16},{9,17... | collective-permute-start | bytes 393224 | tf_op jit(solution)/shard_map/ppermute | solution.py:30
  19.4 4.6 %collective-permute-done.4.p2 = bf16[4,4,2,4,16,128]{5,4,3,2,1,0:T(8,128)(2,1)S(1)} collective-permute-done((bf16[4,4,2,4,16,128]{5,4,3,2,1,0:T(8,128)(2,1)S(1)}, bf16[4,4,2,4,16,128]{5,4,3,2,1,0:T(8,128)(2,1)S(1)}, u32[]{:S(2)}, u32[]{:S(2)}) %collective-permute-start.4) | collective-permute-done | bytes 524320 | tf_op jit(solution)/shard_map/ppermute | solution.py:30
  23.9 0.2 shard_map.22.plain
  24.2 1.3 %collective-permute-done.7.p1 = bf16[4,4,2,16,128]{4,3,2,1,0:T(8,128)(2,1)S(1)} collective-permute-done((bf16[4,4,2,16,128]{4,3,2,1,0:T(8,128)(2,1)S(1)}, bf16[4,4,2,16,128]{4,3,2,1,0:T(8,128)(2,1)S(1)}, u32[]{:S(2)}, u32[]{:S(2)}) %collective-permute-start.7) | collective-permute-done | bytes 131104 | tf_op jit(solution)/shard_map/ppermute | solution.py:30
  25.4 1.4 %collective-permute-done.8.p2 = bf16[4,4,2,16,128]{4,3,2,1,0:T(8,128)(2,1)S(1)} collective-permute-done((bf16[4,4,2,16,128]{4,3,2,1,0:T(8,128)(2,1)S(1)}, bf16[4,4,2,16,128]{4,3,2,1,0:T(8,128)(2,1)S(1)}, u32[]{:S(2)}, u32[]{:S(2)}) %collective-permute-start.8) | collective-permute-done | bytes 131104 | tf_op jit(solution)/shard_map/ppermute | solution.py:30
  26.8 0.1 shard_map.24
  26.9 3.3 %collective-permute-start.10 = (bf16[4,2,5,16,128]{4,3,2,1,0:T(8,128)(2,1)S(1)}, bf16[4,2,5,16,128]{4,3,2,1,0:T(8,128)(2,1)S(1)}, u32[]{:S(2)}, u32[]{:S(2)}) collective-permute-start(bf16[4,2,5,16,128]{4,3,2,1,0:T(8,128)(2,1)S(1)} %get-tuple-element.46), channel_id=1, source_target_pairs={{0,4},{1,5},{2,6},{3,7},{4,0},{5,1},{6,2},{7,3},{8,12},{9,13},{10,... | collective-permute-start | bytes 491528 | tf_op jit(solution)/shard_map/ppermute | solution.py:30
  30.2 0.7 %collective-permute-start.11 = (bf16[4,2,5,16,128]{4,3,2,1,0:T(8,128)(2,1)S(1)}, bf16[4,2,5,16,128]{4,3,2,1,0:T(8,128)(2,1)S(1)}, u32[]{:S(2)}, u32[]{:S(2)}) collective-permute-start(bf16[4,2,5,16,128]{4,3,2,1,0:T(8,128)(2,1)S(1)} %get-tuple-element.47), channel_id=1, source_target_pairs={{0,2},{1,3},{2,4},{3,5},{4,6},{5,7},{6,0},{7,1},{8,10},{9,11},{10,... | collective-permute-start | bytes 491528 | tf_op jit(solution)/shard_map/ppermute | solution.py:30
  30.9 2.6 %collective-permute-start.12 = (bf16[4,2,5,16,128]{4,3,2,1,0:T(8,128)(2,1)S(1)}, bf16[4,2,5,16,128]{4,3,2,1,0:T(8,128)(2,1)S(1)}, u32[]{:S(2)}, u32[]{:S(2)}) collective-permute-start(bf16[4,2,5,16,128]{4,3,2,1,0:T(8,128)(2,1)S(1)} %get-tuple-element.48), channel_id=1, source_target_pairs={{0,6},{1,7},{2,0},{3,1},{4,2},{5,3},{6,4},{7,5},{8,14},{9,15},{10,... | collective-permute-start | bytes 491528 | tf_op jit(solution)/shard_map/ppermute | solution.py:30
  33.4 0.4 collective-permute-done.10
  33.8 2.9 %collective-permute-done.11 = bf16[4,2,5,16,128]{4,3,2,1,0:T(8,128)(2,1)S(1)} collective-permute-done((bf16[4,2,5,16,128]{4,3,2,1,0:T(8,128)(2,1)S(1)}, bf16[4,2,5,16,128]{4,3,2,1,0:T(8,128)(2,1)S(1)}, u32[]{:S(2)}, u32[]{:S(2)}) %collective-permute-start.11) | collective-permute-done | bytes 163872 | tf_op jit(solution)/shard_map/ppermute | solution.py:30
  36.8 16.8 %all_to_all.5 = bf16[8,5,16,128]{3,2,1,0:T(8,128)(2,1)S(1)} all-to-all(bf16[8,5,16,128]{3,2,1,0:T(8,128)(2,1)S(1)} %bitcast.10), channel_id=1, replica_groups={{0,1,64,65,128,129,192,193},{2,3,66,67,130,131,194,195},{4,5,68,69,132,..., dimensions={0} | all-to-all | bytes 327680 | tf_op jit(solution)/shard_map/all_to_all | solution.py:292
  53.7 0.6 %pad_maximum_fusion = f32[6,16,128]{2,1,0:T(8,128)} fusion(f32[2,16,128]{2,1,0:T(8,128)S(1)} %bitcast_reduce_fusion, f32[4,16,128]{2,1,0:T(8,128)S(1)} %slice_reduce_fusion), kind=kLoop, calls=%fused_computation.3 | loop fusion | flops 12288 | bytes 98304 | tf_op jit(solution)/shard_map/concatenate | solution.py:295
  (17 shorter events, 0.5 us)
Async XLA Ops:
  1.6 3.8 %collective-permute-start = (bf16[4,64,16,128]{3,2,1,0:T(8,128)(2,1)S(1)}, bf16[4,64,16,128]{3,2,1,0:T(8,128)(2,1)S(1)}, u32[]{:S(2)}, u32[]{:S(2)}) collective-permute-start(bf16[4,64,16,128]{3,2,1,0:T(8,128)(2,1)S(1)} %shard_map.17), channel_id=1, source_target_pairs={{0,32},{1,33},{2,34},{3,35},{4,36},{5,37},{6,38},{7,39},{8,40},{9,... | collective-permute-start | bytes 3145736 | tf_op jit(solution)/shard_map/ppermute | solution.py:30
  4.8 4.9 %collective-permute-start.1 = (bf16[4,64,16,128]{3,2,1,0:T(8,128)(2,1)S(1)}, bf16[4,64,16,128]{3,2,1,0:T(8,128)(2,1)S(1)}, u32[]{:S(2)}, u32[]{:S(2)}) collective-permute-start(bf16[4,64,16,128]{3,2,1,0:T(8,128)(2,1)S(1)} %get-tuple-element.28), channel_id=1, source_target_pairs={{0,32},{1,33},{2,34},{3,35},{4,36},{5,37},{6,38},{7,39},{8,40},{9,... | collective-permute-start | bytes 3145736 | tf_op jit(solution)/shard_map/ppermute | solution.py:30
  5.3 8.1 %collective-permute-start.2 = (bf16[4,64,16,128]{3,2,1,0:T(8,128)(2,1)S(1)}, bf16[4,64,16,128]{3,2,1,0:T(8,128)(2,1)S(1)}, u32[]{:S(2)}, u32[]{:S(2)}) collective-permute-start(bf16[4,64,16,128]{3,2,1,0:T(8,128)(2,1)S(1)} %get-tuple-element.29), channel_id=1, source_target_pairs={{0,32},{1,33},{2,34},{3,35},{4,36},{5,37},{6,38},{7,39},{8,40},{9,... | collective-permute-start | bytes 3145736 | tf_op jit(solution)/shard_map/ppermute | solution.py:30
  5.6 9.5 %collective-permute-start.6 = (bf16[4,4,4,2,16,128]{5,4,3,2,1,0:T(8,128)(2,1)S(1)}, bf16[4,4,4,2,16,128]{5,4,3,2,1,0:T(8,128)(2,1)S(1)}, u32[]{:S(2)}, u32[]{:S(2)}) collective-permute-start(bf16[4,4,4,2,16,128]{5,4,3,2,1,0:T(8,128)(2,1)S(1)} %get-tuple-element.34), channel_id=1, source_target_pairs={{0,1},{1,0},{2,3},{3,2},{4,5},{5,4},{6,7},{7,6},{8,9},{9,8},{10,11... | collective-permute-start | bytes 1572872 | tf_op jit(solution)/shard_map/ppermute | solution.py:30
  7.6 11.8 %collective-permute-start.3 = (bf16[4,4,2,4,16,128]{5,4,3,2,1,0:T(8,128)(2,1)S(1)}, bf16[4,4,2,4,16,128]{5,4,3,2,1,0:T(8,128)(2,1)S(1)}, u32[]{:S(2)}, u32[]{:S(2)}) collective-permute-start(bf16[4,4,2,4,16,128]{5,4,3,2,1,0:T(8,128)(2,1)S(1)} %get-tuple-element.33), channel_id=1, source_target_pairs={{0,16},{1,17},{2,18},{3,19},{4,20},{5,21},{6,22},{7,23},{8,24},{9,... | collective-permute-start | bytes 1572872 | tf_op jit(solution)/shard_map/ppermute | solution.py:30
  11.3 12.6 %collective-permute-start.4 = (bf16[4,4,2,4,16,128]{5,4,3,2,1,0:T(8,128)(2,1)S(1)}, bf16[4,4,2,4,16,128]{5,4,3,2,1,0:T(8,128)(2,1)S(1)}, u32[]{:S(2)}, u32[]{:S(2)}) collective-permute-start(bf16[4,4,2,4,16,128]{5,4,3,2,1,0:T(8,128)(2,1)S(1)} %get-tuple-element.36), channel_id=1, source_target_pairs={{0,8},{1,9},{2,10},{3,11},{4,12},{5,13},{6,14},{7,15},{8,16},{9,17... | collective-permute-start | bytes 1572872 | tf_op jit(solution)/shard_map/ppermute | solution.py:30
  11.4 12.6 %collective-permute-start.5 = (bf16[4,4,2,4,16,128]{5,4,3,2,1,0:T(8,128)(2,1)S(1)}, bf16[4,4,2,4,16,128]{5,4,3,2,1,0:T(8,128)(2,1)S(1)}, u32[]{:S(2)}, u32[]{:S(2)}) collective-permute-start(bf16[4,4,2,4,16,128]{5,4,3,2,1,0:T(8,128)(2,1)S(1)} %get-tuple-element.37), channel_id=1, source_target_pairs={{0,24},{1,25},{2,26},{3,27},{4,28},{5,29},{6,30},{7,31},{8,0},{9,1... | collective-permute-start | bytes 1572872 | tf_op jit(solution)/shard_map/ppermute | solution.py:30
  15.2 10.3 %collective-permute-start.7 = (bf16[4,4,2,16,128]{4,3,2,1,0:T(8,128)(2,1)S(1)}, bf16[4,4,2,16,128]{4,3,2,1,0:T(8,128)(2,1)S(1)}, u32[]{:S(2)}, u32[]{:S(2)}) collective-permute-start(bf16[4,4,2,16,128]{4,3,2,1,0:T(8,128)(2,1)S(1)} %get-tuple-element.42), channel_id=1, source_target_pairs={{0,16},{1,17},{2,18},{3,19},{4,20},{5,21},{6,22},{7,23},{8,24},{9,... | collective-permute-start | bytes 393224 | tf_op jit(solution)/shard_map/ppermute | solution.py:30
  17.1 9.6 %collective-permute-start.8 = (bf16[4,4,2,16,128]{4,3,2,1,0:T(8,128)(2,1)S(1)}, bf16[4,4,2,16,128]{4,3,2,1,0:T(8,128)(2,1)S(1)}, u32[]{:S(2)}, u32[]{:S(2)}) collective-permute-start(bf16[4,4,2,16,128]{4,3,2,1,0:T(8,128)(2,1)S(1)} %get-tuple-element.43), channel_id=1, source_target_pairs={{0,8},{1,9},{2,10},{3,11},{4,12},{5,13},{6,14},{7,15},{8,16},{9,17... | collective-permute-start | bytes 393224 | tf_op jit(solution)/shard_map/ppermute | solution.py:30
  19.3 7.4 %collective-permute-start.9 = (bf16[4,4,2,16,128]{4,3,2,1,0:T(8,128)(2,1)S(1)}, bf16[4,4,2,16,128]{4,3,2,1,0:T(8,128)(2,1)S(1)}, u32[]{:S(2)}, u32[]{:S(2)}) collective-permute-start(bf16[4,4,2,16,128]{4,3,2,1,0:T(8,128)(2,1)S(1)} %get-tuple-element.44), channel_id=1, source_target_pairs={{0,24},{1,25},{2,26},{3,27},{4,28},{5,29},{6,30},{7,31},{8,0},{9,1... | collective-permute-start | bytes 393224 | tf_op jit(solution)/shard_map/ppermute | solution.py:30
  26.9 6.9 %collective-permute-start.10 = (bf16[4,2,5,16,128]{4,3,2,1,0:T(8,128)(2,1)S(1)}, bf16[4,2,5,16,128]{4,3,2,1,0:T(8,128)(2,1)S(1)}, u32[]{:S(2)}, u32[]{:S(2)}) collective-permute-start(bf16[4,2,5,16,128]{4,3,2,1,0:T(8,128)(2,1)S(1)} %get-tuple-element.46), channel_id=1, source_target_pairs={{0,4},{1,5},{2,6},{3,7},{4,0},{5,1},{6,2},{7,3},{8,12},{9,13},{10,... | collective-permute-start | bytes 491528 | tf_op jit(solution)/shard_map/ppermute | solution.py:30
  30.2 6.5 %collective-permute-start.11 = (bf16[4,2,5,16,128]{4,3,2,1,0:T(8,128)(2,1)S(1)}, bf16[4,2,5,16,128]{4,3,2,1,0:T(8,128)(2,1)S(1)}, u32[]{:S(2)}, u32[]{:S(2)}) collective-permute-start(bf16[4,2,5,16,128]{4,3,2,1,0:T(8,128)(2,1)S(1)} %get-tuple-element.47), channel_id=1, source_target_pairs={{0,2},{1,3},{2,4},{3,5},{4,6},{5,7},{6,0},{7,1},{8,10},{9,11},{10,... | collective-permute-start | bytes 491528 | tf_op jit(solution)/shard_map/ppermute | solution.py:30
  30.9 5.9 %collective-permute-start.12 = (bf16[4,2,5,16,128]{4,3,2,1,0:T(8,128)(2,1)S(1)}, bf16[4,2,5,16,128]{4,3,2,1,0:T(8,128)(2,1)S(1)}, u32[]{:S(2)}, u32[]{:S(2)}) collective-permute-start(bf16[4,2,5,16,128]{4,3,2,1,0:T(8,128)(2,1)S(1)} %get-tuple-element.48), channel_id=1, source_target_pairs={{0,6},{1,7},{2,0},{3,1},{4,2},{5,3},{6,4},{7,5},{8,14},{9,15},{10,... | collective-permute-start | bytes 491528 | tf_op jit(solution)/shard_map/ppermute | solution.py:30

commit v7 on v6

--- a/solution.py
+++ b/solution.py
@@ -282,7 +282,7 @@
                 arrived[what] = along(out, what, True)
 
     paired = run_paired(own[KEPT], arrived[SENT])
-    paired_arrived = {shift: along(paired[shift], shift, True) for shift in (2, 1, 3)}
+    paired_arrived = {shift: along(paired[shift], shift, True) for shift in (1, 3, 2)}
     plain = run_plain(own[0], [arrived[shift] for shift in (2, 1, 3)])
     pieces = run_pieces(plain, paired[0], [paired_arrived[shift] for shift in (2, 1, 3)])
     summed = pieces[0]

time: 54.7 us -> 54.7 us (level)
  no operation moved by 1% of the time
where the time goes in v7:
time: 54.7 us; the launch traced here: 54.3 us
  starting transfers between devices  17.7 us (32%)
  blocking collectives  16.8 us (31%)
  waiting for transfers between devices  10.5 us (19%)
  Pallas kernels  8.44 us (15%)
  other arithmetic  0.77 us (1%)
    ppermute x13, starting transfers between devices, permuted(): return lax.ppermute(values, AXES, pairs)  17.7 us
    all_to_all x1, blocking collectives, on_device(): lax.all_to_all(pieces, AXES, 0, 0, axis_index_groups=z_groups(), tiled=True)  16.8 us
    ppermute x13, waiting for transfers between devices, permuted(): return lax.ppermute(values, AXES, pairs)  10.5 us
    pallas_call x4, Pallas kernels, run_on_grads(): pl.pallas_call(kernel, out_shape=out_shape, in_specs=[pl.BlockSpec(memory...  7.83 us
  transfers between devices with their start and end apart: 13, of which 5 were waited for; matrix products, arithmetic and copies ran while one was open for 0% of the time, Pallas kernels for 12%

profile of v7, /device:TPU:2, one launch (start us, length us, event | category | flops | bytes accessed | tf_op | source)
XLA Modules:
  0.0 54.3 jit_solution(6598527311349716603)
XLA Ops:
  0.0 1.6 %shard_map.17 = bf16[4,64,16,128]{3,2,1,0:T(8,128)(2,1)S(1)} custom-call(f32[4,2,4,4,2,6,16,128]{7,6,5,4,3,2,1,0:T(8,128)} %bitcast.6), custom_call_target="tpu_custom_call" | custom-call | tf_op jit(solution)/shard_map/pallas_call | solution.py:163
  1.7 3.0 %shard_map.18 = (bf16[4,64,16,128]{3,2,1,0:T(8,128)(2,1)S(1)}, bf16[4,64,16,128]{3,2,1,0:T(8,128)(2,1)S(1)}, f32[4,4,2,4,16,128]{5,4,3,2,1,0:T(8,128)S(1)}, f32[4,4,4,2,16,128]{5,4,3,2,1,0:T(8,128)S(1)}) custom-call(f32[4,2,4,4,2,6,16,128]{7,6,5,4,3,2,1,0:T(8,128)} %bitcast.7), custom_call_target="tpu_custom_call" | custom-call | tf_op jit(solution)/shard_map/pallas_call | solution.py:163
  4.8 0.5 collective-permute-start.1
  5.4 0.2 shard_map.19
  5.6 2.0 %collective-permute-start.6 = (bf16[4,4,4,2,16,128]{5,4,3,2,1,0:T(8,128)(2,1)S(1)}, bf16[4,4,4,2,16,128]{5,4,3,2,1,0:T(8,128)(2,1)S(1)}, u32[]{:S(2)}, u32[]{:S(2)}) collective-permute-start(bf16[4,4,4,2,16,128]{5,4,3,2,1,0:T(8,128)(2,1)S(1)} %get-tuple-element.34), channel_id=1, source_target_pairs={{0,1},{1,0},{2,3},{3,2},{4,5},{5,4},{6,7},{7,6},{8,9},{9,8},{10,11... | collective-permute-start | bytes 1572872 | tf_op jit(solution)/shard_map/ppermute | solution.py:30
  7.6 2.1 %collective-permute-start.3 = (bf16[4,4,2,4,16,128]{5,4,3,2,1,0:T(8,128)(2,1)S(1)}, bf16[4,4,2,4,16,128]{5,4,3,2,1,0:T(8,128)(2,1)S(1)}, u32[]{:S(2)}, u32[]{:S(2)}) collective-permute-start(bf16[4,4,2,4,16,128]{5,4,3,2,1,0:T(8,128)(2,1)S(1)} %get-tuple-element.33), channel_id=1, source_target_pairs={{0,16},{1,17},{2,18},{3,19},{4,20},{5,21},{6,22},{7,23},{8,24},{9,... | collective-permute-start | bytes 1572872 | tf_op jit(solution)/shard_map/ppermute | solution.py:30
  9.7 1.6 %shard_map.20 = (bf16[4,4,2,4,16,128]{5,4,3,2,1,0:T(8,128)(2,1)S(1)}, bf16[4,4,2,4,16,128]{5,4,3,2,1,0:T(8,128)(2,1)S(1)}) custom-call(f32[4,2,4,4,2,6,16,128]{7,6,5,4,3,2,1,0:T(8,128)} %bitcast.8, bf16[4,64,16,128]{3,2,1,0:T(8,128)(2,1)S(1)} %collective-permute-done.1.received), custom_call_target="tpu_custom_call" | custom-call | tf_op jit(solution)/shard_map/pallas_call | solution.py:163
  11.4 2.0 %collective-permute-start.5 = (bf16[4,4,2,4,16,128]{5,4,3,2,1,0:T(8,128)(2,1)S(1)}, bf16[4,4,2,4,16,128]{5,4,3,2,1,0:T(8,128)(2,1)S(1)}, u32[]{:S(2)}, u32[]{:S(2)}) collective-permute-start(bf16[4,4,2,4,16,128]{5,4,3,2,1,0:T(8,128)(2,1)S(1)} %get-tuple-element.37), channel_id=1, source_target_pairs={{0,24},{1,25},{2,26},{3,27},{4,28},{5,29},{6,30},{7,31},{8,0},{9,1... | collective-permute-start | bytes 1572872 | tf_op jit(solution)/shard_map/ppermute | solution.py:30
  13.4 1.6 %shard_map.21 = (f32[4,4,2,4,16,128]{5,4,3,2,1,0:T(8,128)S(1)}, f32[4,4,4,2,16,128]{5,4,3,2,1,0:T(8,128)S(1)}) custom-call(f32[4,2,4,4,2,6,16,128]{7,6,5,4,3,2,1,0:T(8,128)} %bitcast.9, bf16[4,64,16,128]{3,2,1,0:T(8,128)(2,1)S(1)} %collective-permute-done.2.received), custom_call_target="tpu_custom_call" | custom-call | tf_op jit(solution)/shard_map/pallas_call | solution.py:163
  15.0 0.1 shard_map.23
  15.2 2.0 %collective-permute-start.7 = (bf16[4,4,2,16,128]{4,3,2,1,0:T(8,128)(2,1)S(1)}, bf16[4,4,2,16,128]{4,3,2,1,0:T(8,128)(2,1)S(1)}, u32[]{:S(2)}, u32[]{:S(2)}) collective-permute-start(bf16[4,4,2,16,128]{4,3,2,1,0:T(8,128)(2,1)S(1)} %get-tuple-element.42), channel_id=1, source_target_pairs={{0,16},{1,17},{2,18},{3,19},{4,20},{5,21},{6,22},{7,23},{8,24},{9,... | collective-permute-start | bytes 393224 | tf_op jit(solution)/shard_map/ppermute | solution.py:30
  17.1 2.2 %collective-permute-start.8 = (bf16[4,4,2,16,128]{4,3,2,1,0:T(8,128)(2,1)S(1)}, bf16[4,4,2,16,128]{4,3,2,1,0:T(8,128)(2,1)S(1)}, u32[]{:S(2)}, u32[]{:S(2)}) collective-permute-start(bf16[4,4,2,16,128]{4,3,2,1,0:T(8,128)(2,1)S(1)} %get-tuple-element.43), channel_id=1, source_target_pairs={{0,8},{1,9},{2,10},{3,11},{4,12},{5,13},{6,14},{7,15},{8,16},{9,17... | collective-permute-start | bytes 393224 | tf_op jit(solution)/shard_map/ppermute | solution.py:30
  19.4 4.6 %collective-permute-done.4.p2 = bf16[4,4,2,4,16,128]{5,4,3,2,1,0:T(8,128)(2,1)S(1)} collective-permute-done((bf16[4,4,2,4,16,128]{5,4,3,2,1,0:T(8,128)(2,1)S(1)}, bf16[4,4,2,4,16,128]{5,4,3,2,1,0:T(8,128)(2,1)S(1)}, u32[]{:S(2)}, u32[]{:S(2)}) %collective-permute-start.4) | collective-permute-done | bytes 524320 | tf_op jit(solution)/shard_map/ppermute | solution.py:30
  23.9 0.2 shard_map.22.plain
  24.2 1.3 %collective-permute-done.7.p1 = bf16[4,4,2,16,128]{4,3,2,1,0:T(8,128)(2,1)S(1)} collective-permute-done((bf16[4,4,2,16,128]{4,3,2,1,0:T(8,128)(2,1)S(1)}, bf16[4,4,2,16,128]{4,3,2,1,0:T(8,128)(2,1)S(1)}, u32[]{:S(2)}, u32[]{:S(2)}) %collective-permute-start.7) | collective-permute-done | bytes 131104 | tf_op jit(solution)/shard_map/ppermute | solution.py:30
  25.4 1.4 %collective-permute-done.8.p2 = bf16[4,4,2,16,128]{4,3,2,1,0:T(8,128)(2,1)S(1)} collective-permute-done((bf16[4,4,2,16,128]{4,3,2,1,0:T(8,128)(2,1)S(1)}, bf16[4,4,2,16,128]{4,3,2,1,0:T(8,128)(2,1)S(1)}, u32[]{:S(2)}, u32[]{:S(2)}) %collective-permute-start.8) | collective-permute-done | bytes 131104 | tf_op jit(solution)/shard_map/ppermute | solution.py:30
  26.8 0.1 shard_map.24
  26.9 3.3 %collective-permute-start.10 = (bf16[4,2,5,16,128]{4,3,2,1,0:T(8,128)(2,1)S(1)}, bf16[4,2,5,16,128]{4,3,2,1,0:T(8,128)(2,1)S(1)}, u32[]{:S(2)}, u32[]{:S(2)}) collective-permute-start(bf16[4,2,5,16,128]{4,3,2,1,0:T(8,128)(2,1)S(1)} %get-tuple-element.46), channel_id=1, source_target_pairs={{0,4},{1,5},{2,6},{3,7},{4,0},{5,1},{6,2},{7,3},{8,12},{9,13},{10,... | collective-permute-start | bytes 491528 | tf_op jit(solution)/shard_map/ppermute | solution.py:30
  30.2 0.7 %collective-permute-start.11 = (bf16[4,2,5,16,128]{4,3,2,1,0:T(8,128)(2,1)S(1)}, bf16[4,2,5,16,128]{4,3,2,1,0:T(8,128)(2,1)S(1)}, u32[]{:S(2)}, u32[]{:S(2)}) collective-permute-start(bf16[4,2,5,16,128]{4,3,2,1,0:T(8,128)(2,1)S(1)} %get-tuple-element.47), channel_id=1, source_target_pairs={{0,2},{1,3},{2,4},{3,5},{4,6},{5,7},{6,0},{7,1},{8,10},{9,11},{10,... | collective-permute-start | bytes 491528 | tf_op jit(solution)/shard_map/ppermute | solution.py:30
  30.9 2.6 %collective-permute-start.12 = (bf16[4,2,5,16,128]{4,3,2,1,0:T(8,128)(2,1)S(1)}, bf16[4,2,5,16,128]{4,3,2,1,0:T(8,128)(2,1)S(1)}, u32[]{:S(2)}, u32[]{:S(2)}) collective-permute-start(bf16[4,2,5,16,128]{4,3,2,1,0:T(8,128)(2,1)S(1)} %get-tuple-element.48), channel_id=1, source_target_pairs={{0,6},{1,7},{2,0},{3,1},{4,2},{5,3},{6,4},{7,5},{8,14},{9,15},{10,... | collective-permute-start | bytes 491528 | tf_op jit(solution)/shard_map/ppermute | solution.py:30
  33.4 0.4 collective-permute-done.10
  33.8 2.9 %collective-permute-done.11 = bf16[4,2,5,16,128]{4,3,2,1,0:T(8,128)(2,1)S(1)} collective-permute-done((bf16[4,2,5,16,128]{4,3,2,1,0:T(8,128)(2,1)S(1)}, bf16[4,2,5,16,128]{4,3,2,1,0:T(8,128)(2,1)S(1)}, u32[]{:S(2)}, u32[]{:S(2)}) %collective-permute-start.11) | collective-permute-done | bytes 163872 | tf_op jit(solution)/shard_map/ppermute | solution.py:30
  36.8 16.8 %all_to_all.5 = bf16[8,5,16,128]{3,2,1,0:T(8,128)(2,1)S(1)} all-to-all(bf16[8,5,16,128]{3,2,1,0:T(8,128)(2,1)S(1)} %bitcast.10), channel_id=1, replica_groups={{0,1,64,65,128,129,192,193},{2,3,66,67,130,131,194,195},{4,5,68,69,132,..., dimensions={0} | all-to-all | bytes 327680 | tf_op jit(solution)/shard_map/all_to_all | solution.py:292
  53.7 0.6 %pad_maximum_fusion = f32[6,16,128]{2,1,0:T(8,128)} fusion(f32[2,16,128]{2,1,0:T(8,128)S(1)} %bitcast_reduce_fusion, f32[4,16,128]{2,1,0:T(8,128)S(1)} %slice_reduce_fusion), kind=kLoop, calls=%fused_computation.3 | loop fusion | flops 12288 | bytes 98304 | tf_op jit(solution)/shard_map/concatenate | solution.py:295
  (17 shorter events, 0.5 us)
Async XLA Ops:
  1.6 3.8 %collective-permute-start = (bf16[4,64,16,128]{3,2,1,0:T(8,128)(2,1)S(1)}, bf16[4,64,16,128]{3,2,1,0:T(8,128)(2,1)S(1)}, u32[]{:S(2)}, u32[]{:S(2)}) collective-permute-start(bf16[4,64,16,128]{3,2,1,0:T(8,128)(2,1)S(1)} %shard_map.17), channel_id=1, source_target_pairs={{0,32},{1,33},{2,34},{3,35},{4,36},{5,37},{6,38},{7,39},{8,40},{9,... | collective-permute-start | bytes 3145736 | tf_op jit(solution)/shard_map/ppermute | solution.py:30
  4.8 4.9 %collective-permute-start.1 = (bf16[4,64,16,128]{3,2,1,0:T(8,128)(2,1)S(1)}, bf16[4,64,16,128]{3,2,1,0:T(8,128)(2,1)S(1)}, u32[]{:S(2)}, u32[]{:S(2)}) collective-permute-start(bf16[4,64,16,128]{3,2,1,0:T(8,128)(2,1)S(1)} %get-tuple-element.28), channel_id=1, source_target_pairs={{0,32},{1,33},{2,34},{3,35},{4,36},{5,37},{6,38},{7,39},{8,40},{9,... | collective-permute-start | bytes 3145736 | tf_op jit(solution)/shard_map/ppermute | solution.py:30
  5.3 8.1 %collective-permute-start.2 = (bf16[4,64,16,128]{3,2,1,0:T(8,128)(2,1)S(1)}, bf16[4,64,16,128]{3,2,1,0:T(8,128)(2,1)S(1)}, u32[]{:S(2)}, u32[]{:S(2)}) collective-permute-start(bf16[4,64,16,128]{3,2,1,0:T(8,128)(2,1)S(1)} %get-tuple-element.29), channel_id=1, source_target_pairs={{0,32},{1,33},{2,34},{3,35},{4,36},{5,37},{6,38},{7,39},{8,40},{9,... | collective-permute-start | bytes 3145736 | tf_op jit(solution)/shard_map/ppermute | solution.py:30
  5.6 9.5 %collective-permute-start.6 = (bf16[4,4,4,2,16,128]{5,4,3,2,1,0:T(8,128)(2,1)S(1)}, bf16[4,4,4,2,16,128]{5,4,3,2,1,0:T(8,128)(2,1)S(1)}, u32[]{:S(2)}, u32[]{:S(2)}) collective-permute-start(bf16[4,4,4,2,16,128]{5,4,3,2,1,0:T(8,128)(2,1)S(1)} %get-tuple-element.34), channel_id=1, source_target_pairs={{0,1},{1,0},{2,3},{3,2},{4,5},{5,4},{6,7},{7,6},{8,9},{9,8},{10,11... | collective-permute-start | bytes 1572872 | tf_op jit(solution)/shard_map/ppermute | solution.py:30
  7.6 11.8 %collective-permute-start.3 = (bf16[4,4,2,4,16,128]{5,4,3,2,1,0:T(8,128)(2,1)S(1)}, bf16[4,4,2,4,16,128]{5,4,3,2,1,0:T(8,128)(2,1)S(1)}, u32[]{:S(2)}, u32[]{:S(2)}) collective-permute-start(bf16[4,4,2,4,16,128]{5,4,3,2,1,0:T(8,128)(2,1)S(1)} %get-tuple-element.33), channel_id=1, source_target_pairs={{0,16},{1,17},{2,18},{3,19},{4,20},{5,21},{6,22},{7,23},{8,24},{9,... | collective-permute-start | bytes 1572872 | tf_op jit(solution)/shard_map/ppermute | solution.py:30
  11.3 12.6 %collective-permute-start.4 = (bf16[4,4,2,4,16,128]{5,4,3,2,1,0:T(8,128)(2,1)S(1)}, bf16[4,4,2,4,16,128]{5,4,3,2,1,0:T(8,128)(2,1)S(1)}, u32[]{:S(2)}, u32[]{:S(2)}) collective-permute-start(bf16[4,4,2,4,16,128]{5,4,3,2,1,0:T(8,128)(2,1)S(1)} %get-tuple-element.36), channel_id=1, source_target_pairs={{0,8},{1,9},{2,10},{3,11},{4,12},{5,13},{6,14},{7,15},{8,16},{9,17... | collective-permute-start | bytes 1572872 | tf_op jit(solution)/shard_map/ppermute | solution.py:30
  11.4 12.6 %collective-permute-start.5 = (bf16[4,4,2,4,16,128]{5,4,3,2,1,0:T(8,128)(2,1)S(1)}, bf16[4,4,2,4,16,128]{5,4,3,2,1,0:T(8,128)(2,1)S(1)}, u32[]{:S(2)}, u32[]{:S(2)}) collective-permute-start(bf16[4,4,2,4,16,128]{5,4,3,2,1,0:T(8,128)(2,1)S(1)} %get-tuple-element.37), channel_id=1, source_target_pairs={{0,24},{1,25},{2,26},{3,27},{4,28},{5,29},{6,30},{7,31},{8,0},{9,1... | collective-permute-start | bytes 1572872 | tf_op jit(solution)/shard_map/ppermute | solution.py:30
  15.2 10.3 %collective-permute-start.7 = (bf16[4,4,2,16,128]{4,3,2,1,0:T(8,128)(2,1)S(1)}, bf16[4,4,2,16,128]{4,3,2,1,0:T(8,128)(2,1)S(1)}, u32[]{:S(2)}, u32[]{:S(2)}) collective-permute-start(bf16[4,4,2,16,128]{4,3,2,1,0:T(8,128)(2,1)S(1)} %get-tuple-element.42), channel_id=1, source_target_pairs={{0,16},{1,17},{2,18},{3,19},{4,20},{5,21},{6,22},{7,23},{8,24},{9,... | collective-permute-start | bytes 393224 | tf_op jit(solution)/shard_map/ppermute | solution.py:30
  17.1 9.6 %collective-permute-start.8 = (bf16[4,4,2,16,128]{4,3,2,1,0:T(8,128)(2,1)S(1)}, bf16[4,4,2,16,128]{4,3,2,1,0:T(8,128)(2,1)S(1)}, u32[]{:S(2)}, u32[]{:S(2)}) collective-permute-start(bf16[4,4,2,16,128]{4,3,2,1,0:T(8,128)(2,1)S(1)} %get-tuple-element.43), channel_id=1, source_target_pairs={{0,8},{1,9},{2,10},{3,11},{4,12},{5,13},{6,14},{7,15},{8,16},{9,17... | collective-permute-start | bytes 393224 | tf_op jit(solution)/shard_map/ppermute | solution.py:30
  19.3 7.4 %collective-permute-start.9 = (bf16[4,4,2,16,128]{4,3,2,1,0:T(8,128)(2,1)S(1)}, bf16[4,4,2,16,128]{4,3,2,1,0:T(8,128)(2,1)S(1)}, u32[]{:S(2)}, u32[]{:S(2)}) collective-permute-start(bf16[4,4,2,16,128]{4,3,2,1,0:T(8,128)(2,1)S(1)} %get-tuple-element.44), channel_id=1, source_target_pairs={{0,24},{1,25},{2,26},{3,27},{4,28},{5,29},{6,30},{7,31},{8,0},{9,1... | collective-permute-start | bytes 393224 | tf_op jit(solution)/shard_map/ppermute | solution.py:30
  26.9 6.9 %collective-permute-start.10 = (bf16[4,2,5,16,128]{4,3,2,1,0:T(8,128)(2,1)S(1)}, bf16[4,2,5,16,128]{4,3,2,1,0:T(8,128)(2,1)S(1)}, u32[]{:S(2)}, u32[]{:S(2)}) collective-permute-start(bf16[4,2,5,16,128]{4,3,2,1,0:T(8,128)(2,1)S(1)} %get-tuple-element.46), channel_id=1, source_target_pairs={{0,4},{1,5},{2,6},{3,7},{4,0},{5,1},{6,2},{7,3},{8,12},{9,13},{10,... | collective-permute-start | bytes 491528 | tf_op jit(solution)/shard_map/ppermute | solution.py:30
  30.2 6.5 %collective-permute-start.11 = (bf16[4,2,5,16,128]{4,3,2,1,0:T(8,128)(2,1)S(1)}, bf16[4,2,5,16,128]{4,3,2,1,0:T(8,128)(2,1)S(1)}, u32[]{:S(2)}, u32[]{:S(2)}) collective-permute-start(bf16[4,2,5,16,128]{4,3,2,1,0:T(8,128)(2,1)S(1)} %get-tuple-element.47), channel_id=1, source_target_pairs={{0,2},{1,3},{2,4},{3,5},{4,6},{5,7},{6,0},{7,1},{8,10},{9,11},{10,... | collective-permute-start | bytes 491528 | tf_op jit(solution)/shard_map/ppermute | solution.py:30
  30.9 5.9 %collective-permute-start.12 = (bf16[4,2,5,16,128]{4,3,2,1,0:T(8,128)(2,1)S(1)}, bf16[4,2,5,16,128]{4,3,2,1,0:T(8,128)(2,1)S(1)}, u32[]{:S(2)}, u32[]{:S(2)}) collective-permute-start(bf16[4,2,5,16,128]{4,3,2,1,0:T(8,128)(2,1)S(1)} %get-tuple-element.48), channel_id=1, source_target_pairs={{0,6},{1,7},{2,0},{3,1},{4,2},{5,3},{6,4},{7,5},{8,14},{9,15},{10,... | collective-permute-start | bytes 491528 | tf_op jit(solution)/shard_map/ppermute | solution.py:30

commit v8 on v7

--- a/solution.py
+++ b/solution.py
@@ -262,7 +262,7 @@
 def on_device(grads):
     rows = grads.shape[1] // (ZH * CORE * X * Y * ZL * SLABS * QB)
     grads = grads.reshape(ZH, CORE, X, Y, ZL, SLABS, rows, QB)
-    groups = ((2, SENT), (1, 3), (0, KEPT))
+    groups = ((SENT, 2), (1, 3), (0, KEPT))
     outs = run_cast(grads, groups[:1], ())
     grads = lax.optimization_barrier((grads, *outs))[0]
     crossed = [to_other_core(out) for out in outs]

time: 54.7 us -> 54.7 us (level)
  no operation moved by 1% of the time
where the time goes in v8:
time: 54.7 us; the launch traced here: 54.3 us
  starting transfers between devices  17.7 us (32%)
  blocking collectives  16.8 us (31%)
  waiting for transfers between devices  10.5 us (19%)
  Pallas kernels  8.44 us (15%)
  other arithmetic  0.77 us (1%)
    ppermute x13, starting transfers between devices, permuted(): return lax.ppermute(values, AXES, pairs)  17.7 us
    all_to_all x1, blocking collectives, on_device(): lax.all_to_all(pieces, AXES, 0, 0, axis_index_groups=z_groups(), tiled=True)  16.8 us
    ppermute x13, waiting for transfers between devices, permuted(): return lax.ppermute(values, AXES, pairs)  10.5 us
    pallas_call x4, Pallas kernels, run_on_grads(): pl.pallas_call(kernel, out_shape=out_shape, in_specs=[pl.BlockSpec(memory...  7.84 us
  transfers between devices with their start and end apart: 13, of which 5 were waited for; matrix products, arithmetic and copies ran while one was open for 0% of the time, Pallas kernels for 12%

profile of v8, /device:TPU:2, one launch (start us, length us, event | category | flops | bytes accessed | tf_op | source)
XLA Modules:
  0.0 54.3 jit_solution(14275023232957577955)
XLA Ops:
  0.0 1.6 %shard_map.17 = bf16[4,64,16,128]{3,2,1,0:T(8,128)(2,1)S(1)} custom-call(f32[4,2,4,4,2,6,16,128]{7,6,5,4,3,2,1,0:T(8,128)} %bitcast.6), custom_call_target="tpu_custom_call" | custom-call | tf_op jit(solution)/shard_map/pallas_call | solution.py:163
  1.7 3.0 %shard_map.18 = (bf16[4,64,16,128]{3,2,1,0:T(8,128)(2,1)S(1)}, bf16[4,64,16,128]{3,2,1,0:T(8,128)(2,1)S(1)}, f32[4,4,4,2,16,128]{5,4,3,2,1,0:T(8,128)S(1)}, f32[4,4,2,4,16,128]{5,4,3,2,1,0:T(8,128)S(1)}) custom-call(f32[4,2,4,4,2,6,16,128]{7,6,5,4,3,2,1,0:T(8,128)} %bitcast.7), custom_call_target="tpu_custom_call" | custom-call | tf_op jit(solution)/shard_map/pallas_call | solution.py:163
  4.8 0.5 collective-permute-start.1
  5.4 0.2 shard_map.19
  5.6 2.0 %collective-permute-start.6 = (bf16[4,4,4,2,16,128]{5,4,3,2,1,0:T(8,128)(2,1)S(1)}, bf16[4,4,4,2,16,128]{5,4,3,2,1,0:T(8,128)(2,1)S(1)}, u32[]{:S(2)}, u32[]{:S(2)}) collective-permute-start(bf16[4,4,4,2,16,128]{5,4,3,2,1,0:T(8,128)(2,1)S(1)} %get-tuple-element.33), channel_id=1, source_target_pairs={{0,1},{1,0},{2,3},{3,2},{4,5},{5,4},{6,7},{7,6},{8,9},{9,8},{10,11... | collective-permute-start | bytes 1572872 | tf_op jit(solution)/shard_map/ppermute | solution.py:30
  7.6 2.1 %collective-permute-start.3 = (bf16[4,4,2,4,16,128]{5,4,3,2,1,0:T(8,128)(2,1)S(1)}, bf16[4,4,2,4,16,128]{5,4,3,2,1,0:T(8,128)(2,1)S(1)}, u32[]{:S(2)}, u32[]{:S(2)}) collective-permute-start(bf16[4,4,2,4,16,128]{5,4,3,2,1,0:T(8,128)(2,1)S(1)} %get-tuple-element.34), channel_id=1, source_target_pairs={{0,16},{1,17},{2,18},{3,19},{4,20},{5,21},{6,22},{7,23},{8,24},{9,... | collective-permute-start | bytes 1572872 | tf_op jit(solution)/shard_map/ppermute | solution.py:30
  9.7 1.6 %shard_map.20 = (bf16[4,4,2,4,16,128]{5,4,3,2,1,0:T(8,128)(2,1)S(1)}, bf16[4,4,2,4,16,128]{5,4,3,2,1,0:T(8,128)(2,1)S(1)}) custom-call(f32[4,2,4,4,2,6,16,128]{7,6,5,4,3,2,1,0:T(8,128)} %bitcast.8, bf16[4,64,16,128]{3,2,1,0:T(8,128)(2,1)S(1)} %collective-permute-done.1.received), custom_call_target="tpu_custom_call" | custom-call | tf_op jit(solution)/shard_map/pallas_call | solution.py:163
  11.4 2.0 %collective-permute-start.5 = (bf16[4,4,2,4,16,128]{5,4,3,2,1,0:T(8,128)(2,1)S(1)}, bf16[4,4,2,4,16,128]{5,4,3,2,1,0:T(8,128)(2,1)S(1)}, u32[]{:S(2)}, u32[]{:S(2)}) collective-permute-start(bf16[4,4,2,4,16,128]{5,4,3,2,1,0:T(8,128)(2,1)S(1)} %get-tuple-element.37), channel_id=1, source_target_pairs={{0,24},{1,25},{2,26},{3,27},{4,28},{5,29},{6,30},{7,31},{8,0},{9,1... | collective-permute-start | bytes 1572872 | tf_op jit(solution)/shard_map/ppermute | solution.py:30
  13.4 1.6 %shard_map.21 = (f32[4,4,2,4,16,128]{5,4,3,2,1,0:T(8,128)S(1)}, f32[4,4,4,2,16,128]{5,4,3,2,1,0:T(8,128)S(1)}) custom-call(f32[4,2,4,4,2,6,16,128]{7,6,5,4,3,2,1,0:T(8,128)} %bitcast.9, bf16[4,64,16,128]{3,2,1,0:T(8,128)(2,1)S(1)} %collective-permute-done.2.received), custom_call_target="tpu_custom_call" | custom-call | tf_op jit(solution)/shard_map/pallas_call | solution.py:163
  15.0 0.1 shard_map.23
  15.2 2.0 %collective-permute-start.7 = (bf16[4,4,2,16,128]{4,3,2,1,0:T(8,128)(2,1)S(1)}, bf16[4,4,2,16,128]{4,3,2,1,0:T(8,128)(2,1)S(1)}, u32[]{:S(2)}, u32[]{:S(2)}) collective-permute-start(bf16[4,4,2,16,128]{4,3,2,1,0:T(8,128)(2,1)S(1)} %get-tuple-element.42), channel_id=1, source_target_pairs={{0,16},{1,17},{2,18},{3,19},{4,20},{5,21},{6,22},{7,23},{8,24},{9,... | collective-permute-start | bytes 393224 | tf_op jit(solution)/shard_map/ppermute | solution.py:30
  17.2 2.2 %collective-permute-start.8 = (bf16[4,4,2,16,128]{4,3,2,1,0:T(8,128)(2,1)S(1)}, bf16[4,4,2,16,128]{4,3,2,1,0:T(8,128)(2,1)S(1)}, u32[]{:S(2)}, u32[]{:S(2)}) collective-permute-start(bf16[4,4,2,16,128]{4,3,2,1,0:T(8,128)(2,1)S(1)} %get-tuple-element.43), channel_id=1, source_target_pairs={{0,8},{1,9},{2,10},{3,11},{4,12},{5,13},{6,14},{7,15},{8,16},{9,17... | collective-permute-start | bytes 393224 | tf_op jit(solution)/shard_map/ppermute | solution.py:30
  19.4 4.6 %collective-permute-done.4.p2 = bf16[4,4,2,4,16,128]{5,4,3,2,1,0:T(8,128)(2,1)S(1)} collective-permute-done((bf16[4,4,2,4,16,128]{5,4,3,2,1,0:T(8,128)(2,1)S(1)}, bf16[4,4,2,4,16,128]{5,4,3,2,1,0:T(8,128)(2,1)S(1)}, u32[]{:S(2)}, u32[]{:S(2)}) %collective-permute-start.4) | collective-permute-done | bytes 524320 | tf_op jit(solution)/shard_map/ppermute | solution.py:30
  23.9 0.2 shard_map.22.plain
  24.2 1.3 %collective-permute-done.7.p1 = bf16[4,4,2,16,128]{4,3,2,1,0:T(8,128)(2,1)S(1)} collective-permute-done((bf16[4,4,2,16,128]{4,3,2,1,0:T(8,128)(2,1)S(1)}, bf16[4,4,2,16,128]{4,3,2,1,0:T(8,128)(2,1)S(1)}, u32[]{:S(2)}, u32[]{:S(2)}) %collective-permute-start.7) | collective-permute-done | bytes 131104 | tf_op jit(solution)/shard_map/ppermute | solution.py:30
  25.4 1.4 %collective-permute-done.8.p2 = bf16[4,4,2,16,128]{4,3,2,1,0:T(8,128)(2,1)S(1)} collective-permute-done((bf16[4,4,2,16,128]{4,3,2,1,0:T(8,128)(2,1)S(1)}, bf16[4,4,2,16,128]{4,3,2,1,0:T(8,128)(2,1)S(1)}, u32[]{:S(2)}, u32[]{:S(2)}) %collective-permute-start.8) | collective-permute-done | bytes 131104 | tf_op jit(solution)/shard_map/ppermute | solution.py:30
  26.8 0.1 shard_map.24
  26.9 3.3 %collective-permute-start.10 = (bf16[4,2,5,16,128]{4,3,2,1,0:T(8,128)(2,1)S(1)}, bf16[4,2,5,16,128]{4,3,2,1,0:T(8,128)(2,1)S(1)}, u32[]{:S(2)}, u32[]{:S(2)}) collective-permute-start(bf16[4,2,5,16,128]{4,3,2,1,0:T(8,128)(2,1)S(1)} %get-tuple-element.46), channel_id=1, source_target_pairs={{0,4},{1,5},{2,6},{3,7},{4,0},{5,1},{6,2},{7,3},{8,12},{9,13},{10,... | collective-permute-start | bytes 491528 | tf_op jit(solution)/shard_map/ppermute | solution.py:30
  30.2 0.7 %collective-permute-start.11 = (bf16[4,2,5,16,128]{4,3,2,1,0:T(8,128)(2,1)S(1)}, bf16[4,2,5,16,128]{4,3,2,1,0:T(8,128)(2,1)S(1)}, u32[]{:S(2)}, u32[]{:S(2)}) collective-permute-start(bf16[4,2,5,16,128]{4,3,2,1,0:T(8,128)(2,1)S(1)} %get-tuple-element.47), channel_id=1, source_target_pairs={{0,2},{1,3},{2,4},{3,5},{4,6},{5,7},{6,0},{7,1},{8,10},{9,11},{10,... | collective-permute-start | bytes 491528 | tf_op jit(solution)/shard_map/ppermute | solution.py:30
  30.9 2.6 %collective-permute-start.12 = (bf16[4,2,5,16,128]{4,3,2,1,0:T(8,128)(2,1)S(1)}, bf16[4,2,5,16,128]{4,3,2,1,0:T(8,128)(2,1)S(1)}, u32[]{:S(2)}, u32[]{:S(2)}) collective-permute-start(bf16[4,2,5,16,128]{4,3,2,1,0:T(8,128)(2,1)S(1)} %get-tuple-element.48), channel_id=1, source_target_pairs={{0,6},{1,7},{2,0},{3,1},{4,2},{5,3},{6,4},{7,5},{8,14},{9,15},{10,... | collective-permute-start | bytes 491528 | tf_op jit(solution)/shard_map/ppermute | solution.py:30
  33.4 0.4 collective-permute-done.10
  33.8 2.9 %collective-permute-done.11 = bf16[4,2,5,16,128]{4,3,2,1,0:T(8,128)(2,1)S(1)} collective-permute-done((bf16[4,2,5,16,128]{4,3,2,1,0:T(8,128)(2,1)S(1)}, bf16[4,2,5,16,128]{4,3,2,1,0:T(8,128)(2,1)S(1)}, u32[]{:S(2)}, u32[]{:S(2)}) %collective-permute-start.11) | collective-permute-done | bytes 163872 | tf_op jit(solution)/shard_map/ppermute | solution.py:30
  36.8 16.8 %all_to_all.5 = bf16[8,5,16,128]{3,2,1,0:T(8,128)(2,1)S(1)} all-to-all(bf16[8,5,16,128]{3,2,1,0:T(8,128)(2,1)S(1)} %bitcast.10), channel_id=1, replica_groups={{0,1,64,65,128,129,192,193},{2,3,66,67,130,131,194,195},{4,5,68,69,132,..., dimensions={0} | all-to-all | bytes 327680 | tf_op jit(solution)/shard_map/all_to_all | solution.py:292
  53.7 0.6 %pad_maximum_fusion = f32[6,16,128]{2,1,0:T(8,128)} fusion(f32[2,16,128]{2,1,0:T(8,128)S(1)} %bitcast_reduce_fusion, f32[4,16,128]{2,1,0:T(8,128)S(1)} %slice_reduce_fusion), kind=kLoop, calls=%fused_computation.3 | loop fusion | flops 12288 | bytes 98304 | tf_op jit(solution)/shard_map/concatenate | solution.py:295
  (17 shorter events, 0.5 us)
Async XLA Ops:
  1.6 3.8 %collective-permute-start = (bf16[4,64,16,128]{3,2,1,0:T(8,128)(2,1)S(1)}, bf16[4,64,16,128]{3,2,1,0:T(8,128)(2,1)S(1)}, u32[]{:S(2)}, u32[]{:S(2)}) collective-permute-start(bf16[4,64,16,128]{3,2,1,0:T(8,128)(2,1)S(1)} %shard_map.17), channel_id=1, source_target_pairs={{0,32},{1,33},{2,34},{3,35},{4,36},{5,37},{6,38},{7,39},{8,40},{9,... | collective-permute-start | bytes 3145736 | tf_op jit(solution)/shard_map/ppermute | solution.py:30
  4.8 4.9 %collective-permute-start.1 = (bf16[4,64,16,128]{3,2,1,0:T(8,128)(2,1)S(1)}, bf16[4,64,16,128]{3,2,1,0:T(8,128)(2,1)S(1)}, u32[]{:S(2)}, u32[]{:S(2)}) collective-permute-start(bf16[4,64,16,128]{3,2,1,0:T(8,128)(2,1)S(1)} %get-tuple-element.28), channel_id=1, source_target_pairs={{0,32},{1,33},{2,34},{3,35},{4,36},{5,37},{6,38},{7,39},{8,40},{9,... | collective-permute-start | bytes 3145736 | tf_op jit(solution)/shard_map/ppermute | solution.py:30
  5.3 8.1 %collective-permute-start.2 = (bf16[4,64,16,128]{3,2,1,0:T(8,128)(2,1)S(1)}, bf16[4,64,16,128]{3,2,1,0:T(8,128)(2,1)S(1)}, u32[]{:S(2)}, u32[]{:S(2)}) collective-permute-start(bf16[4,64,16,128]{3,2,1,0:T(8,128)(2,1)S(1)} %get-tuple-element.29), channel_id=1, source_target_pairs={{0,32},{1,33},{2,34},{3,35},{4,36},{5,37},{6,38},{7,39},{8,40},{9,... | collective-permute-start | bytes 3145736 | tf_op jit(solution)/shard_map/ppermute | solution.py:30
  5.6 9.5 %collective-permute-start.6 = (bf16[4,4,4,2,16,128]{5,4,3,2,1,0:T(8,128)(2,1)S(1)}, bf16[4,4,4,2,16,128]{5,4,3,2,1,0:T(8,128)(2,1)S(1)}, u32[]{:S(2)}, u32[]{:S(2)}) collective-permute-start(bf16[4,4,4,2,16,128]{5,4,3,2,1,0:T(8,128)(2,1)S(1)} %get-tuple-element.33), channel_id=1, source_target_pairs={{0,1},{1,0},{2,3},{3,2},{4,5},{5,4},{6,7},{7,6},{8,9},{9,8},{10,11... | collective-permute-start | bytes 1572872 | tf_op jit(solution)/shard_map/ppermute | solution.py:30
  7.6 11.8 %collective-permute-start.3 = (bf16[4,4,2,4,16,128]{5,4,3,2,1,0:T(8,128)(2,1)S(1)}, bf16[4,4,2,4,16,128]{5,4,3,2,1,0:T(8,128)(2,1)S(1)}, u32[]{:S(2)}, u32[]{:S(2)}) collective-permute-start(bf16[4,4,2,4,16,128]{5,4,3,2,1,0:T(8,128)(2,1)S(1)} %get-tuple-element.34), channel_id=1, source_target_pairs={{0,16},{1,17},{2,18},{3,19},{4,20},{5,21},{6,22},{7,23},{8,24},{9,... | collective-permute-start | bytes 1572872 | tf_op jit(solution)/shard_map/ppermute | solution.py:30
  11.3 12.6 %collective-permute-start.4 = (bf16[4,4,2,4,16,128]{5,4,3,2,1,0:T(8,128)(2,1)S(1)}, bf16[4,4,2,4,16,128]{5,4,3,2,1,0:T(8,128)(2,1)S(1)}, u32[]{:S(2)}, u32[]{:S(2)}) collective-permute-start(bf16[4,4,2,4,16,128]{5,4,3,2,1,0:T(8,128)(2,1)S(1)} %get-tuple-element.36), channel_id=1, source_target_pairs={{0,8},{1,9},{2,10},{3,11},{4,12},{5,13},{6,14},{7,15},{8,16},{9,17... | collective-permute-start | bytes 1572872 | tf_op jit(solution)/shard_map/ppermute | solution.py:30
  11.4 12.6 %collective-permute-start.5 = (bf16[4,4,2,4,16,128]{5,4,3,2,1,0:T(8,128)(2,1)S(1)}, bf16[4,4,2,4,16,128]{5,4,3,2,1,0:T(8,128)(2,1)S(1)}, u32[]{:S(2)}, u32[]{:S(2)}) collective-permute-start(bf16[4,4,2,4,16,128]{5,4,3,2,1,0:T(8,128)(2,1)S(1)} %get-tuple-element.37), channel_id=1, source_target_pairs={{0,24},{1,25},{2,26},{3,27},{4,28},{5,29},{6,30},{7,31},{8,0},{9,1... | collective-permute-start | bytes 1572872 | tf_op jit(solution)/shard_map/ppermute | solution.py:30
  15.2 10.3 %collective-permute-start.7 = (bf16[4,4,2,16,128]{4,3,2,1,0:T(8,128)(2,1)S(1)}, bf16[4,4,2,16,128]{4,3,2,1,0:T(8,128)(2,1)S(1)}, u32[]{:S(2)}, u32[]{:S(2)}) collective-permute-start(bf16[4,4,2,16,128]{4,3,2,1,0:T(8,128)(2,1)S(1)} %get-tuple-element.42), channel_id=1, source_target_pairs={{0,16},{1,17},{2,18},{3,19},{4,20},{5,21},{6,22},{7,23},{8,24},{9,... | collective-permute-start | bytes 393224 | tf_op jit(solution)/shard_map/ppermute | solution.py:30
  17.2 9.6 %collective-permute-start.8 = (bf16[4,4,2,16,128]{4,3,2,1,0:T(8,128)(2,1)S(1)}, bf16[4,4,2,16,128]{4,3,2,1,0:T(8,128)(2,1)S(1)}, u32[]{:S(2)}, u32[]{:S(2)}) collective-permute-start(bf16[4,4,2,16,128]{4,3,2,1,0:T(8,128)(2,1)S(1)} %get-tuple-element.43), channel_id=1, source_target_pairs={{0,8},{1,9},{2,10},{3,11},{4,12},{5,13},{6,14},{7,15},{8,16},{9,17... | collective-permute-start | bytes 393224 | tf_op jit(solution)/shard_map/ppermute | solution.py:30
  19.4 7.4 %collective-permute-start.9 = (bf16[4,4,2,16,128]{4,3,2,1,0:T(8,128)(2,1)S(1)}, bf16[4,4,2,16,128]{4,3,2,1,0:T(8,128)(2,1)S(1)}, u32[]{:S(2)}, u32[]{:S(2)}) collective-permute-start(bf16[4,4,2,16,128]{4,3,2,1,0:T(8,128)(2,1)S(1)} %get-tuple-element.44), channel_id=1, source_target_pairs={{0,24},{1,25},{2,26},{3,27},{4,28},{5,29},{6,30},{7,31},{8,0},{9,1... | collective-permute-start | bytes 393224 | tf_op jit(solution)/shard_map/ppermute | solution.py:30
  26.9 6.9 %collective-permute-start.10 = (bf16[4,2,5,16,128]{4,3,2,1,0:T(8,128)(2,1)S(1)}, bf16[4,2,5,16,128]{4,3,2,1,0:T(8,128)(2,1)S(1)}, u32[]{:S(2)}, u32[]{:S(2)}) collective-permute-start(bf16[4,2,5,16,128]{4,3,2,1,0:T(8,128)(2,1)S(1)} %get-tuple-element.46), channel_id=1, source_target_pairs={{0,4},{1,5},{2,6},{3,7},{4,0},{5,1},{6,2},{7,3},{8,12},{9,13},{10,... | collective-permute-start | bytes 491528 | tf_op jit(solution)/shard_map/ppermute | solution.py:30
  30.2 6.5 %collective-permute-start.11 = (bf16[4,2,5,16,128]{4,3,2,1,0:T(8,128)(2,1)S(1)}, bf16[4,2,5,16,128]{4,3,2,1,0:T(8,128)(2,1)S(1)}, u32[]{:S(2)}, u32[]{:S(2)}) collective-permute-start(bf16[4,2,5,16,128]{4,3,2,1,0:T(8,128)(2,1)S(1)} %get-tuple-element.47), channel_id=1, source_target_pairs={{0,2},{1,3},{2,4},{3,5},{4,6},{5,7},{6,0},{7,1},{8,10},{9,11},{10,... | collective-permute-start | bytes 491528 | tf_op jit(solution)/shard_map/ppermute | solution.py:30
  30.9 5.9 %collective-permute-start.12 = (bf16[4,2,5,16,128]{4,3,2,1,0:T(8,128)(2,1)S(1)}, bf16[4,2,5,16,128]{4,3,2,1,0:T(8,128)(2,1)S(1)}, u32[]{:S(2)}, u32[]{:S(2)}) collective-permute-start(bf16[4,2,5,16,128]{4,3,2,1,0:T(8,128)(2,1)S(1)} %get-tuple-element.48), channel_id=1, source_target_pairs={{0,6},{1,7},{2,0},{3,1},{4,2},{5,3},{6,4},{7,5},{8,14},{9,15},{10,... | collective-permute-start | bytes 491528 | tf_op jit(solution)/shard_map/ppermute | solution.py:30
